TPU v7x, 32 devices: a whole 2x2x4 slice. The times are simulated.
32 devices in a mesh: row: 4 (over y, core), col: 8 (over z, x).
Axes of the slice: x: 2, y: 2, z: 4, core: 2. Of those that a mesh axis runs over, the one named last changes fastest.
Arguments:
- features: bfloat16 [65536, 256], P(('row', 'col')), may hold values from -6 to 6
- hub_features: bfloat16 [512, 256], P(('row', 'col')), may hold values from -6 to 6
- w_self: bfloat16 [256, 256], replicated, may hold values from -0.375 to 0.375
- w_neigh: bfloat16 [256, 256], replicated, may hold values from -0.375 to 0.375
- out_bias: float32 [256], replicated, may hold values from -4 to 4
- local_edges: int32 [65536, 4], P(('row', 'col')), may hold values from 0 to 2047
- hub_edges: int32 [65536, 2], P(('row', 'col')), may hold values from 0 to 511
- remote_edges: int32 [65536, 4], P(('row', 'col')), may hold values from 0 to 511
- send_rows: int32 [32, 512], P(('row', 'col')), may hold values from 0 to 2047
- cotangent: bfloat16 [65536, 256], P(('row', 'col')), may hold values from -6 to 6
Outputs:
- activated: bfloat16 [65536, 256], P(('row', 'col'))
- grad_features: float32 [65536, 256], P(('row', 'col'))
- grad_hubs: float32 [512, 256], P(('row', 'col'))
- grad_w_self: float32 [256, 256], replicated
- grad_w_neigh: float32 [256, 256], replicated
- grad_bias: float32 [256], replicated
All inputs are finite; a program needn't handle non-finite values.
Results may differ from a plain program's by a relative error of at most 0.0075.
Values may be sent and summed in bfloat16 or wider, within the bound.
No kernel may reach another device: no remote copies, remote signals or barrier semaphores. Data moves between devices by JAX's collectives and lax.ppermute only.
A program may use at most 64 MiB of HBM per device.

v0:
```python
import functools

import jax
import jax.numpy as jnp
from jax import lax
from jax.experimental import pallas as pl
from jax.experimental.pallas import tpu as pltpu
from jax.sharding import PartitionSpec as P

AXES = ("row", "col")
LANES = 128
TILE = 256
MOST_VMEM = 60928 * 1024
LESS_VMEM = 8 * 1024 * 1024
NT = (((1,), (1,)), ((), ()))
TN = (((0,), (0,)), ((), ()))
VMEM = pl.BlockSpec(memory_space=pltpu.VMEM)
SMEM = pl.BlockSpec(memory_space=pltpu.SMEM)
HBM = pl.BlockSpec(memory_space=pltpu.HBM)
bf16, f32 = jnp.bfloat16, jnp.float32


def params(limit):
    return pltpu.CompilerParams(vmem_limit_bytes=limit)


def cost(flops, moved):
    return pl.CostEstimate(flops=int(flops), bytes_accessed=int(moved), transcendentals=0)


def along_rows(index_row):
    count = index_row.shape[1]
    return jnp.transpose(jnp.broadcast_to(index_row, (LANES, count))).astype(jnp.int16)


def hits_by_row(columns, first, width):
    rows = columns[0].shape[0]
    lane = lax.broadcasted_iota(jnp.int32, (rows, LANES), 1).astype(jnp.int16)
    one = jnp.ones((rows, LANES), bf16)
    zero = jnp.zeros((rows, LANES), bf16)
    tiles = []
    for start in range(first, first + width, LANES):
        here = lane + jnp.int16(start)
        total = None
        for column in columns:
            hit = jnp.where(column == here, one, zero)
            total = hit if total is None else total + hit
        tiles.append(total)
    return jnp.concatenate(tiles, axis=1) if len(tiles) > 1 else tiles[0]


def hits_by_column(index_rows, first, height):
    count = index_rows[0].shape[1]
    down = lax.broadcasted_iota(jnp.int32, (height, count), 0).astype(jnp.int16)
    one = jnp.ones((height, count), bf16)
    zero = jnp.zeros((height, count), bf16)
    total = None
    for row in index_rows:
        entry = jnp.broadcast_to(row - first, (16, count)).astype(jnp.int16)
        entry = jnp.broadcast_to(entry[None], (height // 16, 16, count)).reshape(height, count)
        hit = jnp.where(entry == down, one, zero)
        total = hit if total is None else total + hit
    return total


def dot(a, b, dims=(((1,), (0,)), ((), ()))):
    return lax.dot_general(a, b, dims, preferred_element_type=f32)


def index_rows(ref, start, count):
    return [ref[j : j + 1, pl.ds(start, count)] for j in range(ref.shape[0])]


def pick_kernel(send_ref, feat_ref, hub_ref, out_ref):
    parts, slab, width = out_ref.shape
    hub_rows = hub_ref.shape[0]
    slots = slab - hub_rows
    total = send_ref.shape[1]
    step = min(512, total)
    for start in range(0, total, step):
        column = along_rows(send_ref[:, start : start + step])
        picked = dot(hits_by_row([column], 0, feat_ref.shape[0]), feat_ref[...])
        out_ref[start // slots : (start + step) // slots, :slots, :] = (
            picked.astype(bf16).reshape(step // slots, slots, width)
        )
    out_ref[:, slots:, :] = jnp.broadcast_to(hub_ref[...][None], (parts, hub_rows, width))


def local_kernel(split, local_ref, remote_ref, hub_ref, feat_ref, sum_ref, by_row_ref, by_col_ref):
    nodes = feat_ref.shape[0]
    columns = [along_rows(row) for row in index_rows(local_ref, 0, TILE)]
    total = None
    for first in range(0, nodes, TILE):
        part = dot(hits_by_row(columns, first, TILE), feat_ref[first : first + TILE, :])
        total = part if total is None else total + part
    sum_ref[...] = total
    for ref, low, high in ((remote_ref, 0, split), (hub_ref, split, by_row_ref.shape[1])):
        index = index_rows(ref, 0, TILE)
        columns = [along_rows(row) for row in index]
        for first in range(low, high, TILE):
            by_row_ref[:, first : first + TILE] = hits_by_row(columns, first - low, TILE)
            by_col_ref[first : first + TILE, :] = hits_by_column(index, first - low, TILE)


def middle_kernel(
    scale,
    slots,
    feat_hbm,
    sum_hbm,
    by_row_hbm,
    by_col_hbm,
    cot_hbm,
    table_ref,
    ws_ref,
    wn_ref,
    bias_ref,
    act_hbm,
    grad_hbm,
    pay_ref,
    feat,
    sums,
    by_row,
    by_col,
    cot,
    act,
    grad_all,
    mean_all,
    block_sem,
    half_sem,
    col_sem,
    out_sem,
):
    nodes, width = feat.shape
    parts, slab, _ = table_ref.shape
    hub_rows = slab - slots
    bounds, hubs = parts * slots, parts * hub_rows
    blocks = nodes // TILE
    halves = 2

    def here(block):
        return slice(block * TILE, (block + 1) * TILE)

    def loads(block):
        at = here(block)
        copies = [
            pltpu.make_async_copy(by_row_hbm.at[at, :], by_row.at[at, :], block_sem.at[0, block]),
            pltpu.make_async_copy(sum_hbm.at[at, :], sums.at[at, :], block_sem.at[1, block]),
        ]
        if block % (blocks // halves) == 0:
            half = block // (blocks // halves)
            at = slice(half * (nodes // halves), (half + 1) * (nodes // halves))
            copies.append(pltpu.make_async_copy(feat_hbm.at[at, :], feat.at[at, :], half_sem.at[0, half]))
            copies.append(pltpu.make_async_copy(cot_hbm.at[at, :], cot.at[at, :], half_sem.at[1, half]))
        return copies

    coming = [loads(block) for block in range(blocks)]
    for group in coming:
        for copy in group:
            copy.start()
    col_load = pltpu.make_async_copy(by_col_hbm, by_col, col_sem)
    col_load.start()
    table = jnp.concatenate(
        [table_ref[:, :slots, :].reshape(bounds, width), table_ref[:, slots:, :].reshape(hubs, width)], axis=0
    )
    stores = []
    bias_total = jnp.zeros((1, width), f32)
    total = None
    for block in range(blocks + 1):
        following = None
        if block < blocks:
            for copy in coming[block]:
                copy.wait()
            at = here(block)
            following = sums[at, :] + dot(by_row[at, :], table)
        if block > 0:
            at = here(block - 1)
            mean = (total * scale).astype(bf16)
            mean_all[at, :] = mean
            pre = dot(feat[at, :], ws_ref[...]) + dot(mean, wn_ref[...]) + bias_ref[...]
            sig = 0.5 * jnp.tanh(0.5 * pre) + 0.5
            active = pre * sig
            act[at, :] = active.astype(bf16)
            grad = (cot[at, :].astype(f32) * (sig + active * (1.0 - sig))).astype(bf16)
            grad_all[at, :] = grad
            bias_total = bias_total + jnp.sum(grad.astype(f32), axis=0, keepdims=True)
            for which, (source, target) in enumerate(((act, act_hbm), (grad_all, grad_hbm))):
                store = pltpu.make_async_copy(source.at[at, :], target.at[at, :], out_sem.at[which, block - 1])
                store.start()
                stores.append(store)
        total = following
    grad = grad_all[...]
    holders = 2 * width // 16
    per = holders // 2
    for which, source in enumerate((feat, mean_all)):
        pay_ref[which * per : (which + 1) * per, slab : slab + 16, :] = (
            dot(source[...], grad, TN).astype(bf16).reshape(per, 16, width)
        )
    if parts > holders:
        pay_ref[holders:, slab : slab + 16, :] = jnp.zeros((parts - holders, 16, width), bf16)
    pay_ref[:, slab + 16 :, :] = jnp.broadcast_to(high_low(bias_total).astype(bf16)[None], (parts, 8, width))
    col_load.wait()
    pay_ref[:, :slots, :] = dot(by_col[:bounds, :], grad).astype(bf16).reshape(parts, slots, width)
    pay_ref[:, slots:slab, :] = dot(by_col[bounds:, :], grad).astype(bf16).reshape(parts, hub_rows, width)
    for store in stores:
        store.wait()


def high_low(row):
    high = row.astype(bf16).astype(f32)
    place = lax.broadcasted_iota(jnp.int32, (8, row.shape[1]), 0)
    return jnp.where(place == 0, high, jnp.where(place == 1, row - high, 0.0))


def sums_kernel(scale, slots, hub_rows, back_ref, wn_ref, weight_ref, bias_ref, hub_ref):
    slab = slots + hub_rows
    total = jnp.sum(back_ref[:, slots:, :].astype(f32), axis=0)
    weight_ref[...] = jnp.broadcast_to(total[hub_rows : hub_rows + 16].astype(bf16)[None], weight_ref.shape)
    bias_ref[...] = jnp.sum(total[hub_rows + 16 :], axis=0, keepdims=True)
    hub = total[:hub_rows]
    high = hub.astype(bf16)
    low = (hub - high.astype(f32)).astype(bf16)
    hub_ref[...] = (dot(high, wn_ref[...], NT) + dot(low, wn_ref[...], NT)) * scale


def scatter_kernel(local_ref, grad_ref, out_ref):
    height = out_ref.shape[0]
    first = pl.program_id(0) * height
    total = None
    for start in range(0, grad_ref.shape[0], TILE):
        rows = index_rows(local_ref, start, TILE)
        part = dot(hits_by_column(rows, first, height), grad_ref[start : start + TILE, :])
        total = part if total is None else total + part
    out_ref[...] = total


def final_kernel(scale, slots, send_ref, back_ref, scat_ref, grad_ref, ws_ref, wn_ref, out_ref):
    height, width = out_ref.shape
    first = pl.program_id(0) * height
    count = send_ref.shape[1]
    returned = back_ref[:, :slots, :].reshape(count, width)
    total = scat_ref[...]
    for start in range(0, count, 512):
        stop = min(count, start + 512)
        hits = hits_by_column([send_ref[:, start:stop]], first, height)
        total = total + dot(hits, returned[start:stop])
    out_ref[...] = dot(grad_ref[...], ws_ref[...], NT) + dot((total * scale).astype(bf16), wn_ref[...], NT)


def call(
    kernel, ins, in_specs, outs, out_specs, name, grid=(), scratch=(), flops=0, moved=0, limit=LESS_VMEM
):
    return pl.pallas_call(
        kernel,
        grid=grid,
        in_specs=in_specs,
        out_specs=out_specs,
        out_shape=outs,
        scratch_shapes=scratch,
        compiler_params=params(limit),
        cost_estimate=cost(flops, moved),
        name=name,
    )(*ins)


def whole_block(shape):
    return pl.BlockSpec(shape, lambda *_: (0,) * len(shape))


def body(
    features,
    hub_features,
    w_self,
    w_neigh,
    out_bias,
    local_edges,
    hub_edges,
    remote_edges,
    send_rows,
    cotangent,
):
    nodes, width = features.shape
    hub_rows = hub_features.shape[0]
    parts = lax.axis_size(AXES)
    slots = send_rows.shape[1] // parts
    slab = slots + hub_rows
    pay = slab + 24
    table = parts * slab
    scale = 1.0 / (local_edges.shape[1] + hub_edges.shape[1] + remote_edges.shape[1])
    local_t, hub_t, remote_t = local_edges.T, hub_edges.T, remote_edges.T
    bias = out_bias.reshape(1, width)
    shape = jax.ShapeDtypeStruct

    def exchange(value):
        return lax.all_to_all(value, AXES, split_axis=0, concat_axis=0, tiled=True)

    sending = call(
        pick_kernel,
        (send_rows, features, hub_features),
        [VMEM, VMEM, VMEM],
        shape((parts, slab, width), bf16),
        whole_block((parts, slab, width)),
        "pick_rows",
        limit=MOST_VMEM,
        flops=2 * parts * slots * nodes * width,
        moved=nodes * width * 2,
    )
    sending, features = lax.optimization_barrier((sending, features))
    received = exchange(sending)

    block = TILE
    local_sum, by_row, by_col = call(
        functools.partial(local_kernel, parts * slots),
        (local_t, remote_t, hub_t, features),
        [pl.BlockSpec((edges.shape[0], block), lambda i: (0, i)) for edges in (local_t, remote_t, hub_t)]
        + [whole_block((nodes, width))],
        [shape((nodes, width), f32), shape((nodes, table), bf16), shape((table, nodes), bf16)],
        [
            pl.BlockSpec((block, width), lambda i: (i, 0)),
            pl.BlockSpec((block, table), lambda i: (i, 0)),
            pl.BlockSpec((table, block), lambda i: (0, i)),
        ],
        "local_gather",
        limit=MOST_VMEM,
        grid=(nodes // block,),
        flops=8 * nodes * nodes * width,
        moved=nodes * table * 4,
    )

    activated, grad_pre, terms = call(
        functools.partial(middle_kernel, scale, slots),
        [features, local_sum, by_row, by_col, cotangent, received, w_self, w_neigh, bias],
        [HBM] * 5 + [VMEM] * 4,
        [shape((nodes, width), bf16)] * 2 + [shape((parts, pay, width), bf16)],
        [HBM] * 2 + [whole_block((parts, pay, width))],
        "activate",
        limit=MOST_VMEM,
        scratch=[
            pltpu.VMEM((nodes, width), bf16),
            pltpu.VMEM((nodes, width), f32),
            pltpu.VMEM((nodes, table), bf16),
            pltpu.VMEM((table, nodes), bf16),
            pltpu.VMEM((nodes, width), bf16),
            pltpu.VMEM((nodes, width), bf16),
            pltpu.VMEM((nodes, width), bf16),
            pltpu.VMEM((nodes, width), bf16),
            pltpu.SemaphoreType.DMA((2, nodes // TILE)),
            pltpu.SemaphoreType.DMA((2, 2)),
            pltpu.SemaphoreType.DMA,
            pltpu.SemaphoreType.DMA((2, nodes // TILE)),
        ],
        flops=4 * nodes * table * width,
        moved=nodes * table * 4,
    )
    back = exchange(terms)

    scattered = call(
        scatter_kernel,
        (local_t, grad_pre),
        [whole_block(local_t.shape), whole_block((nodes, width))],
        shape((nodes, width), f32),
        pl.BlockSpec((block, width), lambda i: (i, 0)),
        "local_scatter",
        limit=MOST_VMEM,
        grid=(nodes // block,),
        flops=8 * nodes * nodes * width,
        moved=nodes * width * 6,
    )
    weight_rows, grad_bias, grad_hubs = call(
        functools.partial(sums_kernel, scale, slots, hub_rows),
        (back, w_neigh),
        [VMEM, VMEM],
        [shape((parts, 16, width), bf16), shape((1, width), f32), shape((hub_rows, width), f32)],
        [whole_block((parts, 16, width)), whole_block((1, width)), whole_block((hub_rows, width))],
        "sums",
        limit=MOST_VMEM,
        moved=parts * (pay + 16) * width * 2,
    )
    weights = exchange(weight_rows)

    height = 2 * TILE
    by_height = pl.BlockSpec((height, width), lambda i: (i, 0))
    grad_features = call(
        functools.partial(final_kernel, scale, slots),
        (send_rows, back, scattered, grad_pre, w_self, w_neigh),
        [whole_block(send_rows.shape), whole_block((parts, pay, width)), by_height, by_height]
        + [whole_block((width, width))] * 2,
        shape((nodes, width), f32),
        by_height,
        "return_scatter",
        limit=MOST_VMEM,
        grid=(nodes // height,),
        flops=2 * nodes * parts * slots * width,
        moved=nodes * width * 10,
    )
    weights = weights[: 2 * width // 16].reshape(2, width, width).astype(f32)
    return (activated, grad_features, grad_hubs, weights[0], weights[1], grad_bias.reshape(width))


def solution(mesh):
    split = P(AXES, None)
    return jax.shard_map(
        body,
        mesh=mesh,
        in_specs=(split, split, P(), P(), P(), split, split, split, split, split),
        out_specs=(split, split, split, P(), P(), P()),
        check_vma=False,
    )
```

profile of v0, /device:TPU:0, one launch (start us, length us, event | category | flops | bytes accessed | tf_op | source)
XLA Modules:
  0.0 85.2 jit_solution(13556715197323128909)
XLA Ops:
  0.6 2.8 %pick_rows.1 = bf16[32,32,256]{2,1,0:T(8,128)(2,1)} custom-call(s32[1,512]{1,0:T(1,128)} %send_ref.3, bf16[2048,256]{1,0:T(8,128)(2,1)} %feat_hbm, bf16[16,256]{1,0:T(8,128)(2,1)} %hub_ref.1), custom_call_target="tpu_custom_call" | custom-call | flops 536870912 | bytes 1048576 | tf_op jit(solution)/shard_map/pick_rows/pallas_call | solution.py:252
  3.4 7.3 %all-to-all-start = ((bf16[32,32,256]{2,1,0:T(8,128)(2,1)}), bf16[32,32,256]{2,1,0:T(8,128)(2,1)S(1)}, u32[]{:S(2)}, u32[]{:S(2)}) async-start(bf16[32,32,256]{2,1,0:T(8,128)(2,1)} %pick_rows.1), calls=%async_computation | async-start | bytes 1048576 | tf_op jit(solution)/shard_map/all_to_all | solution.py:294
  10.7 10.2 %local_gather.1 = (f32[2048,256]{1,0:T(8,128)}, bf16[2048,1024]{1,0:T(8,128)(2,1)}, bf16[1024,2048]{1,0:T(8,128)(2,1)}) custom-call(s32[4,2048]{1,0:T(4,128)} %bitcast.11, s32[4,2048]{1,0:T(4,128)} %bitcast.10, s32[2,2048]{1,0:T(2,128)} %bitcast.13, bf16[2048,256]{1,0:T(8,128)(2,1)} %feat_hbm), custom_call_target="tpu_custom_call" | custom-call | flops 8589934592 | bytes 8388608 | tf_op jit(solution)/shard_map/local_gather/pallas_call | solution.py:252
  20.9 6.2 %all-to-all-done.table_ref = bf16[32,32,256]{2,1,0:T(8,128)(2,1)S(1)} async-done(((bf16[32,32,256]{2,1,0:T(8,128)(2,1)}), bf16[32,32,256]{2,1,0:T(8,128)(2,1)S(1)}, u32[]{:S(2)}, u32[]{:S(2)}) %all-to-all-start) | async-done | bytes 524320 | tf_op jit(solution)/shard_map/all_to_all | solution.py:294
  27.1 0.0 copy-start
  27.1 0.8 copy-done
  27.9 11.1 %activate.1 = (bf16[2048,256]{1,0:T(8,128)(2,1)}, bf16[2048,256]{1,0:T(8,128)(2,1)}, bf16[32,56,256]{2,1,0:T(8,128)(2,1)}) custom-call(bf16[2048,256]{1,0:T(8,128)(2,1)} %feat_hbm, f32[2048,256]{1,0:T(8,128)} %get-tuple-element.18.sum_hbm, bf16[2048,1024]{1,0:T(8,128)(2,1)} %get-tuple-element.19.by_row_hbm, bf16[1024,2048]{1,0:T(8,128)(2,1)} %get-tuple-element.20.by_col_hbm, ...), custom_call_target="tpu_custom_call" | custom-call | flops 2147483648 | bytes 8388608 | tf_op jit(solution)/shard_map/activate/pallas_call | solution.py:252
  39.0 28.1 %all_to_all.15.back_ref = bf16[32,56,256]{2,1,0:T(8,128)(2,1)} all-to-all(bf16[32,56,256]{2,1,0:T(8,128)(2,1)} %get-tuple-element.23), channel_id=1, replica_groups=mesh['row'=4,'col'=8] {'row','col'}, dimensions={0} | all-to-all | bytes 1835008 | tf_op jit(solution)/shard_map/all_to_all | solution.py:294
  67.1 2.0 %sums.1 = (bf16[32,16,256]{2,1,0:T(8,128)(2,1)}, f32[1,256]{1,0:T(1,128)}, f32[16,256]{1,0:T(8,128)}) custom-call(bf16[32,56,256]{2,1,0:T(8,128)(2,1)} %all_to_all.15.back_ref, bf16[256,256]{1,0:T(8,128)(2,1)} %wn_ref.5), custom_call_target="tpu_custom_call" | custom-call | bytes 1179648 | tf_op jit(solution)/shard_map/sums/pallas_call | solution.py:252
  69.1 2.6 %all-to-all-start.2 = ((bf16[32,16,256]{2,1,0:T(8,128)(2,1)}), bf16[32,16,256]{2,1,0:T(8,128)(2,1)S(1)}, u32[]{:S(2)}, u32[]{:S(2)}) async-start(bf16[32,16,256]{2,1,0:T(8,128)(2,1)} %get-tuple-element.26), calls=%async_computation.2 | async-start | bytes 524288 | tf_op jit(solution)/shard_map/all_to_all | solution.py:294
  71.7 6.9 %local_scatter.1.scat_ref = f32[2048,256]{1,0:T(8,128)} custom-call(s32[4,2048]{1,0:T(4,128)} %bitcast.12, bf16[2048,256]{1,0:T(8,128)(2,1)} %get-tuple-element.24.grad_ref), custom_call_target="tpu_custom_call" | custom-call | flops 8589934592 | bytes 3145728 | tf_op jit(solution)/shard_map/local_scatter/pallas_call | solution.py:252
  78.6 5.7 %return_scatter.1 = f32[2048,256]{1,0:T(8,128)} custom-call(s32[1,512]{1,0:T(1,128)} %send_ref.3, bf16[32,56,256]{2,1,0:T(8,128)(2,1)} %all_to_all.15.back_ref, f32[2048,256]{1,0:T(8,128)} %local_scatter.1.scat_ref, bf16[2048,256]{1,0:T(8,128)(2,1)} %get-tuple-element.24.grad_ref, bf16[256,256]{1,0:T(8,128)(2,1)} %ws_ref.3, bf16[256,256]{1,0:T(8,128)(2,1)} %wn_ref.5), custom_call_target="tpu_custom_call" | custom-call | flops 536870912 | bytes 5242880 | tf_op jit(solution)/shard_map/return_scatter/pallas_call | solution.py:252
  84.3 0.0 all-to-all-done.2
  84.3 0.8 fusion
Async XLA Ops:
  3.4 23.7 %all-to-all-start = ((bf16[32,32,256]{2,1,0:T(8,128)(2,1)}), bf16[32,32,256]{2,1,0:T(8,128)(2,1)S(1)}, u32[]{:S(2)}, u32[]{:S(2)}) async-start(bf16[32,32,256]{2,1,0:T(8,128)(2,1)} %pick_rows.1), calls=%async_computation | async-start | bytes 1048576 | tf_op jit(solution)/shard_map/all_to_all | solution.py:294
  27.1 0.8 copy-start
  69.1 15.2 %all-to-all-start.2 = ((bf16[32,16,256]{2,1,0:T(8,128)(2,1)}), bf16[32,16,256]{2,1,0:T(8,128)(2,1)S(1)}, u32[]{:S(2)}, u32[]{:S(2)}) async-start(bf16[32,16,256]{2,1,0:T(8,128)(2,1)} %get-tuple-element.26), calls=%async_computation.2 | async-start | bytes 524288 | tf_op jit(solution)/shard_map/all_to_all | solution.py:294
where the time goes:
time: 85.7 us; the launch traced here: 85.2 us
  Pallas kernels  38.6 us (45%)
  blocking collectives  28.1 us (33%)
  starting transfers between devices  9.88 us (12%)
  waiting for transfers between devices  6.17 us (7%)
  local copies, waits for them, and re-layouts  1.67 us (2%)
    pallas_call x6, Pallas kernels, call(): pl.pallas_call(kernel, grid=grid, in_specs=in_specs, out_specs=out_specs,...  38.6 us
    all_to_all x1, blocking collectives, exchange(): return lax.all_to_all(value, AXES, split_axis=0, concat_axis=0, tiled=True)  28.1 us
    all_to_all x2, starting transfers between devices, exchange(): return lax.all_to_all(value, AXES, split_axis=0, concat_axis=0, tiled=True)  9.88 us
    all_to_all x2, waiting for transfers between devices, exchange(): return lax.all_to_all(value, AXES, split_axis=0, concat_axis=0, tiled=True)  6.17 us
  transfers between devices with their start and end apart: 2, of which 1 were waited for; matrix products, arithmetic and copies ran while one was open for 0% of the time, Pallas kernels for 27%

commit v1 on v0

--- a/solution.py
+++ b/solution.py
@@ -10,8 +10,8 @@
 AXES = ("row", "col")
 LANES = 128
 TILE = 256
-MOST_VMEM = 60928 * 1024
-LESS_VMEM = 8 * 1024 * 1024
+MOST_VMEM = 61952 * 1024
+SOME_VMEM = 44 * 1024 * 1024
 NT = (((1,), (1,)), ((), ()))
 TN = (((0,), (0,)), ((), ()))
 VMEM = pl.BlockSpec(memory_space=pltpu.VMEM)
@@ -33,34 +33,39 @@
     return jnp.transpose(jnp.broadcast_to(index_row, (LANES, count))).astype(jnp.int16)
 
 
+def stack_rows(value, height):
+    count = value.shape[1]
+    return jnp.broadcast_to(value[None], (height // 16, 16, count)).reshape(height, count)
+
+
+def count_hits(entries, here):
+    one, zero = jnp.ones(here.shape, bf16), jnp.zeros(here.shape, bf16)
+    total = None
+    for entry in entries:
+        hit = jnp.where(entry == here, one, zero)
+        total = hit if total is None else total + hit
+    return total
+
+
 def hits_by_row(columns, first, width):
     rows = columns[0].shape[0]
-    lane = lax.broadcasted_iota(jnp.int32, (rows, LANES), 1).astype(jnp.int16)
-    one = jnp.ones((rows, LANES), bf16)
-    zero = jnp.zeros((rows, LANES), bf16)
-    tiles = []
-    for start in range(first, first + width, LANES):
-        here = lane + jnp.int16(start)
-        total = None
-        for column in columns:
-            hit = jnp.where(column == here, one, zero)
-            total = hit if total is None else total + hit
-        tiles.append(total)
+    lane = lax.broadcasted_iota(jnp.int32, (16, LANES), 1).astype(jnp.int16)
+    tiles = [
+        count_hits(columns, stack_rows(lane + jnp.int16(start), rows)) for start in range(first, first + width, LANES)
+    ]
     return jnp.concatenate(tiles, axis=1) if len(tiles) > 1 else tiles[0]
 
 
 def hits_by_column(index_rows, first, height):
     count = index_rows[0].shape[1]
-    down = lax.broadcasted_iota(jnp.int32, (height, count), 0).astype(jnp.int16)
-    one = jnp.ones((height, count), bf16)
-    zero = jnp.zeros((height, count), bf16)
-    total = None
-    for row in index_rows:
-        entry = jnp.broadcast_to(row - first, (16, count)).astype(jnp.int16)
-        entry = jnp.broadcast_to(entry[None], (height // 16, 16, count)).reshape(height, count)
-        hit = jnp.where(entry == down, one, zero)
-        total = hit if total is None else total + hit
-    return total
+    group = 64
+    down = lax.broadcasted_iota(jnp.int32, (group, count), 0).astype(jnp.int16)
+    entries = [
+        stack_rows(jnp.broadcast_to(row - first, (16, count)).astype(jnp.int16), group) for row in index_rows
+    ]
+    return jnp.concatenate(
+        [count_hits(entries, down + jnp.int16(start)) for start in range(0, height, group)], axis=0
+    )
 
 
 def dot(a, b, dims=(((1,), (0,)), ((), ()))):
@@ -86,31 +91,23 @@
     out_ref[:, slots:, :] = jnp.broadcast_to(hub_ref[...][None], (parts, hub_rows, width))
 
 
-def local_kernel(split, local_ref, remote_ref, hub_ref, feat_ref, sum_ref, by_row_ref, by_col_ref):
-    nodes = feat_ref.shape[0]
+def local_kernel(local_ref, feat_ref, sum_ref):
     columns = [along_rows(row) for row in index_rows(local_ref, 0, TILE)]
     total = None
-    for first in range(0, nodes, TILE):
+    for first in range(0, feat_ref.shape[0], TILE):
         part = dot(hits_by_row(columns, first, TILE), feat_ref[first : first + TILE, :])
         total = part if total is None else total + part
     sum_ref[...] = total
-    for ref, low, high in ((remote_ref, 0, split), (hub_ref, split, by_row_ref.shape[1])):
-        index = index_rows(ref, 0, TILE)
-        columns = [along_rows(row) for row in index]
-        for first in range(low, high, TILE):
-            by_row_ref[:, first : first + TILE] = hits_by_row(columns, first - low, TILE)
-            by_col_ref[first : first + TILE, :] = hits_by_column(index, first - low, TILE)
 
 
 def middle_kernel(
     scale,
-    slots,
+    remote_ref,
+    hub_ref,
     feat_hbm,
     sum_hbm,
-    by_row_hbm,
-    by_col_hbm,
     cot_hbm,
-    table_ref,
+    table_hbm,
     ws_ref,
     wn_ref,
     bias_ref,
@@ -119,20 +116,22 @@
     pay_ref,
     feat,
     sums,
-    by_row,
+    cot,
+    bound_part,
+    hub_part,
     by_col,
-    cot,
     act,
     grad_all,
     mean_all,
-    block_sem,
+    sum_sem,
     half_sem,
-    col_sem,
+    table_sem,
     out_sem,
 ):
     nodes, width = feat.shape
-    parts, slab, _ = table_ref.shape
-    hub_rows = slab - slots
+    parts, slots, _ = bound_part.shape
+    hub_rows = hub_part.shape[1]
+    slab = slots + hub_rows
     bounds, hubs = parts * slots, parts * hub_rows
     blocks = nodes // TILE
     halves = 2
@@ -140,12 +139,16 @@
     def here(block):
         return slice(block * TILE, (block + 1) * TILE)
 
+    table_loads = [
+        pltpu.make_async_copy(table_hbm.at[:, :slots, :], bound_part, table_sem.at[0]),
+        pltpu.make_async_copy(table_hbm.at[:, slots:, :], hub_part, table_sem.at[1]),
+    ]
+    for copy in table_loads:
+        copy.start()
+
     def loads(block):
         at = here(block)
-        copies = [
-            pltpu.make_async_copy(by_row_hbm.at[at, :], by_row.at[at, :], block_sem.at[0, block]),
-            pltpu.make_async_copy(sum_hbm.at[at, :], sums.at[at, :], block_sem.at[1, block]),
-        ]
+        copies = [pltpu.make_async_copy(sum_hbm.at[at, :], sums.at[at, :], sum_sem.at[block])]
         if block % (blocks // halves) == 0:
             half = block // (blocks // halves)
             at = slice(half * (nodes // halves), (half + 1) * (nodes // halves))
@@ -157,11 +160,23 @@
     for group in coming:
         for copy in group:
             copy.start()
-    col_load = pltpu.make_async_copy(by_col_hbm, by_col, col_sem)
-    col_load.start()
-    table = jnp.concatenate(
-        [table_ref[:, :slots, :].reshape(bounds, width), table_ref[:, slots:, :].reshape(hubs, width)], axis=0
-    )
+
+    def counts(block):
+        start = block * TILE
+        hits = jnp.concatenate(
+            [
+                hits_by_column(index_rows(remote_ref, start, TILE), 0, bounds),
+                hits_by_column(index_rows(hub_ref, start, TILE), 0, hubs),
+            ],
+            axis=0,
+        )
+        by_col[:, here(block)] = hits
+        return hits
+
+    hits = counts(0)
+    for copy in table_loads:
+        copy.wait()
+    table = jnp.concatenate([bound_part[...].reshape(bounds, width), hub_part[...].reshape(hubs, width)], axis=0)
     stores = []
     bias_total = jnp.zeros((1, width), f32)
     total = None
@@ -170,8 +185,9 @@
         if block < blocks:
             for copy in coming[block]:
                 copy.wait()
-            at = here(block)
-            following = sums[at, :] + dot(by_row[at, :], table)
+            following = sums[here(block), :] + dot(hits, table, TN)
+            if block + 1 < blocks:
+                hits = counts(block + 1)
         if block > 0:
             at = here(block - 1)
             mean = (total * scale).astype(bf16)
@@ -198,7 +214,6 @@
     if parts > holders:
         pay_ref[holders:, slab : slab + 16, :] = jnp.zeros((parts - holders, 16, width), bf16)
     pay_ref[:, slab + 16 :, :] = jnp.broadcast_to(high_low(bias_total).astype(bf16)[None], (parts, 8, width))
-    col_load.wait()
     pay_ref[:, :slots, :] = dot(by_col[:bounds, :], grad).astype(bf16).reshape(parts, slots, width)
     pay_ref[:, slots:slab, :] = dot(by_col[bounds:, :], grad).astype(bf16).reshape(parts, hub_rows, width)
     for store in stores:
@@ -247,7 +262,7 @@
 
 
 def call(
-    kernel, ins, in_specs, outs, out_specs, name, grid=(), scratch=(), flops=0, moved=0, limit=LESS_VMEM
+    kernel, ins, in_specs, outs, out_specs, name, grid=(), scratch=(), flops=0, moved=0, limit=SOME_VMEM
 ):
     return pl.pallas_call(
         kernel,
@@ -308,28 +323,23 @@
     received = exchange(sending)
 
     block = TILE
-    local_sum, by_row, by_col = call(
-        functools.partial(local_kernel, parts * slots),
-        (local_t, remote_t, hub_t, features),
-        [pl.BlockSpec((edges.shape[0], block), lambda i: (0, i)) for edges in (local_t, remote_t, hub_t)]
-        + [whole_block((nodes, width))],
-        [shape((nodes, width), f32), shape((nodes, table), bf16), shape((table, nodes), bf16)],
-        [
-            pl.BlockSpec((block, width), lambda i: (i, 0)),
-            pl.BlockSpec((block, table), lambda i: (i, 0)),
-            pl.BlockSpec((table, block), lambda i: (0, i)),
-        ],
+    local_sum = call(
+        local_kernel,
+        (local_t, features),
+        [pl.BlockSpec((local_t.shape[0], block), lambda i: (0, i)), whole_block((nodes, width))],
+        shape((nodes, width), f32),
+        pl.BlockSpec((block, width), lambda i: (i, 0)),
         "local_gather",
         limit=MOST_VMEM,
         grid=(nodes // block,),
         flops=8 * nodes * nodes * width,
-        moved=nodes * table * 4,
+        moved=nodes * width * 6,
     )
 
     activated, grad_pre, terms = call(
-        functools.partial(middle_kernel, scale, slots),
-        [features, local_sum, by_row, by_col, cotangent, received, w_self, w_neigh, bias],
-        [HBM] * 5 + [VMEM] * 4,
+        functools.partial(middle_kernel, scale),
+        [remote_t, hub_t, features, local_sum, cotangent, received, w_self, w_neigh, bias],
+        [VMEM] * 2 + [HBM] * 4 + [VMEM] * 3,
         [shape((nodes, width), bf16)] * 2 + [shape((parts, pay, width), bf16)],
         [HBM] * 2 + [whole_block((parts, pay, width))],
         "activate",
@@ -337,19 +347,20 @@
         scratch=[
             pltpu.VMEM((nodes, width), bf16),
             pltpu.VMEM((nodes, width), f32),
-            pltpu.VMEM((nodes, table), bf16),
+            pltpu.VMEM((nodes, width), bf16),
+            pltpu.VMEM((parts, slots, width), bf16),
+            pltpu.VMEM((parts, hub_rows, width), bf16),
             pltpu.VMEM((table, nodes), bf16),
             pltpu.VMEM((nodes, width), bf16),
             pltpu.VMEM((nodes, width), bf16),
             pltpu.VMEM((nodes, width), bf16),
-            pltpu.VMEM((nodes, width), bf16),
-            pltpu.SemaphoreType.DMA((2, nodes // TILE)),
+            pltpu.SemaphoreType.DMA((nodes // TILE,)),
             pltpu.SemaphoreType.DMA((2, 2)),
-            pltpu.SemaphoreType.DMA,
+            pltpu.SemaphoreType.DMA((2,)),
             pltpu.SemaphoreType.DMA((2, nodes // TILE)),
         ],
         flops=4 * nodes * table * width,
-        moved=nodes * table * 4,
+        moved=nodes * width * 8,
     )
     back = exchange(terms)
 
@@ -360,7 +371,6 @@
         shape((nodes, width), f32),
         pl.BlockSpec((block, width), lambda i: (i, 0)),
         "local_scatter",
-        limit=MOST_VMEM,
         grid=(nodes // block,),
         flops=8 * nodes * nodes * width,
         moved=nodes * width * 6,
@@ -372,7 +382,6 @@
         [shape((parts, 16, width), bf16), shape((1, width), f32), shape((hub_rows, width), f32)],
         [whole_block((parts, 16, width)), whole_block((1, width)), whole_block((hub_rows, width))],
         "sums",
-        limit=MOST_VMEM,
         moved=parts * (pay + 16) * width * 2,
     )
     weights = exchange(weight_rows)
@@ -387,7 +396,6 @@
         shape((nodes, width), f32),
         by_height,
         "return_scatter",
-        limit=MOST_VMEM,
         grid=(nodes // height,),
         flops=2 * nodes * parts * slots * width,
         moved=nodes * width * 10,

time: 85.7 us -> 81.2 us (0.947)
  Pallas kernels: 38.6 us -> 29.2 us
  waiting for transfers between devices: 6.17 us -> 11.5 us
    pallas_call x6, Pallas kernels: 38.6 us -> 29.2 us  [call(): pl.pallas_call(kernel, grid=grid, in_specs=in_specs, out_specs=out_specs,...]
    all_to_all x2, waiting for transfers between devices: 6.17 us -> 11.5 us  [exchange(): return lax.all_to_all(value, AXES, split_axis=0, concat_axis=0, tiled=True)]
  transfers between devices with their start and end apart: 2 -> 2, of which waited for: 1 -> 2; matrix products, arithmetic and copies ran while one was open for 0% -> 0% of each run, Pallas kernels for 27% -> 19%
where the time goes in v1:
time: 81.2 us; the launch traced here: 80.6 us
  Pallas kernels  29.2 us (36%)
  blocking collectives  27.6 us (34%)
  waiting for transfers between devices  11.5 us (14%)
  starting transfers between devices  9.88 us (12%)
  local copies, waits for them, and re-layouts  1.66 us (2%)
    pallas_call x6, Pallas kernels, call(): pl.pallas_call(kernel, grid=grid, in_specs=in_specs, out_specs=out_specs,...  29.2 us
    all_to_all x1, blocking collectives, exchange(): return lax.all_to_all(value, AXES, split_axis=0, concat_axis=0, tiled=True)  27.6 us
    all_to_all x2, waiting for transfers between devices, exchange(): return lax.all_to_all(value, AXES, split_axis=0, concat_axis=0, tiled=True)  11.5 us
    all_to_all x2, starting transfers between devices, exchange(): return lax.all_to_all(value, AXES, split_axis=0, concat_axis=0, tiled=True)  9.88 us
  transfers between devices with their start and end apart: 2, of which 2 were waited for; matrix products, arithmetic and copies ran while one was open for 0% of the time, Pallas kernels for 19%

profile of v1, /device:TPU:0, one launch (start us, length us, event | category | flops | bytes accessed | tf_op | source)
XLA Modules:
  0.0 80.6 jit_solution(16633846461850733454)
XLA Ops:
  0.6 2.8 %pick_rows.1 = bf16[32,32,256]{2,1,0:T(8,128)(2,1)} custom-call(s32[1,512]{1,0:T(1,128)} %send_ref.3, bf16[2048,256]{1,0:T(8,128)(2,1)} %feat_hbm, bf16[16,256]{1,0:T(8,128)(2,1)} %hub_ref.1), custom_call_target="tpu_custom_call" | custom-call | flops 536870912 | bytes 1048576 | tf_op jit(solution)/shard_map/pick_rows/pallas_call | solution.py:267
  3.4 7.3 %all-to-all-start = ((bf16[32,32,256]{2,1,0:T(8,128)(2,1)}), bf16[32,32,256]{2,1,0:T(8,128)(2,1)S(1)}, u32[]{:S(2)}, u32[]{:S(2)}) async-start(bf16[32,32,256]{2,1,0:T(8,128)(2,1)} %pick_rows.1), calls=%async_computation | async-start | bytes 1048576 | tf_op jit(solution)/shard_map/all_to_all | solution.py:309
  10.7 7.3 %local_gather.1.sum_hbm = f32[2048,256]{1,0:T(8,128)} custom-call(s32[4,2048]{1,0:T(4,128)} %bitcast.7, bf16[2048,256]{1,0:T(8,128)(2,1)} %feat_hbm), custom_call_target="tpu_custom_call" | custom-call | flops 8589934592 | bytes 3145728 | tf_op jit(solution)/shard_map/local_gather/pallas_call | solution.py:267
  18.0 9.0 %all-to-all-done.table_hbm = bf16[32,32,256]{2,1,0:T(8,128)(2,1)S(1)} async-done(((bf16[32,32,256]{2,1,0:T(8,128)(2,1)}), bf16[32,32,256]{2,1,0:T(8,128)(2,1)S(1)}, u32[]{:S(2)}, u32[]{:S(2)}) %all-to-all-start) | async-done | bytes 524320 | tf_op jit(solution)/shard_map/all_to_all | solution.py:309
  27.1 0.0 copy-start.5
  27.1 0.8 copy-done.5
  27.9 0.0 copy-start.1
  27.9 10.2 %activate.1 = (bf16[2048,256]{1,0:T(8,128)(2,1)}, bf16[2048,256]{1,0:T(8,128)(2,1)}, bf16[32,56,256]{2,1,0:T(8,128)(2,1)}) custom-call(s32[4,2048]{1,0:T(4,128)} %bitcast.11, s32[2,2048]{1,0:T(2,128)} %bitcast.12, bf16[2048,256]{1,0:T(8,128)(2,1)} %feat_hbm, f32[2048,256]{1,0:T(8,128)} %local_gather.1.sum_hbm, bf16[2048,256]{1,0:T(8,128)(2,1)} %cot_hbm.1, ...), custom_call_target="tpu_custom_call" | custom-call | flops 2147483648 | bytes 4194304 | tf_op jit(solution)/shard_map/activate/pallas_call | solution.py:267
  38.1 0.0 copy-start
  38.1 0.0 copy-start.4
  38.1 27.6 %all_to_all.15.back_ref = bf16[32,56,256]{2,1,0:T(8,128)(2,1)S(1)} all-to-all(bf16[32,56,256]{2,1,0:T(8,128)(2,1)} %get-tuple-element.17), channel_id=1, replica_groups=mesh['row'=4,'col'=8] {'row','col'}, dimensions={0} | all-to-all | bytes 1835008 | tf_op jit(solution)/shard_map/all_to_all | solution.py:309
  65.7 0.0 copy-done.1
  65.7 0.8 %sums.1 = (bf16[32,16,256]{2,1,0:T(8,128)(2,1)}, f32[1,256]{1,0:T(1,128)}, f32[16,256]{1,0:T(8,128)}) custom-call(bf16[32,56,256]{2,1,0:T(8,128)(2,1)S(1)} %all_to_all.15.back_ref, bf16[256,256]{1,0:T(8,128)(2,1)S(1)} %copy-done.1), custom_call_target="tpu_custom_call" | custom-call | bytes 1179648 | tf_op jit(solution)/shard_map/sums/pallas_call | solution.py:267
  66.5 2.6 %all-to-all-start.2 = ((bf16[32,16,256]{2,1,0:T(8,128)(2,1)}), bf16[32,16,256]{2,1,0:T(8,128)(2,1)S(1)}, u32[]{:S(2)}, u32[]{:S(2)}) async-start(bf16[32,16,256]{2,1,0:T(8,128)(2,1)} %get-tuple-element.20), calls=%async_computation.2 | async-start | bytes 524288 | tf_op jit(solution)/shard_map/all_to_all | solution.py:309
  69.1 0.0 copy-done
  69.1 0.0 copy-done.4
  69.1 0.0 copy-start.2
  69.1 0.0 copy-start.3
  69.1 4.4 %local_scatter.1.scat_ref = f32[2048,256]{1,0:T(8,128)S(1)} custom-call(s32[4,2048]{1,0:T(4,128)S(1)} %bitcast.8, bf16[2048,256]{1,0:T(8,128)(2,1)S(1)} %copy-done), custom_call_target="tpu_custom_call" | custom-call | flops 8589934592 | bytes 3145728 | tf_op jit(solution)/shard_map/local_scatter/pallas_call | solution.py:267
  73.6 0.0 copy-done.2
  73.6 0.0 copy-done.3
  73.6 3.6 %return_scatter.1 = f32[2048,256]{1,0:T(8,128)} custom-call(s32[1,512]{1,0:T(1,128)S(1)} %copy-done.3, bf16[32,56,256]{2,1,0:T(8,128)(2,1)S(1)} %all_to_all.15.back_ref, f32[2048,256]{1,0:T(8,128)S(1)} %local_scatter.1.scat_ref, bf16[2048,256]{1,0:T(8,128)(2,1)S(1)} %copy-done, bf16[256,256]{1,0:T(8,128)(2,1)S(1)} %copy-done.2, bf16[256,256]{1,0:T(8,128)(2,1)S(1)} %copy-done.1), custom_call_target="tpu_custom_call" | custom-call | flops 536870912 | bytes 5242880 | tf_op jit(solution)/shard_map/return_scatter/pallas_call | solution.py:267
  77.2 2.5 %all-to-all-done.2 = bf16[32,16,256]{2,1,0:T(8,128)(2,1)S(1)} async-done(((bf16[32,16,256]{2,1,0:T(8,128)(2,1)}), bf16[32,16,256]{2,1,0:T(8,128)(2,1)S(1)}, u32[]{:S(2)}, u32[]{:S(2)}) %all-to-all-start.2) | async-done | bytes 262176 | tf_op jit(solution)/shard_map/all_to_all | solution.py:309
  79.7 0.8 %fusion = (f32[16,16,256]{2,1,0:T(8,128)}, f32[16,16,256]{2,1,0:T(8,128)}) fusion(bf16[32,16,256]{2,1,0:T(8,128)(2,1)S(1)} %all-to-all-done.2), kind=kLoop, calls=%fused_computation | loop fusion | bytes 1048576 | tf_op jit(solution)/shard_map/slice | solution.py:404
Async XLA Ops:
  3.4 23.7 %all-to-all-start = ((bf16[32,32,256]{2,1,0:T(8,128)(2,1)}), bf16[32,32,256]{2,1,0:T(8,128)(2,1)S(1)}, u32[]{:S(2)}, u32[]{:S(2)}) async-start(bf16[32,32,256]{2,1,0:T(8,128)(2,1)} %pick_rows.1), calls=%async_computation | async-start | bytes 1048576 | tf_op jit(solution)/shard_map/all_to_all | solution.py:309
  27.1 0.8 copy-start.5
  27.9 37.8 %copy-start.1 = (bf16[256,256]{1,0:T(8,128)(2,1)S(1)}, bf16[256,256]{1,0:T(8,128)(2,1)}, u32[]{:S(2)}) copy-start(bf16[256,256]{1,0:T(8,128)(2,1)} %wn_ref.5) | copy-start | bytes 393220
  38.1 31.0 %copy-start = (bf16[2048,256]{1,0:T(8,128)(2,1)S(1)}, bf16[2048,256]{1,0:T(8,128)(2,1)}, u32[]{:S(2)}) copy-start(bf16[2048,256]{1,0:T(8,128)(2,1)} %get-tuple-element.18.grad_ref) | copy-start | bytes 3145732
  38.1 31.0 %copy-start.4 = (s32[2048,4]{0,1:T(4,128)S(1)}, s32[2048,4]{0,1:T(4,128)}, u32[]{:S(2)}) copy-start(s32[2048,4]{0,1:T(4,128)} %param.15) | copy-start | bytes 98308
  66.5 13.2 %all-to-all-start.2 = ((bf16[32,16,256]{2,1,0:T(8,128)(2,1)}), bf16[32,16,256]{2,1,0:T(8,128)(2,1)S(1)}, u32[]{:S(2)}, u32[]{:S(2)}) async-start(bf16[32,16,256]{2,1,0:T(8,128)(2,1)} %get-tuple-element.20), calls=%async_computation.2 | async-start | bytes 524288 | tf_op jit(solution)/shard_map/all_to_all | solution.py:309
  69.1 4.5 %copy-start.2 = (bf16[256,256]{1,0:T(8,128)(2,1)S(1)}, bf16[256,256]{1,0:T(8,128)(2,1)}, u32[]{:S(2)}) copy-start(bf16[256,256]{1,0:T(8,128)(2,1)} %ws_ref.3) | copy-start | bytes 393220
  69.1 4.5 %copy-start.3 = (s32[1,512]{1,0:T(1,128)S(1)}, s32[1,512]{1,0:T(1,128)}, u32[]{:S(2)}) copy-start(s32[1,512]{1,0:T(1,128)} %send_ref.3) | copy-start | bytes 6148

commit v2 on v1

--- a/solution.py
+++ b/solution.py
@@ -76,19 +76,41 @@
     return [ref[j : j + 1, pl.ds(start, count)] for j in range(ref.shape[0])]
 
 
-def pick_kernel(send_ref, feat_ref, hub_ref, out_ref):
+def pick_kernel(send_hbm, feat_hbm, hub_hbm, out_ref, send_ref, feat_ref, hub_ref, small_sem, feat_sem):
     parts, slab, width = out_ref.shape
+    nodes = feat_ref.shape[0]
     hub_rows = hub_ref.shape[0]
     slots = slab - hub_rows
     total = send_ref.shape[1]
     step = min(512, total)
-    for start in range(0, total, step):
-        column = along_rows(send_ref[:, start : start + step])
-        picked = dot(hits_by_row([column], 0, feat_ref.shape[0]), feat_ref[...])
+    chunk = nodes // 4
+    small = [
+        pltpu.make_async_copy(send_hbm, send_ref, small_sem.at[0]),
+        pltpu.make_async_copy(hub_hbm, hub_ref, small_sem.at[1]),
+    ]
+    chunks = [slice(k * chunk, (k + 1) * chunk) for k in range(4)]
+    loads = [
+        pltpu.make_async_copy(feat_hbm.at[at, :], feat_ref.at[at, :], feat_sem.at[k]) for k, at in enumerate(chunks)
+    ]
+    small[0].start()
+    for load in loads:
+        load.start()
+    small[1].start()
+    small[0].wait()
+    starts = range(0, total, step)
+    hits = [hits_by_row([along_rows(send_ref[:, start : start + step])], 0, nodes) for start in starts]
+    small[1].wait()
+    out_ref[:, slots:, :] = jnp.broadcast_to(hub_ref[...][None], (parts, hub_rows, width))
+    picked = [None] * len(hits)
+    for load, at in zip(loads, chunks):
+        load.wait()
+        for k, hit in enumerate(hits):
+            part = dot(hit[:, at], feat_ref[at, :])
+            picked[k] = part if picked[k] is None else picked[k] + part
+    for start, rows in zip(starts, picked):
         out_ref[start // slots : (start + step) // slots, :slots, :] = (
-            picked.astype(bf16).reshape(step // slots, slots, width)
+            rows.astype(bf16).reshape(step // slots, slots, width)
         )
-    out_ref[:, slots:, :] = jnp.broadcast_to(hub_ref[...][None], (parts, hub_rows, width))
 
 
 def local_kernel(local_ref, feat_ref, sum_ref):
@@ -102,81 +124,100 @@
 
 def middle_kernel(
     scale,
-    remote_ref,
-    hub_ref,
+    remote_hbm,
+    hub_hbm,
     feat_hbm,
     sum_hbm,
     cot_hbm,
     table_hbm,
-    ws_ref,
-    wn_ref,
-    bias_ref,
+    ws_hbm,
+    wn_hbm,
+    bias_hbm,
     act_hbm,
     grad_hbm,
-    pay_ref,
+    pay_hbm,
+    remote_ref,
+    hub_ref,
     feat,
     sums,
     cot,
     bound_part,
     hub_part,
+    ws_ref,
+    wn_ref,
+    bias_ref,
     by_col,
     act,
     grad_all,
     mean_all,
-    sum_sem,
-    half_sem,
-    table_sem,
+    bound_pay,
+    hub_pay,
+    weight_pay,
+    small_sem,
+    block_sem,
     out_sem,
+    pay_sem,
 ):
     nodes, width = feat.shape
     parts, slots, _ = bound_part.shape
     hub_rows = hub_part.shape[1]
     slab = slots + hub_rows
     bounds, hubs = parts * slots, parts * hub_rows
-    blocks = nodes // TILE
-    halves = 2
+    size = 2 * TILE
+    blocks = nodes // size
 
     def here(block):
-        return slice(block * TILE, (block + 1) * TILE)
-
-    table_loads = [
-        pltpu.make_async_copy(table_hbm.at[:, :slots, :], bound_part, table_sem.at[0]),
-        pltpu.make_async_copy(table_hbm.at[:, slots:, :], hub_part, table_sem.at[1]),
-    ]
-    for copy in table_loads:
-        copy.start()
+        return slice(block * size, (block + 1) * size)
 
     def loads(block):
         at = here(block)
-        copies = [pltpu.make_async_copy(sum_hbm.at[at, :], sums.at[at, :], sum_sem.at[block])]
-        if block % (blocks // halves) == 0:
-            half = block // (blocks // halves)
-            at = slice(half * (nodes // halves), (half + 1) * (nodes // halves))
-            copies.append(pltpu.make_async_copy(feat_hbm.at[at, :], feat.at[at, :], half_sem.at[0, half]))
-            copies.append(pltpu.make_async_copy(cot_hbm.at[at, :], cot.at[at, :], half_sem.at[1, half]))
-        return copies
-
+        return [
+            pltpu.make_async_copy(source.at[at, :], target.at[at, :], block_sem.at[which, block])
+            for which, (source, target) in enumerate(((sum_hbm, sums), (feat_hbm, feat), (cot_hbm, cot)))
+        ]
+
+    small = [
+        pltpu.make_async_copy(source, target, small_sem.at[which])
+        for which, (source, target) in enumerate(
+            (
+                (remote_hbm, remote_ref),
+                (hub_hbm, hub_ref),
+                (table_hbm.at[:, :slots, :], bound_part),
+                (table_hbm.at[:, slots:, :], hub_part),
+                (ws_hbm, ws_ref),
+                (wn_hbm, wn_ref),
+                (bias_hbm, bias_ref),
+            )
+        )
+    ]
+    for copy in small:
+        copy.start()
     coming = [loads(block) for block in range(blocks)]
     for group in coming:
         for copy in group:
             copy.start()
 
     def counts(block):
-        start = block * TILE
+        start = block * size
         hits = jnp.concatenate(
             [
-                hits_by_column(index_rows(remote_ref, start, TILE), 0, bounds),
-                hits_by_column(index_rows(hub_ref, start, TILE), 0, hubs),
+                hits_by_column(index_rows(remote_ref, start, size), 0, bounds),
+                hits_by_column(index_rows(hub_ref, start, size), 0, hubs),
             ],
             axis=0,
         )
         by_col[:, here(block)] = hits
         return hits
 
+    small[0].wait()
+    small[1].wait()
     hits = counts(0)
-    for copy in table_loads:
+    for copy in small[2:]:
         copy.wait()
-    table = jnp.concatenate([bound_part[...].reshape(bounds, width), hub_part[...].reshape(hubs, width)], axis=0)
+    table = jnp.concatenate(
+        [jnp.transpose(bound_part[...].reshape(bounds, width)), jnp.transpose(hub_part[...].reshape(hubs, width))],
+        axis=1,
+    )
     stores = []
     bias_total = jnp.zeros((1, width), f32)
     total = None
@@ -185,7 +226,7 @@
         if block < blocks:
             for copy in coming[block]:
                 copy.wait()
-            following = sums[here(block), :] + dot(hits, table, TN)
+            following = sums[here(block), :] + jnp.transpose(dot(table, hits))
             if block + 1 < blocks:
                 hits = counts(block + 1)
         if block > 0:
@@ -205,17 +246,26 @@
                 stores.append(store)
         total = following
     grad = grad_all[...]
+
+    def send(source, first, which):
+        store = pltpu.make_async_copy(source, pay_hbm.at[:, first : first + source.shape[1], :], pay_sem.at[which])
+        store.start()
+        stores.append(store)
+
+    bound_pay[...] = dot(by_col[:bounds, :], grad).astype(bf16).reshape(parts, slots, width)
+    send(bound_pay, 0, 0)
+    hub_pay[...] = dot(by_col[bounds:, :], grad).astype(bf16).reshape(parts, hub_rows, width)
+    send(hub_pay, slots, 1)
     holders = 2 * width // 16
     per = holders // 2
+    weight_pay[:, 16:, :] = jnp.broadcast_to(high_low(bias_total).astype(bf16)[None], (parts, 8, width))
     for which, source in enumerate((feat, mean_all)):
-        pay_ref[which * per : (which + 1) * per, slab : slab + 16, :] = (
+        weight_pay[which * per : (which + 1) * per, :16, :] = (
             dot(source[...], grad, TN).astype(bf16).reshape(per, 16, width)
         )
     if parts > holders:
-        pay_ref[holders:, slab : slab + 16, :] = jnp.zeros((parts - holders, 16, width), bf16)
-    pay_ref[:, slab + 16 :, :] = jnp.broadcast_to(high_low(bias_total).astype(bf16)[None], (parts, 8, width))
-    pay_ref[:, :slots, :] = dot(by_col[:bounds, :], grad).astype(bf16).reshape(parts, slots, width)
-    pay_ref[:, slots:slab, :] = dot(by_col[bounds:, :], grad).astype(bf16).reshape(parts, hub_rows, width)
+        weight_pay[holders:, :16, :] = jnp.zeros((parts - holders, 16, width), bf16)
+    send(weight_pay, slab, 2)
     for store in stores:
         store.wait()
 
@@ -235,6 +285,10 @@
     high = hub.astype(bf16)
     low = (hub - high.astype(f32)).astype(bf16)
     hub_ref[...] = (dot(high, wn_ref[...], NT) + dot(low, wn_ref[...], NT)) * scale
+
+
+def spread_kernel(in_ref, out_ref):
+    out_ref[...] = jnp.broadcast_to(in_ref[...][None], out_ref.shape)
 
 
 def scatter_kernel(local_ref, grad_ref, out_ref):
@@ -295,7 +349,8 @@
 ):
     nodes, width = features.shape
     hub_rows = hub_features.shape[0]
-    parts = lax.axis_size(AXES)
+    rows, cols = lax.axis_size("row"), lax.axis_size("col")
+    parts = rows * cols
     slots = send_rows.shape[1] // parts
     slab = slots + hub_rows
     pay = slab + 24
@@ -305,17 +360,24 @@
     bias = out_bias.reshape(1, width)
     shape = jax.ShapeDtypeStruct
 
-    def exchange(value):
-        return lax.all_to_all(value, AXES, split_axis=0, concat_axis=0, tiled=True)
+    def exchange(value, axes=AXES):
+        return lax.all_to_all(value, axes, split_axis=0, concat_axis=0, tiled=True)
 
     sending = call(
         pick_kernel,
         (send_rows, features, hub_features),
-        [VMEM, VMEM, VMEM],
+        [HBM] * 3,
         shape((parts, slab, width), bf16),
         whole_block((parts, slab, width)),
         "pick_rows",
         limit=MOST_VMEM,
+        scratch=[
+            pltpu.VMEM(send_rows.shape, jnp.int32),
+            pltpu.VMEM((nodes, width), bf16),
+            pltpu.VMEM((hub_rows, width), bf16),
+            pltpu.SemaphoreType.DMA((2,)),
+            pltpu.SemaphoreType.DMA((4,)),
+        ],
         flops=2 * parts * slots * nodes * width,
         moved=nodes * width * 2,
     )
@@ -339,25 +401,33 @@
     activated, grad_pre, terms = call(
         functools.partial(middle_kernel, scale),
         [remote_t, hub_t, features, local_sum, cotangent, received, w_self, w_neigh, bias],
-        [VMEM] * 2 + [HBM] * 4 + [VMEM] * 3,
+        [HBM] * 9,
         [shape((nodes, width), bf16)] * 2 + [shape((parts, pay, width), bf16)],
-        [HBM] * 2 + [whole_block((parts, pay, width))],
+        [HBM] * 3,
         "activate",
         limit=MOST_VMEM,
         scratch=[
+            pltpu.VMEM(remote_t.shape, jnp.int32),
+            pltpu.VMEM(hub_t.shape, jnp.int32),
             pltpu.VMEM((nodes, width), bf16),
             pltpu.VMEM((nodes, width), f32),
             pltpu.VMEM((nodes, width), bf16),
             pltpu.VMEM((parts, slots, width), bf16),
             pltpu.VMEM((parts, hub_rows, width), bf16),
+            pltpu.VMEM((width, width), bf16),
+            pltpu.VMEM((width, width), bf16),
+            pltpu.VMEM((1, width), f32),
             pltpu.VMEM((table, nodes), bf16),
             pltpu.VMEM((nodes, width), bf16),
             pltpu.VMEM((nodes, width), bf16),
             pltpu.VMEM((nodes, width), bf16),
-            pltpu.SemaphoreType.DMA((nodes // TILE,)),
-            pltpu.SemaphoreType.DMA((2, 2)),
-            pltpu.SemaphoreType.DMA((2,)),
-            pltpu.SemaphoreType.DMA((2, nodes // TILE)),
+            pltpu.VMEM((parts, slots, width), bf16),
+            pltpu.VMEM((parts, hub_rows, width), bf16),
+            pltpu.VMEM((parts, 24, width), bf16),
+            pltpu.SemaphoreType.DMA((7,)),
+            pltpu.SemaphoreType.DMA((3, nodes // (2 * TILE))),
+            pltpu.SemaphoreType.DMA((2, nodes // (2 * TILE))),
+            pltpu.SemaphoreType.DMA((3,)),
         ],
         flops=4 * nodes * table * width,
         moved=nodes * width * 8,
@@ -379,12 +449,22 @@
         functools.partial(sums_kernel, scale, slots, hub_rows),
         (back, w_neigh),
         [VMEM, VMEM],
-        [shape((parts, 16, width), bf16), shape((1, width), f32), shape((hub_rows, width), f32)],
-        [whole_block((parts, 16, width)), whole_block((1, width)), whole_block((hub_rows, width))],
+        [shape((cols, 16, width), bf16), shape((1, width), f32), shape((hub_rows, width), f32)],
+        [whole_block((cols, 16, width)), whole_block((1, width)), whole_block((hub_rows, width))],
         "sums",
         moved=parts * (pay + 16) * width * 2,
     )
-    weights = exchange(weight_rows)
+    weight_rows = exchange(weight_rows, "col").reshape(cols * 16, width)
+    weight_rows = call(
+        spread_kernel,
+        (weight_rows,),
+        [VMEM],
+        shape((rows, cols * 16, width), bf16),
+        whole_block((rows, cols * 16, width)),
+        "spread_weights",
+        moved=parts * 16 * width * 2,
+    )
+    weights = exchange(weight_rows, "row").reshape(parts, 16, width)
 
     height = 2 * TILE
     by_height = pl.BlockSpec((height, width), lambda i: (i, 0))

time: 81.2 us -> 88.8 us (1.094)
  blocking collectives: 27.6 us -> 36.9 us
  waiting for transfers between devices: 11.5 us -> 9.03 us
    all_to_all x1 -> x2, blocking collectives: 27.6 us -> 36.9 us  [exchange(): return lax.all_to_all(value, axes, split_axis=0, concat_axis=0, tiled=True)]
    all_to_all x2, waiting for transfers between devices: 11.5 us -> 9.03 us  [exchange(): return lax.all_to_all(value, axes, split_axis=0, concat_axis=0, tiled=True)]
    pallas_call x6 -> x7, Pallas kernels: 29.2 us -> 29.1 us  [call(): pl.pallas_call(kernel, grid=grid, in_specs=in_specs, out_specs=out_specs,...]
  transfers between devices with their start and end apart: 2 -> 2, of which waited for: 2 -> 1; matrix products, arithmetic and copies ran while one was open for 0% -> 0% of each run, Pallas kernels for 19% -> 17%
where the time goes in v2:
time: 88.8 us; the launch traced here: 88.1 us
  blocking collectives  36.9 us (42%)
  Pallas kernels  29.1 us (33%)
  starting transfers between devices  10.7 us (12%)
  waiting for transfers between devices  9.03 us (10%)
  local copies, waits for them, and re-layouts  1.65 us (2%)
    all_to_all x2, blocking collectives, exchange(): return lax.all_to_all(value, axes, split_axis=0, concat_axis=0, tiled=True)  36.9 us
    pallas_call x7, Pallas kernels, call(): pl.pallas_call(kernel, grid=grid, in_specs=in_specs, out_specs=out_specs,...  29.1 us
    all_to_all x2, starting transfers between devices, exchange(): return lax.all_to_all(value, axes, split_axis=0, concat_axis=0, tiled=True)  10.7 us
    all_to_all x2, waiting for transfers between devices, exchange(): return lax.all_to_all(value, axes, split_axis=0, concat_axis=0, tiled=True)  9.03 us
  transfers between devices with their start and end apart: 2, of which 1 were waited for; matrix products, arithmetic and copies ran while one was open for 0% of the time, Pallas kernels for 17%

profile of v2, /device:TPU:0, one launch (start us, length us, event | category | flops | bytes accessed | tf_op | source)
XLA Modules:
  0.0 88.1 jit_solution(7816261641435721435)
XLA Ops:
  0.6 3.4 %pick_rows.1 = bf16[32,32,256]{2,1,0:T(8,128)(2,1)} custom-call(s32[1,512]{1,0:T(1,128)} %send_ref.1, bf16[2048,256]{1,0:T(8,128)(2,1)} %feat_hbm.2, bf16[16,256]{1,0:T(8,128)(2,1)} %hub_hbm.1), custom_call_target="tpu_custom_call" | custom-call | flops 536870912 | bytes 1048576 | tf_op jit(solution)/shard_map/pick_rows/pallas_call | solution.py:321
  4.0 7.3 %all-to-all-start = ((bf16[32,32,256]{2,1,0:T(8,128)(2,1)}), bf16[32,32,256]{2,1,0:T(8,128)(2,1)S(1)}, u32[]{:S(2)}, u32[]{:S(2)}) async-start(bf16[32,32,256]{2,1,0:T(8,128)(2,1)} %pick_rows.1), calls=%async_computation | async-start | bytes 1048576 | tf_op jit(solution)/shard_map/all_to_all | solution.py:364
  11.3 7.3 %local_gather.1.sum_hbm = f32[2048,256]{1,0:T(8,128)} custom-call(s32[4,2048]{1,0:T(4,128)} %bitcast.9, bf16[2048,256]{1,0:T(8,128)(2,1)} %feat_hbm.2), custom_call_target="tpu_custom_call" | custom-call | flops 8589934592 | bytes 3145728 | tf_op jit(solution)/shard_map/local_gather/pallas_call | solution.py:321
  18.7 9.0 %all-to-all-done.table_hbm = bf16[32,32,256]{2,1,0:T(8,128)(2,1)S(1)} async-done(((bf16[32,32,256]{2,1,0:T(8,128)(2,1)}), bf16[32,32,256]{2,1,0:T(8,128)(2,1)S(1)}, u32[]{:S(2)}, u32[]{:S(2)}) %all-to-all-start) | async-done | bytes 524320 | tf_op jit(solution)/shard_map/all_to_all | solution.py:364
  27.7 0.0 copy-start.5
  27.7 0.8 copy-done.5
  28.5 0.0 copy-start.1
  28.5 8.8 %activate.1 = (bf16[2048,256]{1,0:T(8,128)(2,1)}, bf16[2048,256]{1,0:T(8,128)(2,1)}, bf16[32,56,256]{2,1,0:T(8,128)(2,1)}) custom-call(s32[4,2048]{1,0:T(4,128)} %bitcast.13, s32[2,2048]{1,0:T(2,128)} %bitcast.14, bf16[2048,256]{1,0:T(8,128)(2,1)} %feat_hbm.2, f32[2048,256]{1,0:T(8,128)} %local_gather.1.sum_hbm, bf16[2048,256]{1,0:T(8,128)(2,1)} %cot_hbm.1, ...), custom_call_target="tpu_custom_call" | custom-call | flops 2147483648 | bytes 4194304 | tf_op jit(solution)/shard_map/activate/pallas_call | solution.py:321
  37.3 0.0 copy-start
  37.3 0.0 copy-start.4
  37.3 27.6 %all_to_all.20.back_ref = bf16[32,56,256]{2,1,0:T(8,128)(2,1)S(1)} all-to-all(bf16[32,56,256]{2,1,0:T(8,128)(2,1)} %get-tuple-element.17), channel_id=1, replica_groups=mesh['row'=4,'col'=8] {'row','col'}, dimensions={0} | all-to-all | bytes 1835008 | tf_op jit(solution)/shard_map/all_to_all | solution.py:364
  64.9 0.0 copy-done.1
  64.9 0.8 sums.1
  65.7 9.4 %all_to_all.21 = bf16[8,16,256]{2,1,0:T(8,128)(2,1)S(1)} all-to-all(bf16[8,16,256]{2,1,0:T(8,128)(2,1)S(1)} %get-tuple-element.20), channel_id=1, replica_groups=mesh['row'=4,'col'=8] {'col'}, dimensions={0} | all-to-all | bytes 131072 | tf_op jit(solution)/shard_map/all_to_all | solution.py:364
  75.0 0.7 spread_weights.1
  75.7 3.4 %all-to-all-start.3 = ((bf16[4,128,256]{2,1,0:T(8,128)(2,1)}), bf16[4,128,256]{2,1,0:T(8,128)(2,1)S(1)}, u32[]{:S(2)}, u32[]{:S(2)}) async-start(bf16[4,128,256]{2,1,0:T(8,128)(2,1)} %spread_weights.1), calls=%async_computation.3 | async-start | bytes 524288 | tf_op jit(solution)/shard_map/all_to_all | solution.py:364
  79.2 0.0 copy-done
  79.2 0.0 copy-done.4
  79.2 0.0 copy-start.2
  79.2 0.0 copy-start.3
  79.2 4.4 %local_scatter.1.scat_ref = f32[2048,256]{1,0:T(8,128)S(1)} custom-call(s32[4,2048]{1,0:T(4,128)S(1)} %bitcast.10, bf16[2048,256]{1,0:T(8,128)(2,1)S(1)} %copy-done), custom_call_target="tpu_custom_call" | custom-call | flops 8589934592 | bytes 3145728 | tf_op jit(solution)/shard_map/local_scatter/pallas_call | solution.py:321
  83.6 0.0 copy-done.2
  83.6 0.0 copy-done.3
  83.7 3.6 %return_scatter.1 = f32[2048,256]{1,0:T(8,128)} custom-call(s32[1,512]{1,0:T(1,128)S(1)} %copy-done.3, bf16[32,56,256]{2,1,0:T(8,128)(2,1)S(1)} %all_to_all.20.back_ref, f32[2048,256]{1,0:T(8,128)S(1)} %local_scatter.1.scat_ref, bf16[2048,256]{1,0:T(8,128)(2,1)S(1)} %copy-done, bf16[256,256]{1,0:T(8,128)(2,1)S(1)} %copy-done.2, bf16[256,256]{1,0:T(8,128)(2,1)S(1)} %copy-done.1), custom_call_target="tpu_custom_call" | custom-call | flops 536870912 | bytes 5242880 | tf_op jit(solution)/shard_map/return_scatter/pallas_call | solution.py:321
  87.3 0.0 all-to-all-done.3
  87.3 0.8 fusion
Async XLA Ops:
  4.0 23.7 %all-to-all-start = ((bf16[32,32,256]{2,1,0:T(8,128)(2,1)}), bf16[32,32,256]{2,1,0:T(8,128)(2,1)S(1)}, u32[]{:S(2)}, u32[]{:S(2)}) async-start(bf16[32,32,256]{2,1,0:T(8,128)(2,1)} %pick_rows.1), calls=%async_computation | async-start | bytes 1048576 | tf_op jit(solution)/shard_map/all_to_all | solution.py:364
  27.7 0.8 copy-start.5
  28.5 36.4 %copy-start.1 = (bf16[256,256]{1,0:T(8,128)(2,1)S(1)}, bf16[256,256]{1,0:T(8,128)(2,1)}, u32[]{:S(2)}) copy-start(bf16[256,256]{1,0:T(8,128)(2,1)} %wn_ref.3) | copy-start | bytes 393220
  37.3 41.9 %copy-start = (bf16[2048,256]{1,0:T(8,128)(2,1)S(1)}, bf16[2048,256]{1,0:T(8,128)(2,1)}, u32[]{:S(2)}) copy-start(bf16[2048,256]{1,0:T(8,128)(2,1)} %get-tuple-element.18.grad_ref) | copy-start | bytes 3145732
  37.3 41.9 %copy-start.4 = (s32[2048,4]{0,1:T(4,128)S(1)}, s32[2048,4]{0,1:T(4,128)}, u32[]{:S(2)}) copy-start(s32[2048,4]{0,1:T(4,128)} %param.15) | copy-start | bytes 98308
  75.7 11.6 %all-to-all-start.3 = ((bf16[4,128,256]{2,1,0:T(8,128)(2,1)}), bf16[4,128,256]{2,1,0:T(8,128)(2,1)S(1)}, u32[]{:S(2)}, u32[]{:S(2)}) async-start(bf16[4,128,256]{2,1,0:T(8,128)(2,1)} %spread_weights.1), calls=%async_computation.3 | async-start | bytes 524288 | tf_op jit(solution)/shard_map/all_to_all | solution.py:364
  79.2 4.5 %copy-start.2 = (bf16[256,256]{1,0:T(8,128)(2,1)S(1)}, bf16[256,256]{1,0:T(8,128)(2,1)}, u32[]{:S(2)}) copy-start(bf16[256,256]{1,0:T(8,128)(2,1)} %ws_ref.1) | copy-start | bytes 393220
  79.2 4.5 %copy-start.3 = (s32[1,512]{1,0:T(1,128)S(1)}, s32[1,512]{1,0:T(1,128)}, u32[]{:S(2)}) copy-start(s32[1,512]{1,0:T(1,128)} %send_ref.1) | copy-start | bytes 6148

commit v3 on v1

--- a/solution.py
+++ b/solution.py
@@ -11,6 +11,7 @@
 LANES = 128
 TILE = 256
 MOST_VMEM = 61952 * 1024
+MUCH_VMEM = 60500 * 1024
 SOME_VMEM = 44 * 1024 * 1024
 NT = (((1,), (1,)), ((), ()))
 TN = (((0,), (0,)), ((), ()))
@@ -91,70 +92,68 @@
     out_ref[:, slots:, :] = jnp.broadcast_to(hub_ref[...][None], (parts, hub_rows, width))
 
 
-def local_kernel(local_ref, feat_ref, sum_ref):
+def local_kernel(split, local_ref, remote_ref, hub_ref, feat_ref, own_ref, cot_ref, sum_ref, pack_ref):
+    nodes, width = feat_ref.shape
     columns = [along_rows(row) for row in index_rows(local_ref, 0, TILE)]
     total = None
-    for first in range(0, feat_ref.shape[0], TILE):
+    for first in range(0, nodes, TILE):
         part = dot(hits_by_row(columns, first, TILE), feat_ref[first : first + TILE, :])
         total = part if total is None else total + part
     sum_ref[...] = total
+    pack_ref[:, :width] = own_ref[...]
+    pack_ref[:, width : 2 * width] = cot_ref[...]
+    place = 2 * width
+    counts = pack_ref.shape[1] - place
+    for ref, share in ((remote_ref, split), (hub_ref, counts - split)):
+        columns = [along_rows(row) for row in index_rows(ref, 0, TILE)]
+        for first in range(0, share, TILE):
+            pack_ref[:, place + first : place + first + TILE] = hits_by_row(columns, first, TILE)
+        place += share
 
 
 def middle_kernel(
     scale,
+    slots,
     remote_ref,
     hub_ref,
-    feat_hbm,
-    sum_hbm,
-    cot_hbm,
-    table_hbm,
+    table_ref,
     ws_ref,
     wn_ref,
     bias_ref,
+    sum_hbm,
+    pack_hbm,
     act_hbm,
     grad_hbm,
-    pay_ref,
-    feat,
+    pay_hbm,
     sums,
-    cot,
-    bound_part,
-    hub_part,
+    pack,
     by_col,
     act,
     grad_all,
     mean_all,
-    sum_sem,
-    half_sem,
-    table_sem,
+    bound_pay,
+    hub_pay,
+    weight_pay,
+    block_sem,
     out_sem,
+    pay_sem,
 ):
-    nodes, width = feat.shape
-    parts, slots, _ = bound_part.shape
-    hub_rows = hub_part.shape[1]
-    slab = slots + hub_rows
+    nodes, width = sums.shape
+    parts, slab, _ = table_ref.shape
+    hub_rows = slab - slots
     bounds, hubs = parts * slots, parts * hub_rows
-    blocks = nodes // TILE
-    halves = 2
+    size = 2 * TILE
+    blocks = nodes // size
 
     def here(block):
-        return slice(block * TILE, (block + 1) * TILE)
-
-    table_loads = [
-        pltpu.make_async_copy(table_hbm.at[:, :slots, :], bound_part, table_sem.at[0]),
-        pltpu.make_async_copy(table_hbm.at[:, slots:, :], hub_part, table_sem.at[1]),
-    ]
-    for copy in table_loads:
-        copy.start()
+        return slice(block * size, (block + 1) * size)
 
     def loads(block):
         at = here(block)
-        copies = [pltpu.make_async_copy(sum_hbm.at[at, :], sums.at[at, :], sum_sem.at[block])]
-        if block % (blocks // halves) == 0:
-            half = block // (blocks // halves)
-            at = slice(half * (nodes // halves), (half + 1) * (nodes // halves))
-            copies.append(pltpu.make_async_copy(feat_hbm.at[at, :], feat.at[at, :], half_sem.at[0, half]))
-            copies.append(pltpu.make_async_copy(cot_hbm.at[at, :], cot.at[at, :], half_sem.at[1, half]))
-        return copies
+        return [
+            pltpu.make_async_copy(source.at[at, :], target.at[at, :], block_sem.at[which, block])
+            for which, (source, target) in enumerate(((pack_hbm, pack), (sum_hbm, sums)))
+        ]
 
     coming = [loads(block) for block in range(blocks)]
     for group in coming:
@@ -162,21 +161,14 @@
             copy.start()
 
     def counts(block):
-        start = block * TILE
-        hits = jnp.concatenate(
-            [
-                hits_by_column(index_rows(remote_ref, start, TILE), 0, bounds),
-                hits_by_column(index_rows(hub_ref, start, TILE), 0, hubs),
-            ],
-            axis=0,
-        )
-        by_col[:, here(block)] = hits
-        return hits
-
-    hits = counts(0)
-    for copy in table_loads:
-        copy.wait()
-    table = jnp.concatenate([bound_part[...].reshape(bounds, width), hub_part[...].reshape(hubs, width)], axis=0)
+        start = block * size
+        by_col[:bounds, here(block)] = hits_by_column(index_rows(remote_ref, start, size), 0, bounds)
+        by_col[bounds:, here(block)] = hits_by_column(index_rows(hub_ref, start, size), 0, hubs)
+
+    counts(0)
+    table = jnp.concatenate(
+        [table_ref[:, :slots, :].reshape(bounds, width), table_ref[:, slots:, :].reshape(hubs, width)], axis=0
+    )
     stores = []
     bias_total = jnp.zeros((1, width), f32)
     total = None
@@ -185,18 +177,18 @@
         if block < blocks:
             for copy in coming[block]:
                 copy.wait()
-            following = sums[here(block), :] + dot(hits, table, TN)
-            if block + 1 < blocks:
-                hits = counts(block + 1)
+            following = sums[here(block), :] + dot(pack[here(block), 2 * width :], table)
+            if block > 0:
+                counts(block)
         if block > 0:
             at = here(block - 1)
             mean = (total * scale).astype(bf16)
             mean_all[at, :] = mean
-            pre = dot(feat[at, :], ws_ref[...]) + dot(mean, wn_ref[...]) + bias_ref[...]
+            pre = dot(pack[at, :width], ws_ref[...]) + dot(mean, wn_ref[...]) + bias_ref[...]
             sig = 0.5 * jnp.tanh(0.5 * pre) + 0.5
             active = pre * sig
             act[at, :] = active.astype(bf16)
-            grad = (cot[at, :].astype(f32) * (sig + active * (1.0 - sig))).astype(bf16)
+            grad = (pack[at, width : 2 * width].astype(f32) * (sig + active * (1.0 - sig))).astype(bf16)
             grad_all[at, :] = grad
             bias_total = bias_total + jnp.sum(grad.astype(f32), axis=0, keepdims=True)
             for which, (source, target) in enumerate(((act, act_hbm), (grad_all, grad_hbm))):
@@ -205,17 +197,24 @@
                 stores.append(store)
         total = following
     grad = grad_all[...]
+
+    def send(source, first, which):
+        store = pltpu.make_async_copy(source, pay_hbm.at[:, first : first + source.shape[1], :], pay_sem.at[which])
+        store.start()
+        stores.append(store)
+
+    bound_pay[...] = dot(by_col[:bounds, :], grad).astype(bf16).reshape(parts, slots, width)
+    send(bound_pay, 0, 0)
+    hub_pay[...] = dot(by_col[bounds:, :], grad).astype(bf16).reshape(parts, hub_rows, width)
+    send(hub_pay, slots, 1)
     holders = 2 * width // 16
     per = holders // 2
-    for which, source in enumerate((feat, mean_all)):
-        pay_ref[which * per : (which + 1) * per, slab : slab + 16, :] = (
-            dot(source[...], grad, TN).astype(bf16).reshape(per, 16, width)
-        )
+    weight_pay[:, 16:, :] = jnp.broadcast_to(high_low(bias_total).astype(bf16)[None], (parts, 8, width))
+    for which, source in enumerate((pack[:, :width], mean_all[...])):
+        weight_pay[which * per : (which + 1) * per, :16, :] = dot(source, grad, TN).astype(bf16).reshape(per, 16, width)
     if parts > holders:
-        pay_ref[holders:, slab : slab + 16, :] = jnp.zeros((parts - holders, 16, width), bf16)
-    pay_ref[:, slab + 16 :, :] = jnp.broadcast_to(high_low(bias_total).astype(bf16)[None], (parts, 8, width))
-    pay_ref[:, :slots, :] = dot(by_col[:bounds, :], grad).astype(bf16).reshape(parts, slots, width)
-    pay_ref[:, slots:slab, :] = dot(by_col[bounds:, :], grad).astype(bf16).reshape(parts, hub_rows, width)
+        weight_pay[holders:, :16, :] = jnp.zeros((parts - holders, 16, width), bf16)
+    send(weight_pay, slab, 2)
     for store in stores:
         store.wait()
 
@@ -323,44 +322,46 @@
     received = exchange(sending)
 
     block = TILE
-    local_sum = call(
-        local_kernel,
-        (local_t, features),
-        [pl.BlockSpec((local_t.shape[0], block), lambda i: (0, i)), whole_block((nodes, width))],
-        shape((nodes, width), f32),
-        pl.BlockSpec((block, width), lambda i: (i, 0)),
+    by_block = pl.BlockSpec((block, width), lambda i: (i, 0))
+    packed = 2 * width + table
+    local_sum, pack = call(
+        functools.partial(local_kernel, parts * slots),
+        (local_t, remote_t, hub_t, features, features, cotangent),
+        [pl.BlockSpec((edges.shape[0], block), lambda i: (0, i)) for edges in (local_t, remote_t, hub_t)]
+        + [whole_block((nodes, width)), by_block, by_block],
+        [shape((nodes, width), f32), shape((nodes, packed), bf16)],
+        [by_block, pl.BlockSpec((block, packed), lambda i: (i, 0))],
         "local_gather",
         limit=MOST_VMEM,
         grid=(nodes // block,),
         flops=8 * nodes * nodes * width,
-        moved=nodes * width * 6,
+        moved=nodes * packed * 2,
     )
 
     activated, grad_pre, terms = call(
-        functools.partial(middle_kernel, scale),
-        [remote_t, hub_t, features, local_sum, cotangent, received, w_self, w_neigh, bias],
-        [VMEM] * 2 + [HBM] * 4 + [VMEM] * 3,
+        functools.partial(middle_kernel, scale, slots),
+        [remote_t, hub_t, received, w_self, w_neigh, bias, local_sum, pack],
+        [VMEM] * 6 + [HBM] * 2,
         [shape((nodes, width), bf16)] * 2 + [shape((parts, pay, width), bf16)],
-        [HBM] * 2 + [whole_block((parts, pay, width))],
+        [HBM] * 3,
         "activate",
-        limit=MOST_VMEM,
+        limit=MUCH_VMEM,
         scratch=[
-            pltpu.VMEM((nodes, width), bf16),
             pltpu.VMEM((nodes, width), f32),
-            pltpu.VMEM((nodes, width), bf16),
-            pltpu.VMEM((parts, slots, width), bf16),
-            pltpu.VMEM((parts, hub_rows, width), bf16),
+            pltpu.VMEM((nodes, packed), bf16),
             pltpu.VMEM((table, nodes), bf16),
             pltpu.VMEM((nodes, width), bf16),
             pltpu.VMEM((nodes, width), bf16),
             pltpu.VMEM((nodes, width), bf16),
-            pltpu.SemaphoreType.DMA((nodes // TILE,)),
-            pltpu.SemaphoreType.DMA((2, 2)),
-            pltpu.SemaphoreType.DMA((2,)),
-            pltpu.SemaphoreType.DMA((2, nodes // TILE)),
+            pltpu.VMEM((parts, slots, width), bf16),
+            pltpu.VMEM((parts, hub_rows, width), bf16),
+            pltpu.VMEM((parts, 24, width), bf16),
+            pltpu.SemaphoreType.DMA((2, nodes // (2 * TILE))),
+            pltpu.SemaphoreType.DMA((2, nodes // (2 * TILE))),
+            pltpu.SemaphoreType.DMA((3,)),
         ],
         flops=4 * nodes * table * width,
-        moved=nodes * width * 8,
+        moved=nodes * packed * 2,
     )
     back = exchange(terms)
 

time: 81.2 us -> 79.9 us (0.984)
  waiting for transfers between devices: 11.5 us -> 8.51 us
  Pallas kernels: 29.2 us -> 30.9 us
    all_to_all x2, waiting for transfers between devices: 11.5 us -> 8.51 us  [exchange(): return lax.all_to_all(value, AXES, split_axis=0, concat_axis=0, tiled=True)]
    pallas_call x6, Pallas kernels: 29.2 us -> 30.9 us  [call(): pl.pallas_call(kernel, grid=grid, in_specs=in_specs, out_specs=out_specs,...]
  transfers between devices with their start and end apart: 2 -> 2, of which waited for: 2 -> 2; matrix products, arithmetic and copies ran while one was open for 0% -> 0% of each run, Pallas kernels for 19% -> 23%
where the time goes in v3:
time: 79.9 us; the launch traced here: 79.3 us
  Pallas kernels  30.9 us (39%)
  blocking collectives  27.6 us (35%)
  starting transfers between devices  9.88 us (12%)
  waiting for transfers between devices  8.51 us (11%)
  local copies, waits for them, and re-layouts  1.71 us (2%)
    pallas_call x6, Pallas kernels, call(): pl.pallas_call(kernel, grid=grid, in_specs=in_specs, out_specs=out_specs,...  30.9 us
    all_to_all x1, blocking collectives, exchange(): return lax.all_to_all(value, AXES, split_axis=0, concat_axis=0, tiled=True)  27.6 us
    all_to_all x2, starting transfers between devices, exchange(): return lax.all_to_all(value, AXES, split_axis=0, concat_axis=0, tiled=True)  9.88 us
    all_to_all x2, waiting for transfers between devices, exchange(): return lax.all_to_all(value, AXES, split_axis=0, concat_axis=0, tiled=True)  8.51 us
  transfers between devices with their start and end apart: 2, of which 2 were waited for; matrix products, arithmetic and copies ran while one was open for 0% of the time, Pallas kernels for 23%

profile of v3, /device:TPU:0, one launch (start us, length us, event | category | flops | bytes accessed | tf_op | source)
XLA Modules:
  0.0 79.3 jit_solution(6667693424832858152)
XLA Ops:
  0.6 2.8 %pick_rows.1 = bf16[32,32,256]{2,1,0:T(8,128)(2,1)} custom-call(s32[1,512]{1,0:T(1,128)} %send_ref.3, bf16[2048,256]{1,0:T(8,128)(2,1)} %own_ref, bf16[16,256]{1,0:T(8,128)(2,1)} %hub_ref.1), custom_call_target="tpu_custom_call" | custom-call | flops 536870912 | bytes 1048576 | tf_op jit(solution)/shard_map/pick_rows/pallas_call | solution.py:266
  3.4 7.3 %all-to-all-start = ((bf16[32,32,256]{2,1,0:T(8,128)(2,1)}), bf16[32,32,256]{2,1,0:T(8,128)(2,1)S(1)}, u32[]{:S(2)}, u32[]{:S(2)}) async-start(bf16[32,32,256]{2,1,0:T(8,128)(2,1)} %pick_rows.1), calls=%async_computation | async-start | bytes 1048576 | tf_op jit(solution)/shard_map/all_to_all | solution.py:308
  10.7 10.3 %local_gather.1 = (f32[2048,256]{1,0:T(8,128)}, bf16[2048,1536]{1,0:T(8,128)(2,1)}) custom-call(s32[4,2048]{1,0:T(4,128)} %bitcast.7, s32[4,2048]{1,0:T(4,128)} %bitcast.11, s32[2,2048]{1,0:T(2,128)} %bitcast.13, bf16[2048,256]{1,0:T(8,128)(2,1)} %own_ref, bf16[2048,256]{1,0:T(8,128)(2,1)} %own_ref, bf16[2048,256]{1,0:T(8,128)(2,1)} %cot_ref.1), custom_call_target="tpu_custom_call" | custom-call | flops 8589934592 | bytes 6291456 | tf_op jit(solution)/shard_map/local_gather/pallas_call | solution.py:266
  21.1 6.0 %all-to-all-done.table_ref = bf16[32,32,256]{2,1,0:T(8,128)(2,1)S(1)} async-done(((bf16[32,32,256]{2,1,0:T(8,128)(2,1)}), bf16[32,32,256]{2,1,0:T(8,128)(2,1)S(1)}, u32[]{:S(2)}, u32[]{:S(2)}) %all-to-all-start) | async-done | bytes 524320 | tf_op jit(solution)/shard_map/all_to_all | solution.py:308
  27.1 0.0 copy-start.5
  27.1 0.8 %copy-done.5 = bf16[32,32,256]{2,1,0:T(8,128)(2,1)} copy-done((bf16[32,32,256]{2,1,0:T(8,128)(2,1)}, bf16[32,32,256]{2,1,0:T(8,128)(2,1)S(1)}, u32[]{:S(2)}) %copy-start.5) | copy-done | bytes 524312
  27.9 0.0 copy-start
  27.9 8.9 %activate.1 = (bf16[2048,256]{1,0:T(8,128)(2,1)}, bf16[2048,256]{1,0:T(8,128)(2,1)}, bf16[32,56,256]{2,1,0:T(8,128)(2,1)}) custom-call(s32[4,2048]{1,0:T(4,128)} %bitcast.12, s32[2,2048]{1,0:T(2,128)} %bitcast.14, bf16[32,32,256]{2,1,0:T(8,128)(2,1)} %copy-done.5, bf16[256,256]{1,0:T(8,128)(2,1)} %ws_ref.3, bf16[256,256]{1,0:T(8,128)(2,1)} %wn_ref.5, ...), custom_call_target="tpu_custom_call" | custom-call | flops 2147483648 | bytes 6291456 | tf_op jit(solution)/shard_map/activate/pallas_call | solution.py:266
  36.8 0.0 copy-start.1
  36.8 0.0 copy-start.4
  36.8 27.6 %all_to_all.15.back_ref = bf16[32,56,256]{2,1,0:T(8,128)(2,1)S(1)} all-to-all(bf16[32,56,256]{2,1,0:T(8,128)(2,1)} %get-tuple-element.21), channel_id=1, replica_groups=mesh['row'=4,'col'=8] {'row','col'}, dimensions={0} | all-to-all | bytes 1835008 | tf_op jit(solution)/shard_map/all_to_all | solution.py:308
  64.4 0.0 copy-done
  64.4 0.8 %sums.1 = (bf16[32,16,256]{2,1,0:T(8,128)(2,1)}, f32[1,256]{1,0:T(1,128)}, f32[16,256]{1,0:T(8,128)}) custom-call(bf16[32,56,256]{2,1,0:T(8,128)(2,1)S(1)} %all_to_all.15.back_ref, bf16[256,256]{1,0:T(8,128)(2,1)S(1)} %copy-done), custom_call_target="tpu_custom_call" | custom-call | bytes 1179648 | tf_op jit(solution)/shard_map/sums/pallas_call | solution.py:266
  65.2 2.6 %all-to-all-start.2 = ((bf16[32,16,256]{2,1,0:T(8,128)(2,1)}), bf16[32,16,256]{2,1,0:T(8,128)(2,1)S(1)}, u32[]{:S(2)}, u32[]{:S(2)}) async-start(bf16[32,16,256]{2,1,0:T(8,128)(2,1)} %get-tuple-element.24), calls=%async_computation.2 | async-start | bytes 524288 | tf_op jit(solution)/shard_map/all_to_all | solution.py:308
  67.8 0.0 copy-done.1
  67.8 0.0 copy-done.4
  67.8 0.0 copy-start.2
  67.9 0.0 copy-start.3
  67.9 4.4 %local_scatter.1.scat_ref = f32[2048,256]{1,0:T(8,128)S(1)} custom-call(s32[4,2048]{1,0:T(4,128)S(1)} %bitcast.8, bf16[2048,256]{1,0:T(8,128)(2,1)S(1)} %copy-done.1), custom_call_target="tpu_custom_call" | custom-call | flops 8589934592 | bytes 3145728 | tf_op jit(solution)/shard_map/local_scatter/pallas_call | solution.py:266
  72.3 0.0 copy-done.2
  72.3 0.0 copy-done.3
  72.3 3.6 %return_scatter.1 = f32[2048,256]{1,0:T(8,128)} custom-call(s32[1,512]{1,0:T(1,128)S(1)} %copy-done.3, bf16[32,56,256]{2,1,0:T(8,128)(2,1)S(1)} %all_to_all.15.back_ref, f32[2048,256]{1,0:T(8,128)S(1)} %local_scatter.1.scat_ref, bf16[2048,256]{1,0:T(8,128)(2,1)S(1)} %copy-done.1, bf16[256,256]{1,0:T(8,128)(2,1)S(1)} %copy-done.2, bf16[256,256]{1,0:T(8,128)(2,1)S(1)} %copy-done), custom_call_target="tpu_custom_call" | custom-call | flops 536870912 | bytes 5242880 | tf_op jit(solution)/shard_map/return_scatter/pallas_call | solution.py:266
  76.0 2.5 %all-to-all-done.2 = bf16[32,16,256]{2,1,0:T(8,128)(2,1)S(1)} async-done(((bf16[32,16,256]{2,1,0:T(8,128)(2,1)}), bf16[32,16,256]{2,1,0:T(8,128)(2,1)S(1)}, u32[]{:S(2)}, u32[]{:S(2)}) %all-to-all-start.2) | async-done | bytes 262176 | tf_op jit(solution)/shard_map/all_to_all | solution.py:308
  78.5 0.8 %fusion = (f32[16,16,256]{2,1,0:T(8,128)}, f32[16,16,256]{2,1,0:T(8,128)}) fusion(bf16[32,16,256]{2,1,0:T(8,128)(2,1)S(1)} %all-to-all-done.2), kind=kLoop, calls=%fused_computation | loop fusion | bytes 1048576 | tf_op jit(solution)/shard_map/slice | solution.py:405
Async XLA Ops:
  3.4 23.7 %all-to-all-start = ((bf16[32,32,256]{2,1,0:T(8,128)(2,1)}), bf16[32,32,256]{2,1,0:T(8,128)(2,1)S(1)}, u32[]{:S(2)}, u32[]{:S(2)}) async-start(bf16[32,32,256]{2,1,0:T(8,128)(2,1)} %pick_rows.1), calls=%async_computation | async-start | bytes 1048576 | tf_op jit(solution)/shard_map/all_to_all | solution.py:308
  27.1 0.8 %copy-start.5 = (bf16[32,32,256]{2,1,0:T(8,128)(2,1)}, bf16[32,32,256]{2,1,0:T(8,128)(2,1)S(1)}, u32[]{:S(2)}) copy-start(bf16[32,32,256]{2,1,0:T(8,128)(2,1)S(1)} %all-to-all-done.table_ref) | copy-start | bytes 1572868
  27.9 36.5 %copy-start = (bf16[256,256]{1,0:T(8,128)(2,1)S(1)}, bf16[256,256]{1,0:T(8,128)(2,1)}, u32[]{:S(2)}) copy-start(bf16[256,256]{1,0:T(8,128)(2,1)} %wn_ref.5) | copy-start | bytes 393220
  36.8 31.0 %copy-start.1 = (bf16[2048,256]{1,0:T(8,128)(2,1)S(1)}, bf16[2048,256]{1,0:T(8,128)(2,1)}, u32[]{:S(2)}) copy-start(bf16[2048,256]{1,0:T(8,128)(2,1)} %get-tuple-element.22.grad_ref) | copy-start | bytes 3145732
  36.8 31.0 %copy-start.4 = (s32[2048,4]{0,1:T(4,128)S(1)}, s32[2048,4]{0,1:T(4,128)}, u32[]{:S(2)}) copy-start(s32[2048,4]{0,1:T(4,128)} %param.15) | copy-start | bytes 98308
  65.2 13.2 %all-to-all-start.2 = ((bf16[32,16,256]{2,1,0:T(8,128)(2,1)}), bf16[32,16,256]{2,1,0:T(8,128)(2,1)S(1)}, u32[]{:S(2)}, u32[]{:S(2)}) async-start(bf16[32,16,256]{2,1,0:T(8,128)(2,1)} %get-tuple-element.24), calls=%async_computation.2 | async-start | bytes 524288 | tf_op jit(solution)/shard_map/all_to_all | solution.py:308
  67.8 4.5 %copy-start.2 = (bf16[256,256]{1,0:T(8,128)(2,1)S(1)}, bf16[256,256]{1,0:T(8,128)(2,1)}, u32[]{:S(2)}) copy-start(bf16[256,256]{1,0:T(8,128)(2,1)} %ws_ref.3) | copy-start | bytes 393220
  67.9 4.5 %copy-start.3 = (s32[1,512]{1,0:T(1,128)S(1)}, s32[1,512]{1,0:T(1,128)}, u32[]{:S(2)}) copy-start(s32[1,512]{1,0:T(1,128)} %send_ref.3) | copy-start | bytes 6148

commit v4 on v3

--- a/solution.py
+++ b/solution.py
@@ -11,7 +11,6 @@
 LANES = 128
 TILE = 256
 MOST_VMEM = 61952 * 1024
-MUCH_VMEM = 60500 * 1024
 SOME_VMEM = 44 * 1024 * 1024
 NT = (((1,), (1,)), ((), ()))
 TN = (((0,), (0,)), ((), ()))
@@ -100,8 +99,8 @@
         part = dot(hits_by_row(columns, first, TILE), feat_ref[first : first + TILE, :])
         total = part if total is None else total + part
     sum_ref[...] = total
-    pack_ref[:, :width] = own_ref[...]
-    pack_ref[:, width : 2 * width] = cot_ref[...]
+    pack_ref[:, :width] = cot_ref[...]
+    pack_ref[:, width : 2 * width] = own_ref[...]
     place = 2 * width
     counts = pack_ref.shape[1] - place
     for ref, share in ((remote_ref, split), (hub_ref, counts - split)):
@@ -114,36 +113,29 @@
 def middle_kernel(
     scale,
     slots,
-    remote_ref,
-    hub_ref,
     table_ref,
     ws_ref,
     wn_ref,
     bias_ref,
-    sum_hbm,
+    sum_ref,
     pack_hbm,
     act_hbm,
     grad_hbm,
-    pay_hbm,
-    sums,
+    pay_ref,
     pack,
-    by_col,
     act,
     grad_all,
-    mean_all,
-    bound_pay,
-    hub_pay,
-    weight_pay,
-    block_sem,
+    grad_t,
+    in_sem,
     out_sem,
-    pay_sem,
 ):
-    nodes, width = sums.shape
+    nodes, width = sum_ref.shape
     parts, slab, _ = table_ref.shape
     hub_rows = slab - slots
     bounds, hubs = parts * slots, parts * hub_rows
     size = 2 * TILE
     blocks = nodes // size
+    features, counts = slice(width, 2 * width), 3 * width
 
     def here(block):
         return slice(block * size, (block + 1) * size)
@@ -151,70 +143,58 @@
     def loads(block):
         at = here(block)
         return [
-            pltpu.make_async_copy(source.at[at, :], target.at[at, :], block_sem.at[which, block])
-            for which, (source, target) in enumerate(((pack_hbm, pack), (sum_hbm, sums)))
+            pltpu.make_async_copy(pack_hbm.at[at, : 2 * width], pack.at[at, : 2 * width], in_sem.at[0, block]),
+            pltpu.make_async_copy(pack_hbm.at[at, 2 * width :], pack.at[at, counts:], in_sem.at[1, block]),
         ]
 
     coming = [loads(block) for block in range(blocks)]
     for group in coming:
         for copy in group:
             copy.start()
-
-    def counts(block):
-        start = block * size
-        by_col[:bounds, here(block)] = hits_by_column(index_rows(remote_ref, start, size), 0, bounds)
-        by_col[bounds:, here(block)] = hits_by_column(index_rows(hub_ref, start, size), 0, hubs)
-
-    counts(0)
     table = jnp.concatenate(
         [table_ref[:, :slots, :].reshape(bounds, width), table_ref[:, slots:, :].reshape(hubs, width)], axis=0
     )
+    half_weights = jnp.concatenate([ws_ref[...], wn_ref[...]], axis=0) * jnp.bfloat16(0.5)
+    half_bias = 0.5 * bias_ref[...]
     stores = []
-    bias_total = jnp.zeros((1, width), f32)
     total = None
     for block in range(blocks + 1):
         following = None
         if block < blocks:
             for copy in coming[block]:
                 copy.wait()
-            following = sums[here(block), :] + dot(pack[here(block), 2 * width :], table)
-            if block > 0:
-                counts(block)
+            following = sum_ref[here(block), :] + dot(pack[here(block), counts:], table)
         if block > 0:
             at = here(block - 1)
-            mean = (total * scale).astype(bf16)
-            mean_all[at, :] = mean
-            pre = dot(pack[at, :width], ws_ref[...]) + dot(mean, wn_ref[...]) + bias_ref[...]
-            sig = 0.5 * jnp.tanh(0.5 * pre) + 0.5
-            active = pre * sig
-            act[at, :] = active.astype(bf16)
-            grad = (pack[at, width : 2 * width].astype(f32) * (sig + active * (1.0 - sig))).astype(bf16)
+            pack[at, 2 * width : counts] = (total * scale).astype(bf16)
+            half = dot(pack[at, width:counts], half_weights) + half_bias
+            tanh = jnp.tanh(half)
+            above = 1.0 + tanh
+            act[at, :] = (half * above).astype(bf16)
+            slope = above * (0.5 + (0.5 * half) * (1.0 - tanh))
+            grad = (pack[at, :width].astype(f32) * slope).astype(bf16)
             grad_all[at, :] = grad
-            bias_total = bias_total + jnp.sum(grad.astype(f32), axis=0, keepdims=True)
+            grad_t[:, at] = jnp.transpose(grad)
             for which, (source, target) in enumerate(((act, act_hbm), (grad_all, grad_hbm))):
                 store = pltpu.make_async_copy(source.at[at, :], target.at[at, :], out_sem.at[which, block - 1])
                 store.start()
                 stores.append(store)
         total = following
-    grad = grad_all[...]
-
-    def send(source, first, which):
-        store = pltpu.make_async_copy(source, pay_hbm.at[:, first : first + source.shape[1], :], pay_sem.at[which])
-        store.start()
-        stores.append(store)
-
-    bound_pay[...] = dot(by_col[:bounds, :], grad).astype(bf16).reshape(parts, slots, width)
-    send(bound_pay, 0, 0)
-    hub_pay[...] = dot(by_col[bounds:, :], grad).astype(bf16).reshape(parts, hub_rows, width)
-    send(hub_pay, slots, 1)
+
+    def terms(first, count):
+        return jnp.transpose(dot(grad_t[...], pack[:, first : first + count])).astype(bf16).reshape(-1, 16, width)
+
     holders = 2 * width // 16
-    per = holders // 2
-    weight_pay[:, 16:, :] = jnp.broadcast_to(high_low(bias_total).astype(bf16)[None], (parts, 8, width))
-    for which, source in enumerate((pack[:, :width], mean_all[...])):
-        weight_pay[which * per : (which + 1) * per, :16, :] = dot(source, grad, TN).astype(bf16).reshape(per, 16, width)
+    pay_ref[:holders, slab : slab + 16, :] = terms(width, 2 * width)
     if parts > holders:
-        weight_pay[holders:, :16, :] = jnp.zeros((parts - holders, 16, width), bf16)
-    send(weight_pay, slab, 2)
+        pay_ref[holders:, slab : slab + 16, :] = jnp.zeros((parts - holders, 16, width), bf16)
+    bias_total = dot(jnp.ones((16, nodes), bf16), grad_all[...])[:1]
+    pay_ref[:, slab + 16 :, :] = jnp.broadcast_to(high_low(bias_total).astype(bf16)[None], (parts, 8, width))
+    step = 2 * width
+    for low, total_rows, place, rows in ((0, bounds, 0, slots), (bounds, hubs, slots, hub_rows)):
+        for first in range(0, total_rows, step):
+            part = terms(counts + low + first, step).reshape(step // rows, rows, width)
+            pay_ref[first // rows : (first + step) // rows, place : place + rows, :] = part
     for store in stores:
         store.wait()
 
@@ -329,10 +309,9 @@
         (local_t, remote_t, hub_t, features, features, cotangent),
         [pl.BlockSpec((edges.shape[0], block), lambda i: (0, i)) for edges in (local_t, remote_t, hub_t)]
         + [whole_block((nodes, width)), by_block, by_block],
-        [shape((nodes, width), f32), shape((nodes, packed), bf16)],
+        [shape((nodes, width), f32), pltpu.HBM((nodes, packed), bf16)],
         [by_block, pl.BlockSpec((block, packed), lambda i: (i, 0))],
         "local_gather",
-        limit=MOST_VMEM,
         grid=(nodes // block,),
         flops=8 * nodes * nodes * width,
         moved=nodes * packed * 2,
@@ -340,25 +319,18 @@
 
     activated, grad_pre, terms = call(
         functools.partial(middle_kernel, scale, slots),
-        [remote_t, hub_t, received, w_self, w_neigh, bias, local_sum, pack],
-        [VMEM] * 6 + [HBM] * 2,
+        [received, w_self, w_neigh, bias, local_sum, pack],
+        [VMEM] * 5 + [HBM],
         [shape((nodes, width), bf16)] * 2 + [shape((parts, pay, width), bf16)],
-        [HBM] * 3,
+        [HBM] * 2 + [VMEM],
         "activate",
-        limit=MUCH_VMEM,
         scratch=[
-            pltpu.VMEM((nodes, width), f32),
-            pltpu.VMEM((nodes, packed), bf16),
-            pltpu.VMEM((table, nodes), bf16),
+            pltpu.VMEM((nodes, packed + width), bf16),
             pltpu.VMEM((nodes, width), bf16),
             pltpu.VMEM((nodes, width), bf16),
-            pltpu.VMEM((nodes, width), bf16),
-            pltpu.VMEM((parts, slots, width), bf16),
-            pltpu.VMEM((parts, hub_rows, width), bf16),
-            pltpu.VMEM((parts, 24, width), bf16),
+            pltpu.VMEM((width, nodes), bf16),
             pltpu.SemaphoreType.DMA((2, nodes // (2 * TILE))),
             pltpu.SemaphoreType.DMA((2, nodes // (2 * TILE))),
-            pltpu.SemaphoreType.DMA((3,)),
         ],
         flops=4 * nodes * table * width,
         moved=nodes * packed * 2,

time: 79.9 us -> 77.3 us (0.967)
  Pallas kernels: 30.9 us -> 25.9 us
  local copies, waits for them, and re-layouts: 1.71 us -> 4.29 us
  blocking collectives: 27.6 us -> 26.8 us
    pallas_call x6, Pallas kernels: 30.9 us -> 25.9 us  [call(): pl.pallas_call(kernel, grid=grid, in_specs=in_specs, out_specs=out_specs,...]
    unnamed x12 -> x22, local copies, waits for them, and re-layouts: 0.86 us -> 3.44 us
  transfers between devices with their start and end apart: 2 -> 2, of which waited for: 2 -> 2; matrix products, arithmetic and copies ran while one was open for 0% -> 0% of each run, Pallas kernels for 23% -> 20%
where the time goes in v4:
time: 77.3 us; the launch traced here: 77 us
  blocking collectives  26.8 us (35%)
  Pallas kernels  25.9 us (34%)
  starting transfers between devices  9.88 us (13%)
  waiting for transfers between devices  9.26 us (12%)
  local copies, waits for them, and re-layouts  4.29 us (6%)
    all_to_all x1, blocking collectives, exchange(): return lax.all_to_all(value, AXES, split_axis=0, concat_axis=0, tiled=True)  26.8 us
    pallas_call x6, Pallas kernels, call(): pl.pallas_call(kernel, grid=grid, in_specs=in_specs, out_specs=out_specs,...  25.9 us
    all_to_all x2, starting transfers between devices, exchange(): return lax.all_to_all(value, AXES, split_axis=0, concat_axis=0, tiled=True)  9.88 us
    all_to_all x2, waiting for transfers between devices, exchange(): return lax.all_to_all(value, AXES, split_axis=0, concat_axis=0, tiled=True)  9.26 us
    unnamed x22, local copies, waits for them, and re-layouts  3.44 us
  transfers between devices with their start and end apart: 2, of which 2 were waited for; matrix products, arithmetic and copies ran while one was open for 0% of the time, Pallas kernels for 20%

profile of v4, /device:TPU:0, one launch (start us, length us, event | category | flops | bytes accessed | tf_op | source)
XLA Modules:
  0.0 77.0 jit_solution(17226526890170672949)
XLA Ops:
  0.6 0.0 copy-start.8
  0.6 0.0 copy-start.10
  0.7 0.0 copy-start.9
  0.7 2.8 %pick_rows.1 = bf16[32,32,256]{2,1,0:T(8,128)(2,1)} custom-call(s32[1,512]{1,0:T(1,128)} %send_ref.3, bf16[2048,256]{1,0:T(8,128)(2,1)} %own_ref, bf16[16,256]{1,0:T(8,128)(2,1)} %hub_ref.1), custom_call_target="tpu_custom_call" | custom-call | flops 536870912 | bytes 1048576 | tf_op jit(solution)/shard_map/pick_rows/pallas_call | solution.py:246
  3.5 7.3 %all-to-all-start = ((bf16[32,32,256]{2,1,0:T(8,128)(2,1)}), bf16[32,32,256]{2,1,0:T(8,128)(2,1)S(1)}, u32[]{:S(2)}, u32[]{:S(2)}) async-start(bf16[32,32,256]{2,1,0:T(8,128)(2,1)} %pick_rows.1), calls=%async_computation | async-start | bytes 1048576 | tf_op jit(solution)/shard_map/all_to_all | solution.py:288
  10.8 0.0 copy-done.8
  10.8 0.0 copy-done.10
  10.8 0.0 copy-done.9
  10.8 0.0 copy-start.6
  10.8 1.2 %copy-done.6 = bf16[2048,256]{1,0:T(8,128)(2,1)S(1)} copy-done((bf16[2048,256]{1,0:T(8,128)(2,1)S(1)}, bf16[2048,256]{1,0:T(8,128)(2,1)}, u32[]{:S(2)}) %copy-start.6) | copy-done | bytes 1048600
  12.0 0.0 copy-start.7
  12.0 1.2 %copy-done.7 = bf16[2048,256]{1,0:T(8,128)(2,1)S(1)} copy-done((bf16[2048,256]{1,0:T(8,128)(2,1)S(1)}, bf16[2048,256]{1,0:T(8,128)(2,1)}, u32[]{:S(2)}) %copy-start.7) | copy-done | bytes 1048600
  13.2 0.0 copy-start
  13.2 0.0 copy-start.3
  13.2 7.1 %local_gather.1 = (f32[2048,256]{1,0:T(8,128)S(1)}, bf16[2048,1536]{1,0:T(8,128)(2,1)}) custom-call(s32[4,2048]{1,0:T(4,128)S(1)} %bitcast.9, s32[4,2048]{1,0:T(4,128)S(1)} %bitcast.8, s32[2,2048]{1,0:T(2,128)S(1)} %bitcast.11, bf16[2048,256]{1,0:T(8,128)(2,1)S(1)} %copy-done.6, bf16[2048,256]{1,0:T(8,128)(2,1)S(1)} %copy-done.6, bf16[2048,256]{1,0:T(8,128)(2,1)S(1)} %copy-done.7), custom_call_target="tpu_custom_call" | custom-call | flops 8589934592 | bytes 6291456 | tf_op jit(solution)/shard_map/local_gather/pallas_call | solution.py:246
  20.4 6.7 %all-to-all-done.table_ref = bf16[32,32,256]{2,1,0:T(8,128)(2,1)S(1)} async-done(((bf16[32,32,256]{2,1,0:T(8,128)(2,1)}), bf16[32,32,256]{2,1,0:T(8,128)(2,1)S(1)}, u32[]{:S(2)}, u32[]{:S(2)}) %all-to-all-start) | async-done | bytes 524320 | tf_op jit(solution)/shard_map/all_to_all | solution.py:288
  27.1 0.0 copy-done
  27.1 0.0 copy-done.3
  27.1 0.0 copy-done.5
  27.1 7.1 %activate.1 = (bf16[2048,256]{1,0:T(8,128)(2,1)}, bf16[2048,256]{1,0:T(8,128)(2,1)S(1)}, bf16[32,56,256]{2,1,0:T(8,128)(2,1)S(1)}) custom-call(bf16[32,32,256]{2,1,0:T(8,128)(2,1)S(1)} %all-to-all-done.table_ref, bf16[256,256]{1,0:T(8,128)(2,1)S(1)} %copy-done.3, bf16[256,256]{1,0:T(8,128)(2,1)S(1)} %copy-done, f32[1,256]{1,0:T(1,128)S(1)} %bitcast.7, ...), custom_call_target="tpu_custom_call" | custom-call | flops 2147483648 | bytes 6291456 | tf_op jit(solution)/shard_map/activate/pallas_call | solution.py:246
  34.2 0.0 copy-start.1
  34.2 1.0 %copy-done.1 = bf16[2048,256]{1,0:T(8,128)(2,1)} copy-done((bf16[2048,256]{1,0:T(8,128)(2,1)}, bf16[2048,256]{1,0:T(8,128)(2,1)S(1)}, u32[]{:S(2)}) %copy-start.1) | copy-done | bytes 1048600
  35.2 26.8 %all_to_all.15.back_ref = bf16[32,56,256]{2,1,0:T(8,128)(2,1)S(1)} all-to-all(bf16[32,56,256]{2,1,0:T(8,128)(2,1)S(1)} %get-tuple-element.21), channel_id=1, replica_groups=mesh['row'=4,'col'=8] {'row','col'}, dimensions={0} | all-to-all | bytes 1835008 | tf_op jit(solution)/shard_map/all_to_all | solution.py:288
  62.0 0.8 %sums.1 = (bf16[32,16,256]{2,1,0:T(8,128)(2,1)}, f32[1,256]{1,0:T(1,128)}, f32[16,256]{1,0:T(8,128)}) custom-call(bf16[32,56,256]{2,1,0:T(8,128)(2,1)S(1)} %all_to_all.15.back_ref, bf16[256,256]{1,0:T(8,128)(2,1)S(1)} %copy-done), custom_call_target="tpu_custom_call" | custom-call | bytes 1179648 | tf_op jit(solution)/shard_map/sums/pallas_call | solution.py:246
  62.9 2.6 %all-to-all-start.2 = ((bf16[32,16,256]{2,1,0:T(8,128)(2,1)}), bf16[32,16,256]{2,1,0:T(8,128)(2,1)S(1)}, u32[]{:S(2)}, u32[]{:S(2)}) async-start(bf16[32,16,256]{2,1,0:T(8,128)(2,1)} %get-tuple-element.24), calls=%async_computation.2 | async-start | bytes 524288 | tf_op jit(solution)/shard_map/all_to_all | solution.py:288
  65.5 0.0 copy-done.2
  65.5 0.0 copy-start.4
  65.5 4.4 %local_scatter.1.scat_ref = f32[2048,256]{1,0:T(8,128)S(1)} custom-call(s32[4,2048]{1,0:T(4,128)S(1)} %bitcast.10, bf16[2048,256]{1,0:T(8,128)(2,1)S(1)} %copy-done.2), custom_call_target="tpu_custom_call" | custom-call | flops 8589934592 | bytes 3145728 | tf_op jit(solution)/shard_map/local_scatter/pallas_call | solution.py:246
  69.9 0.0 copy-done.4
  69.9 3.6 %return_scatter.1 = f32[2048,256]{1,0:T(8,128)} custom-call(s32[1,512]{1,0:T(1,128)S(1)} %copy-done.4, bf16[32,56,256]{2,1,0:T(8,128)(2,1)S(1)} %all_to_all.15.back_ref, f32[2048,256]{1,0:T(8,128)S(1)} %local_scatter.1.scat_ref, bf16[2048,256]{1,0:T(8,128)(2,1)S(1)} %copy-done.2, bf16[256,256]{1,0:T(8,128)(2,1)S(1)} %copy-done.3, bf16[256,256]{1,0:T(8,128)(2,1)S(1)} %copy-done), custom_call_target="tpu_custom_call" | custom-call | flops 536870912 | bytes 5242880 | tf_op jit(solution)/shard_map/return_scatter/pallas_call | solution.py:246
  73.6 2.5 %all-to-all-done.2 = bf16[32,16,256]{2,1,0:T(8,128)(2,1)S(1)} async-done(((bf16[32,16,256]{2,1,0:T(8,128)(2,1)}), bf16[32,16,256]{2,1,0:T(8,128)(2,1)S(1)}, u32[]{:S(2)}, u32[]{:S(2)}) %all-to-all-start.2) | async-done | bytes 262176 | tf_op jit(solution)/shard_map/all_to_all | solution.py:288
  76.1 0.8 %fusion = (f32[16,16,256]{2,1,0:T(8,128)}, f32[16,16,256]{2,1,0:T(8,128)}) fusion(bf16[32,16,256]{2,1,0:T(8,128)(2,1)S(1)} %all-to-all-done.2), kind=kLoop, calls=%fused_computation | loop fusion | bytes 1048576 | tf_op jit(solution)/shard_map/slice | solution.py:377
  (2 shorter events, 0.0 us)
Async XLA Ops:
  0.6 10.1 %copy-start.8 = (s32[2048,4]{0,1:T(4,128)S(1)}, s32[2048,4]{0,1:T(4,128)}, u32[]{:S(2)}) copy-start(s32[2048,4]{0,1:T(4,128)} %param.17) | copy-start | bytes 98308
  0.6 10.1 %copy-start.10 = (s32[2048,2]{0,1:T(2,128)S(1)}, s32[2048,2]{0,1:T(2,128)}, u32[]{:S(2)}) copy-start(s32[2048,2]{0,1:T(2,128)} %param.16) | copy-start | bytes 49156
  0.7 10.1 %copy-start.9 = (s32[2048,4]{0,1:T(4,128)S(1)}, s32[2048,4]{0,1:T(4,128)}, u32[]{:S(2)}) copy-start(s32[2048,4]{0,1:T(4,128)} %param.15) | copy-start | bytes 98308
  3.5 23.7 %all-to-all-start = ((bf16[32,32,256]{2,1,0:T(8,128)(2,1)}), bf16[32,32,256]{2,1,0:T(8,128)(2,1)S(1)}, u32[]{:S(2)}, u32[]{:S(2)}) async-start(bf16[32,32,256]{2,1,0:T(8,128)(2,1)} %pick_rows.1), calls=%async_computation | async-start | bytes 1048576 | tf_op jit(solution)/shard_map/all_to_all | solution.py:288
  10.8 1.2 %copy-start.6 = (bf16[2048,256]{1,0:T(8,128)(2,1)S(1)}, bf16[2048,256]{1,0:T(8,128)(2,1)}, u32[]{:S(2)}) copy-start(bf16[2048,256]{1,0:T(8,128)(2,1)} %own_ref) | copy-start | bytes 3145732
  12.0 1.2 %copy-start.7 = (bf16[2048,256]{1,0:T(8,128)(2,1)S(1)}, bf16[2048,256]{1,0:T(8,128)(2,1)}, u32[]{:S(2)}) copy-start(bf16[2048,256]{1,0:T(8,128)(2,1)} %cot_ref.1) | copy-start | bytes 3145732
  13.2 13.9 %copy-start = (bf16[256,256]{1,0:T(8,128)(2,1)S(1)}, bf16[256,256]{1,0:T(8,128)(2,1)}, u32[]{:S(2)}) copy-start(bf16[256,256]{1,0:T(8,128)(2,1)} %wn_ref.5) | copy-start | bytes 393220
  13.2 13.9 %copy-start.3 = (bf16[256,256]{1,0:T(8,128)(2,1)S(1)}, bf16[256,256]{1,0:T(8,128)(2,1)}, u32[]{:S(2)}) copy-start(bf16[256,256]{1,0:T(8,128)(2,1)} %ws_ref.3) | copy-start | bytes 393220
  13.2 13.9 %copy-start.5 = (f32[256]{0:T(256)S(1)}, f32[256]{0:T(256)}, u32[]{:S(2)}) copy-start(f32[256]{0:T(256)} %param.14) | copy-start | bytes 3076
  34.2 1.0 %copy-start.1 = (bf16[2048,256]{1,0:T(8,128)(2,1)}, bf16[2048,256]{1,0:T(8,128)(2,1)S(1)}, u32[]{:S(2)}) copy-start(bf16[2048,256]{1,0:T(8,128)(2,1)S(1)} %get-tuple-element.22.grad_ref) | copy-start | bytes 3145732
  35.2 30.3 %copy-start.2 = (bf16[2048,256]{1,0:T(8,128)(2,1)S(1)}, bf16[2048,256]{1,0:T(8,128)(2,1)}, u32[]{:S(2)}) copy-start(bf16[2048,256]{1,0:T(8,128)(2,1)} %copy-done.1) | copy-start | bytes 3145732
  62.9 13.2 %all-to-all-start.2 = ((bf16[32,16,256]{2,1,0:T(8,128)(2,1)}), bf16[32,16,256]{2,1,0:T(8,128)(2,1)S(1)}, u32[]{:S(2)}, u32[]{:S(2)}) async-start(bf16[32,16,256]{2,1,0:T(8,128)(2,1)} %get-tuple-element.24), calls=%async_computation.2 | async-start | bytes 524288 | tf_op jit(solution)/shard_map/all_to_all | solution.py:288
  65.5 4.4 %copy-start.4 = (s32[1,512]{1,0:T(1,128)S(1)}, s32[1,512]{1,0:T(1,128)}, u32[]{:S(2)}) copy-start(s32[1,512]{1,0:T(1,128)} %send_ref.3) | copy-start | bytes 6148

commit v5 on v4

--- a/solution.py
+++ b/solution.py
@@ -125,7 +125,7 @@
     pack,
     act,
     grad_all,
-    grad_t,
+    terms,
     in_sem,
     out_sem,
 ):
@@ -158,13 +158,17 @@
     half_bias = 0.5 * bias_ref[...]
     stores = []
     total = None
-    for block in range(blocks + 1):
+    turned = None
+    for block in range(blocks + 2):
         following = None
         if block < blocks:
             for copy in coming[block]:
                 copy.wait()
             following = sum_ref[here(block), :] + dot(pack[here(block), counts:], table)
-        if block > 0:
+        if block > 1:
+            part = dot(turned, pack[here(block - 2), width:])
+            terms[...] = part if block == 2 else terms[...] + part
+        if 0 < block <= blocks:
             at = here(block - 1)
             pack[at, 2 * width : counts] = (total * scale).astype(bf16)
             half = dot(pack[at, width:counts], half_weights) + half_bias
@@ -174,42 +178,59 @@
             slope = above * (0.5 + (0.5 * half) * (1.0 - tanh))
             grad = (pack[at, :width].astype(f32) * slope).astype(bf16)
             grad_all[at, :] = grad
-            grad_t[:, at] = jnp.transpose(grad)
+            turned = jnp.transpose(grad)
             for which, (source, target) in enumerate(((act, act_hbm), (grad_all, grad_hbm))):
                 store = pltpu.make_async_copy(source.at[at, :], target.at[at, :], out_sem.at[which, block - 1])
                 store.start()
                 stores.append(store)
         total = following
 
-    def terms(first, count):
-        return jnp.transpose(dot(grad_t[...], pack[:, first : first + count])).astype(bf16).reshape(-1, 16, width)
+    pieces = width // LANES
+    tall = slab + 16
+
+    def put(low, high, place, rows, value):
+        value = value.astype(bf16).reshape(high - low, rows, width)
+        for piece in range(pieces):
+            at = piece * tall + place
+            pay_ref[low:high, at : at + rows, :] = value[:, :, piece * LANES : (piece + 1) * LANES]
+
+    def term_rows(first, count):
+        return jnp.transpose(terms[:, first : first + count])
 
     holders = 2 * width // 16
-    pay_ref[:holders, slab : slab + 16, :] = terms(width, 2 * width)
+    put(0, holders, slab, 16, term_rows(0, 2 * width))
     if parts > holders:
-        pay_ref[holders:, slab : slab + 16, :] = jnp.zeros((parts - holders, 16, width), bf16)
-    bias_total = dot(jnp.ones((16, nodes), bf16), grad_all[...])[:1]
-    pay_ref[:, slab + 16 :, :] = jnp.broadcast_to(high_low(bias_total).astype(bf16)[None], (parts, 8, width))
+        put(holders, parts, slab, 16, jnp.zeros(((parts - holders) * 16, width), f32))
     step = 2 * width
     for low, total_rows, place, rows in ((0, bounds, 0, slots), (bounds, hubs, slots, hub_rows)):
         for first in range(0, total_rows, step):
-            part = terms(counts + low + first, step).reshape(step // rows, rows, width)
-            pay_ref[first // rows : (first + step) // rows, place : place + rows, :] = part
+            put(first // rows, (first + step) // rows, place, rows, term_rows(2 * width + low + first, step))
+    bias_total = dot(jnp.ones((16, nodes), bf16), grad_all[...])[:1]
+    high = bias_total.astype(bf16).astype(f32)
+    line = lax.broadcasted_iota(jnp.int32, (8, LANES), 0)
+    rows = jnp.zeros((8, LANES), f32)
+    for piece in range(pieces):
+        lanes = slice(piece * LANES, (piece + 1) * LANES)
+        rows = jnp.where(line == piece, high[:, lanes], rows)
+        rows = jnp.where(line == pieces + piece, (bias_total - high)[:, lanes], rows)
+    pay_ref[:, pieces * tall :, :] = jnp.broadcast_to(rows.astype(bf16)[None], (parts, 8, LANES))
     for store in stores:
         store.wait()
 
 
-def high_low(row):
-    high = row.astype(bf16).astype(f32)
-    place = lax.broadcasted_iota(jnp.int32, (8, row.shape[1]), 0)
-    return jnp.where(place == 0, high, jnp.where(place == 1, row - high, 0.0))
-
-
 def sums_kernel(scale, slots, hub_rows, back_ref, wn_ref, weight_ref, bias_ref, hub_ref):
-    slab = slots + hub_rows
-    total = jnp.sum(back_ref[:, slots:, :].astype(f32), axis=0)
-    weight_ref[...] = jnp.broadcast_to(total[hub_rows : hub_rows + 16].astype(bf16)[None], weight_ref.shape)
-    bias_ref[...] = jnp.sum(total[hub_rows + 16 :], axis=0, keepdims=True)
+    tall = slots + hub_rows + 16
+    pieces = back_ref.shape[1] // tall
+    sums = [
+        jnp.sum(back_ref[:, piece * tall + slots : (piece + 1) * tall, :].astype(f32), axis=0)
+        for piece in range(pieces)
+    ]
+    total = jnp.concatenate(sums, axis=1)
+    weight_ref[...] = jnp.broadcast_to(total[hub_rows:].astype(bf16)[None], weight_ref.shape)
+    tail = jnp.sum(back_ref[:, pieces * tall :, :].astype(f32), axis=0)
+    bias_ref[...] = jnp.concatenate(
+        [tail[piece : piece + 1] + tail[pieces + piece : pieces + piece + 1] for piece in range(pieces)], axis=1
+    )
     hub = total[:hub_rows]
     high = hub.astype(bf16)
     low = (hub - high.astype(f32)).astype(bf16)
@@ -231,7 +252,11 @@
     height, width = out_ref.shape
     first = pl.program_id(0) * height
     count = send_ref.shape[1]
-    returned = back_ref[:, :slots, :].reshape(count, width)
+    pieces = width // LANES
+    tall = back_ref.shape[1] // pieces // 16 * 16
+    returned = jnp.concatenate(
+        [back_ref[:, piece * tall : piece * tall + slots, :].reshape(count, LANES) for piece in range(pieces)], axis=1
+    )
     total = scat_ref[...]
     for start in range(0, count, 512):
         stop = min(count, start + 512)
@@ -277,7 +302,8 @@
     parts = lax.axis_size(AXES)
     slots = send_rows.shape[1] // parts
     slab = slots + hub_rows
-    pay = slab + 24
+    pieces = width // LANES
+    pay = pieces * (slab + 16) + 8
     table = parts * slab
     scale = 1.0 / (local_edges.shape[1] + hub_edges.shape[1] + remote_edges.shape[1])
     local_t, hub_t, remote_t = local_edges.T, hub_edges.T, remote_edges.T
@@ -321,14 +347,14 @@
         functools.partial(middle_kernel, scale, slots),
         [received, w_self, w_neigh, bias, local_sum, pack],
         [VMEM] * 5 + [HBM],
-        [shape((nodes, width), bf16)] * 2 + [shape((parts, pay, width), bf16)],
+        [pltpu.HBM((nodes, width), bf16)] * 2 + [shape((parts, pay, LANES), bf16)],
         [HBM] * 2 + [VMEM],
         "activate",
         scratch=[
             pltpu.VMEM((nodes, packed + width), bf16),
             pltpu.VMEM((nodes, width), bf16),
             pltpu.VMEM((nodes, width), bf16),
-            pltpu.VMEM((width, nodes), bf16),
+            pltpu.VMEM((width, 2 * width + table), f32),
             pltpu.SemaphoreType.DMA((2, nodes // (2 * TILE))),
             pltpu.SemaphoreType.DMA((2, nodes // (2 * TILE))),
         ],
@@ -355,7 +381,7 @@
         [shape((parts, 16, width), bf16), shape((1, width), f32), shape((hub_rows, width), f32)],
         [whole_block((parts, 16, width)), whole_block((1, width)), whole_block((hub_rows, width))],
         "sums",
-        moved=parts * (pay + 16) * width * 2,
+        moved=parts * pay * width * 2,
     )
     weights = exchange(weight_rows)
 
@@ -364,7 +390,7 @@
     grad_features = call(
         functools.partial(final_kernel, scale, slots),
         (send_rows, back, scattered, grad_pre, w_self, w_neigh),
-        [whole_block(send_rows.shape), whole_block((parts, pay, width)), by_height, by_height]
+        [whole_block(send_rows.shape), whole_block((parts, pay, LANES)), by_height, by_height]
         + [whole_block((width, width))] * 2,
         shape((nodes, width), f32),
         by_height,

time: 77.3 us -> 76.4 us (0.988)
  local copies, waits for them, and re-layouts: 4.29 us -> 6.1 us
  Pallas kernels: 25.9 us -> 24.5 us
  blocking collectives: 26.8 us -> 25.5 us
    unnamed x22, local copies, waits for them, and re-layouts: 3.44 us -> 5.26 us
    pallas_call x6, Pallas kernels: 25.9 us -> 24.5 us  [call(): pl.pallas_call(kernel, grid=grid, in_specs=in_specs, out_specs=out_specs,...]
    all_to_all x1, blocking collectives: 26.8 us -> 25.5 us  [exchange(): return lax.all_to_all(value, AXES, split_axis=0, concat_axis=0, tiled=True)]
where the time goes in v5:
time: 76.4 us; the launch traced here: 76 us
  blocking collectives  25.5 us (33%)
  Pallas kernels  24.5 us (32%)
  starting transfers between devices  9.88 us (13%)
  waiting for transfers between devices  9.26 us (12%)
  local copies, waits for them, and re-layouts  6.1 us (8%)
  between operations  0.77 us (1%)
    all_to_all x1, blocking collectives, exchange(): return lax.all_to_all(value, AXES, split_axis=0, concat_axis=0, tiled=True)  25.5 us
    pallas_call x6, Pallas kernels, call(): pl.pallas_call(kernel, grid=grid, in_specs=in_specs, out_specs=out_specs,...  24.5 us
    all_to_all x2, starting transfers between devices, exchange(): return lax.all_to_all(value, AXES, split_axis=0, concat_axis=0, tiled=True)  9.88 us
    all_to_all x2, waiting for transfers between devices, exchange(): return lax.all_to_all(value, AXES, split_axis=0, concat_axis=0, tiled=True)  9.26 us
    unnamed x22, local copies, waits for them, and re-layouts  5.26 us
  transfers between devices with their start and end apart: 2, of which 2 were waited for; matrix products, arithmetic and copies ran while one was open for 0% of the time, Pallas kernels for 20%

profile of v5, /device:TPU:0, one launch (start us, length us, event | category | flops | bytes accessed | tf_op | source)
XLA Modules:
  0.0 76.0 jit_solution(7471105796875014657)
XLA Ops:
  0.6 0.0 copy-start.8
  0.6 0.0 copy-start.10
  0.7 0.0 copy-start.9
  0.7 2.8 %pick_rows.1 = bf16[32,32,256]{2,1,0:T(8,128)(2,1)} custom-call(s32[1,512]{1,0:T(1,128)} %send_ref.3, bf16[2048,256]{1,0:T(8,128)(2,1)} %own_ref, bf16[16,256]{1,0:T(8,128)(2,1)} %hub_ref.1), custom_call_target="tpu_custom_call" | custom-call | flops 536870912 | bytes 1048576 | tf_op jit(solution)/shard_map/pick_rows/pallas_call | solution.py:271
  3.5 7.3 %all-to-all-start = ((bf16[32,32,256]{2,1,0:T(8,128)(2,1)}), bf16[32,32,256]{2,1,0:T(8,128)(2,1)S(1)}, u32[]{:S(2)}, u32[]{:S(2)}) async-start(bf16[32,32,256]{2,1,0:T(8,128)(2,1)} %pick_rows.1), calls=%async_computation | async-start | bytes 1048576 | tf_op jit(solution)/shard_map/all_to_all | solution.py:314
  10.8 0.0 copy-done.8
  10.8 0.0 copy-done.10
  10.8 0.0 copy-done.9
  10.8 0.0 copy-start.6
  10.8 1.2 %copy-done.6 = bf16[2048,256]{1,0:T(8,128)(2,1)S(1)} copy-done((bf16[2048,256]{1,0:T(8,128)(2,1)S(1)}, bf16[2048,256]{1,0:T(8,128)(2,1)}, u32[]{:S(2)}) %copy-start.6) | copy-done | bytes 1048600
  12.0 0.0 copy-start.7
  12.0 1.2 %copy-done.7 = bf16[2048,256]{1,0:T(8,128)(2,1)S(1)} copy-done((bf16[2048,256]{1,0:T(8,128)(2,1)S(1)}, bf16[2048,256]{1,0:T(8,128)(2,1)}, u32[]{:S(2)}) %copy-start.7) | copy-done | bytes 1048600
  13.2 0.0 copy-start.1
  13.2 7.1 %local_gather.1 = (f32[2048,256]{1,0:T(8,128)S(1)}, bf16[2048,1536]{1,0:T(8,128)(2,1)}) custom-call(s32[4,2048]{1,0:T(4,128)S(1)} %bitcast.9, s32[4,2048]{1,0:T(4,128)S(1)} %bitcast.8, s32[2,2048]{1,0:T(2,128)S(1)} %bitcast.11, bf16[2048,256]{1,0:T(8,128)(2,1)S(1)} %copy-done.6, bf16[2048,256]{1,0:T(8,128)(2,1)S(1)} %copy-done.6, bf16[2048,256]{1,0:T(8,128)(2,1)S(1)} %copy-done.7), custom_call_target="tpu_custom_call" | custom-call | flops 8589934592 | bytes 6291456 | tf_op jit(solution)/shard_map/local_gather/pallas_call | solution.py:271
  20.4 6.7 %all-to-all-done.table_ref = bf16[32,32,256]{2,1,0:T(8,128)(2,1)S(1)} async-done(((bf16[32,32,256]{2,1,0:T(8,128)(2,1)}), bf16[32,32,256]{2,1,0:T(8,128)(2,1)S(1)}, u32[]{:S(2)}, u32[]{:S(2)}) %all-to-all-start) | async-done | bytes 524320 | tf_op jit(solution)/shard_map/all_to_all | solution.py:314
  27.1 0.0 copy-done.1
  27.1 0.0 copy-done.3
  27.1 0.0 copy-done.5
  27.1 0.0 copy-start
  27.1 2.8 %copy-done = bf16[2048,1536]{1,0:T(8,128)(2,1)S(1)} copy-done((bf16[2048,1536]{1,0:T(8,128)(2,1)S(1)}, bf16[2048,1536]{1,0:T(8,128)(2,1)}, u32[]{:S(2)}) %copy-start) | copy-done | bytes 6291480
  29.9 5.7 %activate.1 = (bf16[2048,256]{1,0:T(8,128)(2,1)}, bf16[2048,256]{1,0:T(8,128)(2,1)}, bf16[32,104,128]{2,1,0:T(8,128)(2,1)S(1)}) custom-call(bf16[32,32,256]{2,1,0:T(8,128)(2,1)S(1)} %all-to-all-done.table_ref, bf16[256,256]{1,0:T(8,128)(2,1)S(1)} %copy-done.3, bf16[256,256]{1,0:T(8,128)(2,1)S(1)} %copy-done.1, f32[1,256]{1,0:T(1,128)S(1)} %bitcast.7, ...), custom_call_target="tpu_custom_call" | custom-call | flops 2147483648 | bytes 6291456 | tf_op jit(solution)/shard_map/activate/pallas_call | solution.py:271
  35.6 0.0 copy-start.2
  35.6 25.5 %all_to_all.15.back_ref = bf16[32,104,128]{2,1,0:T(8,128)(2,1)S(1)} all-to-all(bf16[32,104,128]{2,1,0:T(8,128)(2,1)S(1)} %get-tuple-element.21), channel_id=1, replica_groups=mesh['row'=4,'col'=8] {'row','col'}, dimensions={0} | all-to-all | bytes 1703936 | tf_op jit(solution)/shard_map/all_to_all | solution.py:314
  61.1 0.8 %sums.1 = (bf16[32,16,256]{2,1,0:T(8,128)(2,1)}, f32[1,256]{1,0:T(1,128)}, f32[16,256]{1,0:T(8,128)}) custom-call(bf16[32,104,128]{2,1,0:T(8,128)(2,1)S(1)} %all_to_all.15.back_ref, bf16[256,256]{1,0:T(8,128)(2,1)S(1)} %copy-done.1), custom_call_target="tpu_custom_call" | custom-call | bytes 1703936 | tf_op jit(solution)/shard_map/sums/pallas_call | solution.py:271
  61.9 2.6 %all-to-all-start.2 = ((bf16[32,16,256]{2,1,0:T(8,128)(2,1)}), bf16[32,16,256]{2,1,0:T(8,128)(2,1)S(1)}, u32[]{:S(2)}, u32[]{:S(2)}) async-start(bf16[32,16,256]{2,1,0:T(8,128)(2,1)} %get-tuple-element.24), calls=%async_computation.2 | async-start | bytes 524288 | tf_op jit(solution)/shard_map/all_to_all | solution.py:314
  64.5 0.0 copy-done.2
  64.5 0.0 copy-start.4
  64.5 4.4 %local_scatter.1.scat_ref = f32[2048,256]{1,0:T(8,128)S(1)} custom-call(s32[4,2048]{1,0:T(4,128)S(1)} %bitcast.10, bf16[2048,256]{1,0:T(8,128)(2,1)S(1)} %copy-done.2), custom_call_target="tpu_custom_call" | custom-call | flops 8589934592 | bytes 3145728 | tf_op jit(solution)/shard_map/local_scatter/pallas_call | solution.py:271
  68.9 0.0 copy-done.4
  68.9 3.6 %return_scatter.1 = f32[2048,256]{1,0:T(8,128)} custom-call(s32[1,512]{1,0:T(1,128)S(1)} %copy-done.4, bf16[32,104,128]{2,1,0:T(8,128)(2,1)S(1)} %all_to_all.15.back_ref, f32[2048,256]{1,0:T(8,128)S(1)} %local_scatter.1.scat_ref, bf16[2048,256]{1,0:T(8,128)(2,1)S(1)} %copy-done.2, bf16[256,256]{1,0:T(8,128)(2,1)S(1)} %copy-done.3, bf16[256,256]{1,0:T(8,128)(2,1)S(1)} %copy-done.1), custom_call_target="tpu_custom_call" | custom-call | flops 536870912 | bytes 5242880 | tf_op jit(solution)/shard_map/return_scatter/pallas_call | solution.py:271
  72.6 2.5 %all-to-all-done.2 = bf16[32,16,256]{2,1,0:T(8,128)(2,1)S(1)} async-done(((bf16[32,16,256]{2,1,0:T(8,128)(2,1)}), bf16[32,16,256]{2,1,0:T(8,128)(2,1)S(1)}, u32[]{:S(2)}, u32[]{:S(2)}) %all-to-all-start.2) | async-done | bytes 262176 | tf_op jit(solution)/shard_map/all_to_all | solution.py:314
  75.1 0.8 %fusion = (f32[16,16,256]{2,1,0:T(8,128)}, f32[16,16,256]{2,1,0:T(8,128)}) fusion(bf16[32,16,256]{2,1,0:T(8,128)(2,1)S(1)} %all-to-all-done.2), kind=kLoop, calls=%fused_computation | loop fusion | bytes 1048576 | tf_op jit(solution)/shard_map/slice | solution.py:403
  (2 shorter events, 0.0 us)
Async XLA Ops:
  0.6 10.1 %copy-start.8 = (s32[2048,4]{0,1:T(4,128)S(1)}, s32[2048,4]{0,1:T(4,128)}, u32[]{:S(2)}) copy-start(s32[2048,4]{0,1:T(4,128)} %param.17) | copy-start | bytes 98308
  0.6 10.1 %copy-start.10 = (s32[2048,2]{0,1:T(2,128)S(1)}, s32[2048,2]{0,1:T(2,128)}, u32[]{:S(2)}) copy-start(s32[2048,2]{0,1:T(2,128)} %param.16) | copy-start | bytes 49156
  0.7 10.1 %copy-start.9 = (s32[2048,4]{0,1:T(4,128)S(1)}, s32[2048,4]{0,1:T(4,128)}, u32[]{:S(2)}) copy-start(s32[2048,4]{0,1:T(4,128)} %param.15) | copy-start | bytes 98308
  3.5 23.7 %all-to-all-start = ((bf16[32,32,256]{2,1,0:T(8,128)(2,1)}), bf16[32,32,256]{2,1,0:T(8,128)(2,1)S(1)}, u32[]{:S(2)}, u32[]{:S(2)}) async-start(bf16[32,32,256]{2,1,0:T(8,128)(2,1)} %pick_rows.1), calls=%async_computation | async-start | bytes 1048576 | tf_op jit(solution)/shard_map/all_to_all | solution.py:314
  10.8 1.2 %copy-start.6 = (bf16[2048,256]{1,0:T(8,128)(2,1)S(1)}, bf16[2048,256]{1,0:T(8,128)(2,1)}, u32[]{:S(2)}) copy-start(bf16[2048,256]{1,0:T(8,128)(2,1)} %own_ref) | copy-start | bytes 3145732
  12.0 1.2 %copy-start.7 = (bf16[2048,256]{1,0:T(8,128)(2,1)S(1)}, bf16[2048,256]{1,0:T(8,128)(2,1)}, u32[]{:S(2)}) copy-start(bf16[2048,256]{1,0:T(8,128)(2,1)} %cot_ref.1) | copy-start | bytes 3145732
  13.2 13.9 %copy-start.1 = (bf16[256,256]{1,0:T(8,128)(2,1)S(1)}, bf16[256,256]{1,0:T(8,128)(2,1)}, u32[]{:S(2)}) copy-start(bf16[256,256]{1,0:T(8,128)(2,1)} %wn_ref.5) | copy-start | bytes 393220
  13.2 13.9 %copy-start.3 = (bf16[256,256]{1,0:T(8,128)(2,1)S(1)}, bf16[256,256]{1,0:T(8,128)(2,1)}, u32[]{:S(2)}) copy-start(bf16[256,256]{1,0:T(8,128)(2,1)} %ws_ref.3) | copy-start | bytes 393220
  13.2 13.9 %copy-start.5 = (f32[256]{0:T(256)S(1)}, f32[256]{0:T(256)}, u32[]{:S(2)}) copy-start(f32[256]{0:T(256)} %param.14) | copy-start | bytes 3076
  27.1 2.8 %copy-start = (bf16[2048,1536]{1,0:T(8,128)(2,1)S(1)}, bf16[2048,1536]{1,0:T(8,128)(2,1)}, u32[]{:S(2)}) copy-start(bf16[2048,1536]{1,0:T(8,128)(2,1)} %get-tuple-element.19.pack_hbm) | copy-start | bytes 18874372
  35.6 28.9 %copy-start.2 = (bf16[2048,256]{1,0:T(8,128)(2,1)S(1)}, bf16[2048,256]{1,0:T(8,128)(2,1)}, u32[]{:S(2)}) copy-start(bf16[2048,256]{1,0:T(8,128)(2,1)} %get-tuple-element.22.grad_ref) | copy-start | bytes 3145732
  61.9 13.2 %all-to-all-start.2 = ((bf16[32,16,256]{2,1,0:T(8,128)(2,1)}), bf16[32,16,256]{2,1,0:T(8,128)(2,1)S(1)}, u32[]{:S(2)}, u32[]{:S(2)}) async-start(bf16[32,16,256]{2,1,0:T(8,128)(2,1)} %get-tuple-element.24), calls=%async_computation.2 | async-start | bytes 524288 | tf_op jit(solution)/shard_map/all_to_all | solution.py:314
  64.5 4.4 %copy-start.4 = (s32[1,512]{1,0:T(1,128)S(1)}, s32[1,512]{1,0:T(1,128)}, u32[]{:S(2)}) copy-start(s32[1,512]{1,0:T(1,128)} %send_ref.3) | copy-start | bytes 6148

commit v6 on v5

--- a/solution.py
+++ b/solution.py
@@ -12,6 +12,7 @@
 TILE = 256
 MOST_VMEM = 61952 * 1024
 SOME_VMEM = 44 * 1024 * 1024
+MUCH_VMEM = 50 * 1024 * 1024
 NT = (((1,), (1,)), ((), ()))
 TN = (((0,), (0,)), ((), ()))
 VMEM = pl.BlockSpec(memory_space=pltpu.VMEM)
@@ -350,6 +351,7 @@
         [pltpu.HBM((nodes, width), bf16)] * 2 + [shape((parts, pay, LANES), bf16)],
         [HBM] * 2 + [VMEM],
         "activate",
+        limit=MUCH_VMEM,
         scratch=[
             pltpu.VMEM((nodes, packed + width), bf16),
             pltpu.VMEM((nodes, width), bf16),

time: 76.4 us -> 74.5 us (0.975)
  local copies, waits for them, and re-layouts: 6.1 us -> 3.33 us
  Pallas kernels: 24.5 us -> 25.4 us
    unnamed x22 -> x20, local copies, waits for them, and re-layouts: 5.26 us -> 2.48 us
    pallas_call x6, Pallas kernels: 24.5 us -> 25.4 us  [call(): pl.pallas_call(kernel, grid=grid, in_specs=in_specs, out_specs=out_specs,...]
  transfers between devices with their start and end apart: 2 -> 2, of which waited for: 2 -> 2; matrix products, arithmetic and copies ran while one was open for 0% -> 0% of each run, Pallas kernels for 20% -> 21%
where the time goes in v6:
time: 74.5 us; the launch traced here: 74.1 us
  blocking collectives  25.5 us (34%)
  Pallas kernels  25.4 us (34%)
  starting transfers between devices  9.88 us (13%)
  waiting for transfers between devices  9.25 us (12%)
  local copies, waits for them, and re-layouts  3.33 us (4%)
  between operations  0.76 us (1%)
    all_to_all x1, blocking collectives, exchange(): return lax.all_to_all(value, AXES, split_axis=0, concat_axis=0, tiled=True)  25.5 us
    pallas_call x6, Pallas kernels, call(): pl.pallas_call(kernel, grid=grid, in_specs=in_specs, out_specs=out_specs,...  25.4 us
    all_to_all x2, starting transfers between devices, exchange(): return lax.all_to_all(value, AXES, split_axis=0, concat_axis=0, tiled=True)  9.88 us
    all_to_all x2, waiting for transfers between devices, exchange(): return lax.all_to_all(value, AXES, split_axis=0, concat_axis=0, tiled=True)  9.25 us
    unnamed x20, local copies, waits for them, and re-layouts  2.48 us
  transfers between devices with their start and end apart: 2, of which 2 were waited for; matrix products, arithmetic and copies ran while one was open for 0% of the time, Pallas kernels for 21%

profile of v6, /device:TPU:0, one launch (start us, length us, event | category | flops | bytes accessed | tf_op | source)
XLA Modules:
  0.0 74.1 jit_solution(14896453154310452825)
XLA Ops:
  0.6 0.0 copy-start.7
  0.6 0.0 copy-start.9
  0.7 0.0 copy-start.8
  0.7 2.8 %pick_rows.1 = bf16[32,32,256]{2,1,0:T(8,128)(2,1)} custom-call(s32[1,512]{1,0:T(1,128)} %send_ref.3, bf16[2048,256]{1,0:T(8,128)(2,1)} %own_ref, bf16[16,256]{1,0:T(8,128)(2,1)} %hub_ref.1), custom_call_target="tpu_custom_call" | custom-call | flops 536870912 | bytes 1048576 | tf_op jit(solution)/shard_map/pick_rows/pallas_call | solution.py:272
  3.5 7.3 %all-to-all-start = ((bf16[32,32,256]{2,1,0:T(8,128)(2,1)}), bf16[32,32,256]{2,1,0:T(8,128)(2,1)S(1)}, u32[]{:S(2)}, u32[]{:S(2)}) async-start(bf16[32,32,256]{2,1,0:T(8,128)(2,1)} %pick_rows.1), calls=%async_computation | async-start | bytes 1048576 | tf_op jit(solution)/shard_map/all_to_all | solution.py:315
  10.8 0.0 copy-done.7
  10.8 0.0 copy-done.9
  10.8 0.0 copy-done.8
  10.8 0.0 copy-start.5
  10.8 1.2 %copy-done.5 = bf16[2048,256]{1,0:T(8,128)(2,1)S(1)} copy-done((bf16[2048,256]{1,0:T(8,128)(2,1)S(1)}, bf16[2048,256]{1,0:T(8,128)(2,1)}, u32[]{:S(2)}) %copy-start.5) | copy-done | bytes 1048600
  12.0 0.0 copy-start.6
  12.0 1.2 %copy-done.6 = bf16[2048,256]{1,0:T(8,128)(2,1)S(1)} copy-done((bf16[2048,256]{1,0:T(8,128)(2,1)S(1)}, bf16[2048,256]{1,0:T(8,128)(2,1)}, u32[]{:S(2)}) %copy-start.6) | copy-done | bytes 1048600
  13.2 0.0 copy-start
  13.2 0.0 copy-start.2
  13.2 0.0 copy-start.4
  13.2 7.1 %local_gather.1 = (f32[2048,256]{1,0:T(8,128)S(1)}, bf16[2048,1536]{1,0:T(8,128)(2,1)}) custom-call(s32[4,2048]{1,0:T(4,128)S(1)} %bitcast.9, s32[4,2048]{1,0:T(4,128)S(1)} %bitcast.8, s32[2,2048]{1,0:T(2,128)S(1)} %bitcast.11, bf16[2048,256]{1,0:T(8,128)(2,1)S(1)} %copy-done.5, bf16[2048,256]{1,0:T(8,128)(2,1)S(1)} %copy-done.5, bf16[2048,256]{1,0:T(8,128)(2,1)S(1)} %copy-done.6), custom_call_target="tpu_custom_call" | custom-call | flops 8589934592 | bytes 6291456 | tf_op jit(solution)/shard_map/local_gather/pallas_call | solution.py:272
  20.4 6.7 %all-to-all-done.table_ref = bf16[32,32,256]{2,1,0:T(8,128)(2,1)S(1)} async-done(((bf16[32,32,256]{2,1,0:T(8,128)(2,1)}), bf16[32,32,256]{2,1,0:T(8,128)(2,1)S(1)}, u32[]{:S(2)}, u32[]{:S(2)}) %all-to-all-start) | async-done | bytes 524320 | tf_op jit(solution)/shard_map/all_to_all | solution.py:315
  27.1 0.0 copy-done
  27.1 0.0 copy-done.2
  27.1 0.0 copy-done.4
  27.1 6.6 %activate.1 = (bf16[2048,256]{1,0:T(8,128)(2,1)}, bf16[2048,256]{1,0:T(8,128)(2,1)}, bf16[32,104,128]{2,1,0:T(8,128)(2,1)S(1)}) custom-call(bf16[32,32,256]{2,1,0:T(8,128)(2,1)S(1)} %all-to-all-done.table_ref, bf16[256,256]{1,0:T(8,128)(2,1)S(1)} %copy-done.2, bf16[256,256]{1,0:T(8,128)(2,1)S(1)} %copy-done, f32[1,256]{1,0:T(1,128)S(1)} %bitcast.7, ...), custom_call_target="tpu_custom_call" | custom-call | flops 2147483648 | bytes 6291456 | tf_op jit(solution)/shard_map/activate/pallas_call | solution.py:272
  33.7 0.0 copy-start.1
  33.7 25.5 %all_to_all.15.back_ref = bf16[32,104,128]{2,1,0:T(8,128)(2,1)S(1)} all-to-all(bf16[32,104,128]{2,1,0:T(8,128)(2,1)S(1)} %get-tuple-element.21), channel_id=1, replica_groups=mesh['row'=4,'col'=8] {'row','col'}, dimensions={0} | all-to-all | bytes 1703936 | tf_op jit(solution)/shard_map/all_to_all | solution.py:315
  59.2 0.8 %sums.1 = (bf16[32,16,256]{2,1,0:T(8,128)(2,1)}, f32[1,256]{1,0:T(1,128)}, f32[16,256]{1,0:T(8,128)}) custom-call(bf16[32,104,128]{2,1,0:T(8,128)(2,1)S(1)} %all_to_all.15.back_ref, bf16[256,256]{1,0:T(8,128)(2,1)S(1)} %copy-done), custom_call_target="tpu_custom_call" | custom-call | bytes 1703936 | tf_op jit(solution)/shard_map/sums/pallas_call | solution.py:272
  60.0 2.6 %all-to-all-start.2 = ((bf16[32,16,256]{2,1,0:T(8,128)(2,1)}), bf16[32,16,256]{2,1,0:T(8,128)(2,1)S(1)}, u32[]{:S(2)}, u32[]{:S(2)}) async-start(bf16[32,16,256]{2,1,0:T(8,128)(2,1)} %get-tuple-element.24), calls=%async_computation.2 | async-start | bytes 524288 | tf_op jit(solution)/shard_map/all_to_all | solution.py:315
  62.6 0.0 copy-done.1
  62.6 0.0 copy-start.3
  62.6 4.4 %local_scatter.1.scat_ref = f32[2048,256]{1,0:T(8,128)S(1)} custom-call(s32[4,2048]{1,0:T(4,128)S(1)} %bitcast.10, bf16[2048,256]{1,0:T(8,128)(2,1)S(1)} %copy-done.1), custom_call_target="tpu_custom_call" | custom-call | flops 8589934592 | bytes 3145728 | tf_op jit(solution)/shard_map/local_scatter/pallas_call | solution.py:272
  67.1 0.0 copy-done.3
  67.1 3.6 %return_scatter.1 = f32[2048,256]{1,0:T(8,128)} custom-call(s32[1,512]{1,0:T(1,128)S(1)} %copy-done.3, bf16[32,104,128]{2,1,0:T(8,128)(2,1)S(1)} %all_to_all.15.back_ref, f32[2048,256]{1,0:T(8,128)S(1)} %local_scatter.1.scat_ref, bf16[2048,256]{1,0:T(8,128)(2,1)S(1)} %copy-done.1, bf16[256,256]{1,0:T(8,128)(2,1)S(1)} %copy-done.2, bf16[256,256]{1,0:T(8,128)(2,1)S(1)} %copy-done), custom_call_target="tpu_custom_call" | custom-call | flops 536870912 | bytes 5242880 | tf_op jit(solution)/shard_map/return_scatter/pallas_call | solution.py:272
  70.7 2.5 %all-to-all-done.2 = bf16[32,16,256]{2,1,0:T(8,128)(2,1)S(1)} async-done(((bf16[32,16,256]{2,1,0:T(8,128)(2,1)}), bf16[32,16,256]{2,1,0:T(8,128)(2,1)S(1)}, u32[]{:S(2)}, u32[]{:S(2)}) %all-to-all-start.2) | async-done | bytes 262176 | tf_op jit(solution)/shard_map/all_to_all | solution.py:315
  73.2 0.8 %fusion = (f32[16,16,256]{2,1,0:T(8,128)}, f32[16,16,256]{2,1,0:T(8,128)}) fusion(bf16[32,16,256]{2,1,0:T(8,128)(2,1)S(1)} %all-to-all-done.2), kind=kLoop, calls=%fused_computation | loop fusion | bytes 1048576 | tf_op jit(solution)/shard_map/slice | solution.py:405
Async XLA Ops:
  0.6 10.1 %copy-start.7 = (s32[2048,4]{0,1:T(4,128)S(1)}, s32[2048,4]{0,1:T(4,128)}, u32[]{:S(2)}) copy-start(s32[2048,4]{0,1:T(4,128)} %param.17) | copy-start | bytes 98308
  0.6 10.1 %copy-start.9 = (s32[2048,2]{0,1:T(2,128)S(1)}, s32[2048,2]{0,1:T(2,128)}, u32[]{:S(2)}) copy-start(s32[2048,2]{0,1:T(2,128)} %param.16) | copy-start | bytes 49156
  0.7 10.1 %copy-start.8 = (s32[2048,4]{0,1:T(4,128)S(1)}, s32[2048,4]{0,1:T(4,128)}, u32[]{:S(2)}) copy-start(s32[2048,4]{0,1:T(4,128)} %param.15) | copy-start | bytes 98308
  3.5 23.7 %all-to-all-start = ((bf16[32,32,256]{2,1,0:T(8,128)(2,1)}), bf16[32,32,256]{2,1,0:T(8,128)(2,1)S(1)}, u32[]{:S(2)}, u32[]{:S(2)}) async-start(bf16[32,32,256]{2,1,0:T(8,128)(2,1)} %pick_rows.1), calls=%async_computation | async-start | bytes 1048576 | tf_op jit(solution)/shard_map/all_to_all | solution.py:315
  10.8 1.2 %copy-start.5 = (bf16[2048,256]{1,0:T(8,128)(2,1)S(1)}, bf16[2048,256]{1,0:T(8,128)(2,1)}, u32[]{:S(2)}) copy-start(bf16[2048,256]{1,0:T(8,128)(2,1)} %own_ref) | copy-start | bytes 3145732
  12.0 1.2 %copy-start.6 = (bf16[2048,256]{1,0:T(8,128)(2,1)S(1)}, bf16[2048,256]{1,0:T(8,128)(2,1)}, u32[]{:S(2)}) copy-start(bf16[2048,256]{1,0:T(8,128)(2,1)} %cot_ref.1) | copy-start | bytes 3145732
  13.2 13.9 %copy-start = (bf16[256,256]{1,0:T(8,128)(2,1)S(1)}, bf16[256,256]{1,0:T(8,128)(2,1)}, u32[]{:S(2)}) copy-start(bf16[256,256]{1,0:T(8,128)(2,1)} %wn_ref.5) | copy-start | bytes 393220
  13.2 13.9 %copy-start.2 = (bf16[256,256]{1,0:T(8,128)(2,1)S(1)}, bf16[256,256]{1,0:T(8,128)(2,1)}, u32[]{:S(2)}) copy-start(bf16[256,256]{1,0:T(8,128)(2,1)} %ws_ref.3) | copy-start | bytes 393220
  13.2 13.9 %copy-start.4 = (f32[256]{0:T(256)S(1)}, f32[256]{0:T(256)}, u32[]{:S(2)}) copy-start(f32[256]{0:T(256)} %param.14) | copy-start | bytes 3076
  33.7 28.9 %copy-start.1 = (bf16[2048,256]{1,0:T(8,128)(2,1)S(1)}, bf16[2048,256]{1,0:T(8,128)(2,1)}, u32[]{:S(2)}) copy-start(bf16[2048,256]{1,0:T(8,128)(2,1)} %get-tuple-element.22.grad_ref) | copy-start | bytes 3145732
  60.0 13.2 %all-to-all-start.2 = ((bf16[32,16,256]{2,1,0:T(8,128)(2,1)}), bf16[32,16,256]{2,1,0:T(8,128)(2,1)S(1)}, u32[]{:S(2)}, u32[]{:S(2)}) async-start(bf16[32,16,256]{2,1,0:T(8,128)(2,1)} %get-tuple-element.24), calls=%async_computation.2 | async-start | bytes 524288 | tf_op jit(solution)/shard_map/all_to_all | solution.py:315
  62.6 4.4 %copy-start.3 = (s32[1,512]{1,0:T(1,128)S(1)}, s32[1,512]{1,0:T(1,128)}, u32[]{:S(2)}) copy-start(s32[1,512]{1,0:T(1,128)} %send_ref.3) | copy-start | bytes 6148

commit v7 on v6

--- a/solution.py
+++ b/solution.py
@@ -12,7 +12,7 @@
 TILE = 256
 MOST_VMEM = 61952 * 1024
 SOME_VMEM = 44 * 1024 * 1024
-MUCH_VMEM = 50 * 1024 * 1024
+MUCH_VMEM = 47 * 1024 * 1024
 NT = (((1,), (1,)), ((), ()))
 TN = (((0,), (0,)), ((), ()))
 VMEM = pl.BlockSpec(memory_space=pltpu.VMEM)
@@ -114,6 +114,7 @@
 def middle_kernel(
     scale,
     slots,
+    core_ref,
     table_ref,
     ws_ref,
     wn_ref,
@@ -122,7 +123,9 @@
     pack_hbm,
     act_hbm,
     grad_hbm,
-    pay_ref,
+    bound_ref,
+    keep_ref,
+    give_ref,
     pack,
     act,
     grad_all,
@@ -187,52 +190,89 @@
         total = following
 
     pieces = width // LANES
-    tall = slab + 16
-
-    def put(low, high, place, rows, value):
-        value = value.astype(bf16).reshape(high - low, rows, width)
+    step = 2 * width
+
+    def term_rows(first, rows):
+        return jnp.transpose(terms[:, first : first + step]).reshape(step // rows, rows, width)
+
+    def lanes(piece):
+        return slice(piece * LANES, (piece + 1) * LANES)
+
+    first_core = core_ref[0] == 0
+    half = hub_rows // 2
+    weights = term_rows(0, hub_rows)
+    for low in range(0, hubs, step):
+        hub_terms = term_rows(step + bounds + low, hub_rows)
+        if low > 0:
+            weights = jnp.zeros_like(weights)
+        front = jnp.concatenate([hub_terms[:, :half], weights[:, :half]], axis=1)
+        back = jnp.concatenate([hub_terms[:, half:], weights[:, half:]], axis=1)
+        keep, give = jnp.where(first_core, front, back), jnp.where(first_core, back, front).astype(bf16)
+        at = slice(low // hub_rows, (low + step) // hub_rows)
         for piece in range(pieces):
-            at = piece * tall + place
-            pay_ref[low:high, at : at + rows, :] = value[:, :, piece * LANES : (piece + 1) * LANES]
-
-    def term_rows(first, count):
-        return jnp.transpose(terms[:, first : first + count])
-
-    holders = 2 * width // 16
-    put(0, holders, slab, 16, term_rows(0, 2 * width))
-    if parts > holders:
-        put(holders, parts, slab, 16, jnp.zeros(((parts - holders) * 16, width), f32))
-    step = 2 * width
-    for low, total_rows, place, rows in ((0, bounds, 0, slots), (bounds, hubs, slots, hub_rows)):
-        for first in range(0, total_rows, step):
-            put(first // rows, (first + step) // rows, place, rows, term_rows(2 * width + low + first, step))
+            there = slice(piece * hub_rows, (piece + 1) * hub_rows)
+            keep_ref[at, there, :] = keep[:, :, lanes(piece)]
+            give_ref[at, there, :] = give[:, :, lanes(piece)]
     bias_total = dot(jnp.ones((16, nodes), bf16), grad_all[...])[:1]
-    high = bias_total.astype(bf16).astype(f32)
+    rows = bias_rows([bias_total[:, lanes(piece)] for piece in range(pieces)])
+    keep_ref[:, pieces * hub_rows :, :] = jnp.broadcast_to(rows[None], (parts, 8, LANES))
+    give_ref[:, pieces * hub_rows :, :] = jnp.broadcast_to(rows.astype(bf16)[None], (parts, 8, LANES))
+    for low in range(0, bounds, step):
+        bound_terms = term_rows(step + low, slots).astype(bf16)
+        for piece in range(pieces):
+            bound_ref[low // slots : (low + step) // slots, piece * slots : (piece + 1) * slots, :] = (
+                bound_terms[:, :, lanes(piece)]
+            )
+    for store in stores:
+        store.wait()
+
+
+def bias_rows(parts):
     line = lax.broadcasted_iota(jnp.int32, (8, LANES), 0)
     rows = jnp.zeros((8, LANES), f32)
-    for piece in range(pieces):
-        lanes = slice(piece * LANES, (piece + 1) * LANES)
-        rows = jnp.where(line == piece, high[:, lanes], rows)
-        rows = jnp.where(line == pieces + piece, (bias_total - high)[:, lanes], rows)
-    pay_ref[:, pieces * tall :, :] = jnp.broadcast_to(rows.astype(bf16)[None], (parts, 8, LANES))
-    for store in stores:
-        store.wait()
-
-
-def sums_kernel(scale, slots, hub_rows, back_ref, wn_ref, weight_ref, bias_ref, hub_ref):
-    tall = slots + hub_rows + 16
-    pieces = back_ref.shape[1] // tall
-    sums = [
-        jnp.sum(back_ref[:, piece * tall + slots : (piece + 1) * tall, :].astype(f32), axis=0)
-        for piece in range(pieces)
-    ]
-    total = jnp.concatenate(sums, axis=1)
-    weight_ref[...] = jnp.broadcast_to(total[hub_rows:].astype(bf16)[None], weight_ref.shape)
-    tail = jnp.sum(back_ref[:, pieces * tall :, :].astype(f32), axis=0)
+    for piece, value in enumerate(parts):
+        high = value.astype(bf16).astype(f32)
+        rows = jnp.where(line == piece, high, rows)
+        rows = jnp.where(line == len(parts) + piece, value - high, rows)
+    return rows
+
+
+def join_kernel(bound_ref, keep_ref, got_ref, out_ref):
+    parts, tall, _ = keep_ref.shape
+    place = bound_ref.shape[1]
+    pieces = (tall - 8) // 16
+    out_ref[:, :place, :] = bound_ref[...]
+    both = keep_ref[:, : tall - 8, :] + got_ref[:, : tall - 8, :].astype(f32)
+    out_ref[:, place : place + tall - 8, :] = both.astype(bf16)
+    tail = keep_ref[0, tall - 8 :, :] + got_ref[0, tall - 8 :, :].astype(f32)
+    rows = bias_rows([tail[piece : piece + 1] + tail[pieces + piece : pieces + piece + 1] for piece in range(pieces)])
+    out_ref[:, place + tall - 8 :, :] = jnp.broadcast_to(rows.astype(bf16)[None], (parts, 8, LANES))
+
+
+def sums_kernel(scale, slots, hub_rows, rows, back_ref, wn_ref, weight_ref, bias_ref, hub_ref):
+    parts, tall, _ = back_ref.shape
+    pieces = (tall - 8) // (slots + hub_rows)
+    half = hub_rows // 2
+    whole = back_ref[:, pieces * slots :, :].astype(f32)
+    count = whole.shape[1]
+    whole = whole.reshape(rows // 2, 2, parts // rows, count, LANES)
+    total = jnp.sum(jnp.sum(whole, axis=2), axis=0)
+
+    def table(first):
+        return jnp.concatenate(
+            [
+                jnp.concatenate([total[core, piece * hub_rows + first : piece * hub_rows + first + half] for core in (0, 1)], axis=0)
+                for piece in range(pieces)
+            ],
+            axis=1,
+        )
+
+    weight_ref[...] = jnp.broadcast_to(table(half).astype(bf16)[None], weight_ref.shape)
+    tail = 0.5 * (total[0, count - 8 :] + total[1, count - 8 :])
     bias_ref[...] = jnp.concatenate(
         [tail[piece : piece + 1] + tail[pieces + piece : pieces + piece + 1] for piece in range(pieces)], axis=1
     )
-    hub = total[:hub_rows]
+    hub = table(0)
     high = hub.astype(bf16)
     low = (hub - high.astype(f32)).astype(bf16)
     hub_ref[...] = (dot(high, wn_ref[...], NT) + dot(low, wn_ref[...], NT)) * scale
@@ -253,10 +293,12 @@
     height, width = out_ref.shape
     first = pl.program_id(0) * height
     count = send_ref.shape[1]
-    pieces = width // LANES
-    tall = back_ref.shape[1] // pieces // 16 * 16
     returned = jnp.concatenate(
-        [back_ref[:, piece * tall : piece * tall + slots, :].reshape(count, LANES) for piece in range(pieces)], axis=1
+        [
+            back_ref[:, piece * slots : (piece + 1) * slots, :].reshape(count, LANES)
+            for piece in range(width // LANES)
+        ],
+        axis=1,
     )
     total = scat_ref[...]
     for start in range(0, count, 512):
@@ -304,7 +346,9 @@
     slots = send_rows.shape[1] // parts
     slab = slots + hub_rows
     pieces = width // LANES
-    pay = pieces * (slab + 16) + 8
+    pay = pieces * slab + 8
+    core = (lax.axis_index("row") % 2).astype(jnp.int32).reshape(1)
+    rows = lax.axis_size("row")
     table = parts * slab
     scale = 1.0 / (local_edges.shape[1] + hub_edges.shape[1] + remote_edges.shape[1])
     local_t, hub_t, remote_t = local_edges.T, hub_edges.T, remote_edges.T
@@ -344,12 +388,17 @@
         moved=nodes * packed * 2,
     )
 
-    activated, grad_pre, terms = call(
+    activated, grad_pre, bound_terms, keep, give = call(
         functools.partial(middle_kernel, scale, slots),
-        [received, w_self, w_neigh, bias, local_sum, pack],
-        [VMEM] * 5 + [HBM],
-        [pltpu.HBM((nodes, width), bf16)] * 2 + [shape((parts, pay, LANES), bf16)],
-        [HBM] * 2 + [VMEM],
+        [core, received, w_self, w_neigh, bias, local_sum, pack],
+        [SMEM] + [VMEM] * 5 + [HBM],
+        [pltpu.HBM((nodes, width), bf16)] * 2
+        + [
+            shape((parts, pieces * slots, LANES), bf16),
+            shape((parts, pieces * hub_rows + 8, LANES), f32),
+            shape((parts, pieces * hub_rows + 8, LANES), bf16),
+        ],
+        [HBM] * 2 + [VMEM] * 3,
         "activate",
         limit=MUCH_VMEM,
         scratch=[
@@ -363,7 +412,18 @@
         flops=4 * nodes * table * width,
         moved=nodes * packed * 2,
     )
-    back = exchange(terms)
+    got = lax.ppermute(give, "row", [(r, r ^ 1) for r in range(rows)])
+    back = exchange(
+        call(
+            join_kernel,
+            [bound_terms, keep, got],
+            [VMEM] * 3,
+            shape((parts, pay, LANES), bf16),
+            VMEM,
+            "join_siblings",
+            moved=parts * pay * LANES * 6,
+        )
+    )
 
     scattered = call(
         scatter_kernel,
@@ -377,7 +437,7 @@
         moved=nodes * width * 6,
     )
     weight_rows, grad_bias, grad_hubs = call(
-        functools.partial(sums_kernel, scale, slots, hub_rows),
+        functools.partial(sums_kernel, scale, slots, hub_rows, rows),
         (back, w_neigh),
         [VMEM, VMEM],
         [shape((parts, 16, width), bf16), shape((1, width), f32), shape((hub_rows, width), f32)],

time: 74.5 us -> 70.6 us (0.948)
  blocking collectives: 25.5 us -> 19.8 us
  waiting for transfers between devices: 9.25 us -> 10.9 us
    all_to_all x1, blocking collectives: 25.5 us -> 19.8 us  [exchange(): return lax.all_to_all(value, AXES, split_axis=0, concat_axis=0, tiled=True)]
    ppermute x0 -> x1, waiting for transfers between devices: none -> 1.62 us  [body(): got = lax.ppermute(give, 'row', [(r, r ^ 1) for r in range(rows)])]
    pallas_call x6 -> x7, Pallas kernels: 25.4 us -> 25.5 us  [call(): pl.pallas_call(kernel, grid=grid, in_specs=in_specs, out_specs=out_specs,...]
  transfers between devices with their start and end apart: 2 -> 3, of which waited for: 2 -> 3; matrix products, arithmetic and copies ran while one was open for 0% -> 0% of each run, Pallas kernels for 21% -> 22%
where the time goes in v7:
time: 70.6 us; the launch traced here: 70.2 us
  Pallas kernels  25.5 us (36%)
  blocking collectives  19.8 us (28%)
  waiting for transfers between devices  10.9 us (15%)
  starting transfers between devices  9.95 us (14%)
  local copies, waits for them, and re-layouts  3.32 us (5%)
  between operations  0.78 us (1%)
    pallas_call x7, Pallas kernels, call(): pl.pallas_call(kernel, grid=grid, in_specs=in_specs, out_specs=out_specs,...  25.5 us
    all_to_all x1, blocking collectives, exchange(): return lax.all_to_all(value, AXES, split_axis=0, concat_axis=0, tiled=True)  19.8 us
    all_to_all x2, starting transfers between devices, exchange(): return lax.all_to_all(value, AXES, split_axis=0, concat_axis=0, tiled=True)  9.88 us
    all_to_all x2, waiting for transfers between devices, exchange(): return lax.all_to_all(value, AXES, split_axis=0, concat_axis=0, tiled=True)  9.24 us
    unnamed x20, local copies, waits for them, and re-layouts  2.48 us
    ppermute x1, waiting for transfers between devices, body(): got = lax.ppermute(give, 'row', [(r, r ^ 1) for r in range(rows)])  1.62 us
  transfers between devices with their start and end apart: 3, of which 3 were waited for; matrix products, arithmetic and copies ran while one was open for 0% of the time, Pallas kernels for 22%

profile of v7, /device:TPU:0, one launch (start us, length us, event | category | flops | bytes accessed | tf_op | source)
XLA Modules:
  0.0 70.2 jit_solution(4322012014351127235)
XLA Ops:
  0.6 0.0 copy-start.7
  0.6 0.0 copy-start.9
  0.7 0.0 copy-start.8
  0.7 2.8 %pick_rows.1 = bf16[32,32,256]{2,1,0:T(8,128)(2,1)} custom-call(s32[1,512]{1,0:T(1,128)} %send_ref.3, bf16[2048,256]{1,0:T(8,128)(2,1)} %own_ref, bf16[16,256]{1,0:T(8,128)(2,1)} %hub_ref.1), custom_call_target="tpu_custom_call" | custom-call | flops 536870912 | bytes 1048576 | tf_op jit(solution)/shard_map/pick_rows/pallas_call | solution.py:314
  3.5 7.3 %all-to-all-start = ((bf16[32,32,256]{2,1,0:T(8,128)(2,1)}), bf16[32,32,256]{2,1,0:T(8,128)(2,1)S(1)}, u32[]{:S(2)}, u32[]{:S(2)}) async-start(bf16[32,32,256]{2,1,0:T(8,128)(2,1)} %pick_rows.1), calls=%async_computation | async-start | bytes 1048576 | tf_op jit(solution)/shard_map/all_to_all | solution.py:359
  10.8 0.0 copy-done.7
  10.8 0.0 copy-done.9
  10.8 0.0 copy-done.8
  10.8 0.0 copy-start.5
  10.8 1.2 %copy-done.5 = bf16[2048,256]{1,0:T(8,128)(2,1)S(1)} copy-done((bf16[2048,256]{1,0:T(8,128)(2,1)S(1)}, bf16[2048,256]{1,0:T(8,128)(2,1)}, u32[]{:S(2)}) %copy-start.5) | copy-done | bytes 1048600
  12.0 0.0 copy-start.6
  12.0 1.2 %copy-done.6 = bf16[2048,256]{1,0:T(8,128)(2,1)S(1)} copy-done((bf16[2048,256]{1,0:T(8,128)(2,1)S(1)}, bf16[2048,256]{1,0:T(8,128)(2,1)}, u32[]{:S(2)}) %copy-start.6) | copy-done | bytes 1048600
  13.3 0.0 copy-start
  13.3 7.1 %local_gather.1 = (f32[2048,256]{1,0:T(8,128)S(1)}, bf16[2048,1536]{1,0:T(8,128)(2,1)}) custom-call(s32[4,2048]{1,0:T(4,128)S(1)} %bitcast.10, s32[4,2048]{1,0:T(4,128)S(1)} %bitcast.9, s32[2,2048]{1,0:T(2,128)S(1)} %bitcast.12, bf16[2048,256]{1,0:T(8,128)(2,1)S(1)} %copy-done.5, bf16[2048,256]{1,0:T(8,128)(2,1)S(1)} %copy-done.5, ...), custom_call_target="tpu_custom_call" | custom-call | flops 8589934592 | bytes 6291456 | tf_op jit(solution)/shard_map/local_gather/pallas_call | solution.py:314
  20.4 6.7 %all-to-all-done.table_ref = bf16[32,32,256]{2,1,0:T(8,128)(2,1)S(1)} async-done(((bf16[32,32,256]{2,1,0:T(8,128)(2,1)}), bf16[32,32,256]{2,1,0:T(8,128)(2,1)S(1)}, u32[]{:S(2)}, u32[]{:S(2)}) %all-to-all-start) | async-done | bytes 524320 | tf_op jit(solution)/shard_map/all_to_all | solution.py:359
  27.1 0.0 copy-done
  27.1 0.0 copy-done.2
  27.1 0.0 copy-done.4
  27.1 6.6 %activate.1 = (bf16[2048,256]{1,0:T(8,128)(2,1)}, bf16[2048,256]{1,0:T(8,128)(2,1)}, bf16[32,32,128]{2,1,0:T(8,128)(2,1)S(1)}, f32[32,40,128]{2,1,0:T(8,128)S(1)}, bf16[32,40,128]{2,1,0:T(8,128)(2,1)S(1)}) custom-call(s32[1]{0:T(128)} %bitcast.core_ref, bf16[32,32,256]{2,1,0:T(8,128)(2,1)S(1)} %all-to-all-done.table_ref, bf16[256,256]{1,0:T(8,128)(2,1)S(1)} %copy-done.2, ...), custom_call_target="tpu_custom_call" | custom-call | flops 2147483648 | bytes 6291456 | tf_op jit(solution)/shard_map/activate/pallas_call | solution.py:314
  33.7 0.1 collective-permute-start
  33.8 1.6 %collective-permute-done.got_ref = bf16[32,40,128]{2,1,0:T(8,128)(2,1)S(1)} collective-permute-done((bf16[32,40,128]{2,1,0:T(8,128)(2,1)S(1)}, bf16[32,40,128]{2,1,0:T(8,128)(2,1)S(1)}, u32[]{:S(2)}, u32[]{:S(2)}) %collective-permute-start) | collective-permute-done | bytes 327712 | tf_op jit(solution)/shard_map/ppermute | solution.py:415
  35.4 0.1 join_siblings.1
  35.5 19.8 %all_to_all.15.back_ref = bf16[32,72,128]{2,1,0:T(8,128)(2,1)S(1)} all-to-all(bf16[32,72,128]{2,1,0:T(8,128)(2,1)S(1)} %join_siblings.1), channel_id=1, replica_groups=mesh['row'=4,'col'=8] {'row','col'}, dimensions={0} | all-to-all | bytes 1179648 | tf_op jit(solution)/shard_map/all_to_all | solution.py:359
  55.3 0.8 %sums.1 = (bf16[32,16,256]{2,1,0:T(8,128)(2,1)}, f32[1,256]{1,0:T(1,128)}, f32[16,256]{1,0:T(8,128)}) custom-call(bf16[32,72,128]{2,1,0:T(8,128)(2,1)S(1)} %all_to_all.15.back_ref, bf16[256,256]{1,0:T(8,128)(2,1)S(1)} %copy-done), custom_call_target="tpu_custom_call" | custom-call | bytes 1179648 | tf_op jit(solution)/shard_map/sums/pallas_call | solution.py:314
  56.1 2.6 %all-to-all-start.2 = ((bf16[32,16,256]{2,1,0:T(8,128)(2,1)}), bf16[32,16,256]{2,1,0:T(8,128)(2,1)S(1)}, u32[]{:S(2)}, u32[]{:S(2)}) async-start(bf16[32,16,256]{2,1,0:T(8,128)(2,1)} %get-tuple-element.28), calls=%async_computation.2 | async-start | bytes 524288 | tf_op jit(solution)/shard_map/all_to_all | solution.py:359
  58.7 0.0 copy-done.1
  58.7 0.0 copy-start.3
  58.7 4.4 %local_scatter.1.scat_ref = f32[2048,256]{1,0:T(8,128)S(1)} custom-call(s32[4,2048]{1,0:T(4,128)S(1)} %bitcast.11, bf16[2048,256]{1,0:T(8,128)(2,1)S(1)} %copy-done.1), custom_call_target="tpu_custom_call" | custom-call | flops 8589934592 | bytes 3145728 | tf_op jit(solution)/shard_map/local_scatter/pallas_call | solution.py:314
  63.2 0.0 copy-done.3
  63.2 3.6 %return_scatter.1 = f32[2048,256]{1,0:T(8,128)} custom-call(s32[1,512]{1,0:T(1,128)S(1)} %copy-done.3, bf16[32,72,128]{2,1,0:T(8,128)(2,1)S(1)} %all_to_all.15.back_ref, f32[2048,256]{1,0:T(8,128)S(1)} %local_scatter.1.scat_ref, bf16[2048,256]{1,0:T(8,128)(2,1)S(1)} %copy-done.1, bf16[256,256]{1,0:T(8,128)(2,1)S(1)} %copy-done.2, bf16[256,256]{1,0:T(8,128)(2,1)S(1)} %copy-done), custom_call_target="tpu_custom_call" | custom-call | flops 536870912 | bytes 5242880 | tf_op jit(solution)/shard_map/return_scatter/pallas_call | solution.py:314
  66.8 2.5 %all-to-all-done.2 = bf16[32,16,256]{2,1,0:T(8,128)(2,1)S(1)} async-done(((bf16[32,16,256]{2,1,0:T(8,128)(2,1)}), bf16[32,16,256]{2,1,0:T(8,128)(2,1)S(1)}, u32[]{:S(2)}, u32[]{:S(2)}) %all-to-all-start.2) | async-done | bytes 262176 | tf_op jit(solution)/shard_map/all_to_all | solution.py:359
  69.4 0.8 %fusion = (f32[16,16,256]{2,1,0:T(8,128)}, f32[16,16,256]{2,1,0:T(8,128)}) fusion(bf16[32,16,256]{2,1,0:T(8,128)(2,1)S(1)} %all-to-all-done.2), kind=kLoop, calls=%fused_computation | loop fusion | bytes 1048576 | tf_op jit(solution)/shard_map/slice | solution.py:465
  (3 shorter events, 0.0 us)
Async XLA Ops:
  0.6 10.1 %copy-start.7 = (s32[2048,4]{0,1:T(4,128)S(1)}, s32[2048,4]{0,1:T(4,128)}, u32[]{:S(2)}) copy-start(s32[2048,4]{0,1:T(4,128)} %param.17) | copy-start | bytes 98308
  0.6 10.1 %copy-start.9 = (s32[2048,2]{0,1:T(2,128)S(1)}, s32[2048,2]{0,1:T(2,128)}, u32[]{:S(2)}) copy-start(s32[2048,2]{0,1:T(2,128)} %param.16) | copy-start | bytes 49156
  0.7 10.1 %copy-start.8 = (s32[2048,4]{0,1:T(4,128)S(1)}, s32[2048,4]{0,1:T(4,128)}, u32[]{:S(2)}) copy-start(s32[2048,4]{0,1:T(4,128)} %param.15) | copy-start | bytes 98308
  3.5 23.7 %all-to-all-start = ((bf16[32,32,256]{2,1,0:T(8,128)(2,1)}), bf16[32,32,256]{2,1,0:T(8,128)(2,1)S(1)}, u32[]{:S(2)}, u32[]{:S(2)}) async-start(bf16[32,32,256]{2,1,0:T(8,128)(2,1)} %pick_rows.1), calls=%async_computation | async-start | bytes 1048576 | tf_op jit(solution)/shard_map/all_to_all | solution.py:359
  10.8 1.2 %copy-start.5 = (bf16[2048,256]{1,0:T(8,128)(2,1)S(1)}, bf16[2048,256]{1,0:T(8,128)(2,1)}, u32[]{:S(2)}) copy-start(bf16[2048,256]{1,0:T(8,128)(2,1)} %own_ref) | copy-start | bytes 3145732
  12.0 1.2 %copy-start.6 = (bf16[2048,256]{1,0:T(8,128)(2,1)S(1)}, bf16[2048,256]{1,0:T(8,128)(2,1)}, u32[]{:S(2)}) copy-start(bf16[2048,256]{1,0:T(8,128)(2,1)} %cot_ref.1) | copy-start | bytes 3145732
  13.3 13.9 %copy-start = (bf16[256,256]{1,0:T(8,128)(2,1)S(1)}, bf16[256,256]{1,0:T(8,128)(2,1)}, u32[]{:S(2)}) copy-start(bf16[256,256]{1,0:T(8,128)(2,1)} %wn_ref.5) | copy-start | bytes 393220
  13.3 13.9 %copy-start.2 = (bf16[256,256]{1,0:T(8,128)(2,1)S(1)}, bf16[256,256]{1,0:T(8,128)(2,1)}, u32[]{:S(2)}) copy-start(bf16[256,256]{1,0:T(8,128)(2,1)} %ws_ref.3) | copy-start | bytes 393220
  13.3 13.9 %copy-start.4 = (f32[256]{0:T(256)S(1)}, f32[256]{0:T(256)}, u32[]{:S(2)}) copy-start(f32[256]{0:T(256)} %param.14) | copy-start | bytes 3076
  33.7 1.7 %collective-permute-start = (bf16[32,40,128]{2,1,0:T(8,128)(2,1)S(1)}, bf16[32,40,128]{2,1,0:T(8,128)(2,1)S(1)}, u32[]{:S(2)}, u32[]{:S(2)}) collective-permute-start(bf16[32,40,128]{2,1,0:T(8,128)(2,1)S(1)} %get-tuple-element.25), channel_id=1, source_target_pairs={{0,8},{8,0},{16,24},{24,16},{1,9},{9,1},{17,25},{25,17},{2,10},{10... | collective-permute-start | bytes 983048 | tf_op jit(solution)/shard_map/ppermute | solution.py:415
  35.4 23.3 %copy-start.1 = (bf16[2048,256]{1,0:T(8,128)(2,1)S(1)}, bf16[2048,256]{1,0:T(8,128)(2,1)}, u32[]{:S(2)}) copy-start(bf16[2048,256]{1,0:T(8,128)(2,1)} %get-tuple-element.26.grad_ref) | copy-start | bytes 3145732
  56.1 13.2 %all-to-all-start.2 = ((bf16[32,16,256]{2,1,0:T(8,128)(2,1)}), bf16[32,16,256]{2,1,0:T(8,128)(2,1)S(1)}, u32[]{:S(2)}, u32[]{:S(2)}) async-start(bf16[32,16,256]{2,1,0:T(8,128)(2,1)} %get-tuple-element.28), calls=%async_computation.2 | async-start | bytes 524288 | tf_op jit(solution)/shard_map/all_to_all | solution.py:359
  58.7 4.4 %copy-start.3 = (s32[1,512]{1,0:T(1,128)S(1)}, s32[1,512]{1,0:T(1,128)}, u32[]{:S(2)}) copy-start(s32[1,512]{1,0:T(1,128)} %send_ref.3) | copy-start | bytes 6148

commit v8 on v7

--- a/solution.py
+++ b/solution.py
@@ -77,10 +77,17 @@
     return [ref[j : j + 1, pl.ds(start, count)] for j in range(ref.shape[0])]
 
 
-def pick_kernel(send_ref, feat_ref, hub_ref, out_ref):
+def by_core(value, rows, cols):
+    half = value.shape[0] // 2
+    value = value.astype(f32)
+    halves = [value[core * half : (core + 1) * half] for core in (0, 1)]
+    blocks = [jnp.broadcast_to(halves[row % 2][None], (cols,) + halves[0].shape) for row in range(rows)]
+    return jnp.concatenate(blocks, axis=0).astype(bf16)
+
+
+def pick_kernel(rows, send_ref, feat_ref, hub_ref, out_ref):
     parts, slab, width = out_ref.shape
-    hub_rows = hub_ref.shape[0]
-    slots = slab - hub_rows
+    slots = slab - hub_ref.shape[0] // 2
     total = send_ref.shape[1]
     step = min(512, total)
     for start in range(0, total, step):
@@ -89,10 +96,14 @@
         out_ref[start // slots : (start + step) // slots, :slots, :] = (
             picked.astype(bf16).reshape(step // slots, slots, width)
         )
-    out_ref[:, slots:, :] = jnp.broadcast_to(hub_ref[...][None], (parts, hub_rows, width))
-
-
-def local_kernel(split, local_ref, remote_ref, hub_ref, feat_ref, own_ref, cot_ref, sum_ref, pack_ref):
+    out_ref[:, slots:, :] = by_core(hub_ref[...], rows, parts // rows)
+
+
+def half_kernel(slots, table_ref, out_ref):
+    out_ref[...] = table_ref[:, slots:, :].astype(f32).reshape(out_ref.shape).astype(bf16)
+
+
+def local_kernel(split, hub_rows, core_ref, local_ref, remote_ref, hub_ref, feat_ref, own_ref, cot_ref, sum_ref, pack_ref):
     nodes, width = feat_ref.shape
     columns = [along_rows(row) for row in index_rows(local_ref, 0, TILE)]
     total = None
@@ -104,8 +115,16 @@
     pack_ref[:, width : 2 * width] = own_ref[...]
     place = 2 * width
     counts = pack_ref.shape[1] - place
-    for ref, share in ((remote_ref, split), (hub_ref, counts - split)):
-        columns = [along_rows(row) for row in index_rows(ref, 0, TILE)]
+    half = hub_rows // 2
+    hubs = []
+    for hub in index_rows(hub_ref, 0, TILE):
+        owner = lax.div(hub, jnp.int32(hub_rows))
+        within = hub - owner * hub_rows
+        other = (within >= half) != (core_ref[0] == 1)
+        within = jnp.where(within >= half, within - half, within)
+        hubs.append(owner * half + within + jnp.where(other, (counts - split) // 2, 0))
+    for index, share in ((index_rows(remote_ref, 0, TILE), split), (hubs, counts - split)):
+        columns = [along_rows(row) for row in index]
         for first in range(0, share, TILE):
             pack_ref[:, place + first : place + first + TILE] = hits_by_row(columns, first, TILE)
         place += share
@@ -116,6 +135,8 @@
     slots,
     core_ref,
     table_ref,
+    near_ref,
+    far_ref,
     ws_ref,
     wn_ref,
     bias_ref,
@@ -135,7 +156,8 @@
 ):
     nodes, width = sum_ref.shape
     parts, slab, _ = table_ref.shape
-    hub_rows = slab - slots
+    half = slab - slots
+    hub_rows = 2 * half
     bounds, hubs = parts * slots, parts * hub_rows
     size = 2 * TILE
     blocks = nodes // size
@@ -156,7 +178,7 @@
         for copy in group:
             copy.start()
     table = jnp.concatenate(
-        [table_ref[:, :slots, :].reshape(bounds, width), table_ref[:, slots:, :].reshape(hubs, width)], axis=0
+        [table_ref[:, :slots, :].reshape(bounds, width), near_ref[...], far_ref[...]], axis=0
     )
     half_weights = jnp.concatenate([ws_ref[...], wn_ref[...]], axis=0) * jnp.bfloat16(0.5)
     half_bias = 0.5 * bias_ref[...]
@@ -175,11 +197,11 @@
         if 0 < block <= blocks:
             at = here(block - 1)
             pack[at, 2 * width : counts] = (total * scale).astype(bf16)
-            half = dot(pack[at, width:counts], half_weights) + half_bias
-            tanh = jnp.tanh(half)
+            arg = dot(pack[at, width:counts], half_weights) + half_bias
+            tanh = jnp.tanh(arg)
             above = 1.0 + tanh
-            act[at, :] = (half * above).astype(bf16)
-            slope = above * (0.5 + (0.5 * half) * (1.0 - tanh))
+            act[at, :] = (arg * above).astype(bf16)
+            slope = above * (0.5 + (0.5 * arg) * (1.0 - tanh))
             grad = (pack[at, :width].astype(f32) * slope).astype(bf16)
             grad_all[at, :] = grad
             turned = jnp.transpose(grad)
@@ -192,23 +214,24 @@
     pieces = width // LANES
     step = 2 * width
 
-    def term_rows(first, rows):
-        return jnp.transpose(terms[:, first : first + step]).reshape(step // rows, rows, width)
+    def term_rows(first, count, rows):
+        return jnp.transpose(terms[:, first : first + count]).reshape(count // rows, rows, width)
 
     def lanes(piece):
         return slice(piece * LANES, (piece + 1) * LANES)
 
     first_core = core_ref[0] == 0
-    half = hub_rows // 2
-    weights = term_rows(0, hub_rows)
-    for low in range(0, hubs, step):
-        hub_terms = term_rows(step + bounds + low, hub_rows)
+    weights = term_rows(0, step, hub_rows)
+    own = jnp.where(first_core, weights[:, :half], weights[:, half:])
+    other = jnp.where(first_core, weights[:, half:], weights[:, :half])
+    count = step // hub_rows
+    for low in range(0, parts, count):
         if low > 0:
-            weights = jnp.zeros_like(weights)
-        front = jnp.concatenate([hub_terms[:, :half], weights[:, :half]], axis=1)
-        back = jnp.concatenate([hub_terms[:, half:], weights[:, half:]], axis=1)
-        keep, give = jnp.where(first_core, front, back), jnp.where(first_core, back, front).astype(bf16)
-        at = slice(low // hub_rows, (low + step) // hub_rows)
+            own = other = jnp.zeros_like(own)
+        first = step + bounds + low * half
+        keep = jnp.concatenate([term_rows(first, count * half, half), own], axis=1)
+        give = jnp.concatenate([term_rows(first + hubs // 2, count * half, half), other], axis=1).astype(bf16)
+        at = slice(low, low + count)
         for piece in range(pieces):
             there = slice(piece * hub_rows, (piece + 1) * hub_rows)
             keep_ref[at, there, :] = keep[:, :, lanes(piece)]
@@ -218,7 +241,7 @@
     keep_ref[:, pieces * hub_rows :, :] = jnp.broadcast_to(rows[None], (parts, 8, LANES))
     give_ref[:, pieces * hub_rows :, :] = jnp.broadcast_to(rows.astype(bf16)[None], (parts, 8, LANES))
     for low in range(0, bounds, step):
-        bound_terms = term_rows(step + low, slots).astype(bf16)
+        bound_terms = term_rows(step + low, step, slots).astype(bf16)
         for piece in range(pieces):
             bound_ref[low // slots : (low + step) // slots, piece * slots : (piece + 1) * slots, :] = (
                 bound_terms[:, :, lanes(piece)]
@@ -249,33 +272,51 @@
     out_ref[:, place + tall - 8 :, :] = jnp.broadcast_to(rows.astype(bf16)[None], (parts, 8, LANES))
 
 
-def sums_kernel(scale, slots, hub_rows, rows, back_ref, wn_ref, weight_ref, bias_ref, hub_ref):
+def chip_sums(slots, hub_rows, rows, back_ref):
     parts, tall, _ = back_ref.shape
     pieces = (tall - 8) // (slots + hub_rows)
-    half = hub_rows // 2
     whole = back_ref[:, pieces * slots :, :].astype(f32)
     count = whole.shape[1]
     whole = whole.reshape(rows // 2, 2, parts // rows, count, LANES)
-    total = jnp.sum(jnp.sum(whole, axis=2), axis=0)
-
-    def table(first):
-        return jnp.concatenate(
-            [
-                jnp.concatenate([total[core, piece * hub_rows + first : piece * hub_rows + first + half] for core in (0, 1)], axis=0)
-                for piece in range(pieces)
-            ],
-            axis=1,
-        )
-
-    weight_ref[...] = jnp.broadcast_to(table(half).astype(bf16)[None], weight_ref.shape)
-    tail = 0.5 * (total[0, count - 8 :] + total[1, count - 8 :])
+    return jnp.sum(jnp.sum(whole, axis=2), axis=0), pieces
+
+
+def both_halves(total, pieces, hub_rows, first):
+    half = hub_rows // 2
+    columns = []
+    for piece in range(pieces):
+        place = piece * hub_rows + first
+        columns.append(jnp.concatenate([total[0, place : place + half], total[1, place : place + half]], axis=0))
+    return jnp.concatenate(columns, axis=1)
+
+
+def weight_sum_kernel(slots, hub_rows, rows, back_ref, out_ref):
+    total, pieces = chip_sums(slots, hub_rows, rows, back_ref)
+    weight = both_halves(total, pieces, hub_rows, hub_rows // 2)
+    out_ref[...] = by_core(weight.astype(bf16), rows, out_ref.shape[0] // rows)
+
+
+def other_sums_kernel(scale, slots, hub_rows, rows, back_ref, wn_ref, bias_ref, hub_ref):
+    total, pieces = chip_sums(slots, hub_rows, rows, back_ref)
+    tail = 0.5 * (total[0, pieces * hub_rows :] + total[1, pieces * hub_rows :])
     bias_ref[...] = jnp.concatenate(
         [tail[piece : piece + 1] + tail[pieces + piece : pieces + piece + 1] for piece in range(pieces)], axis=1
     )
-    hub = table(0)
+    hub = both_halves(total, pieces, hub_rows, 0)
     high = hub.astype(bf16)
     low = (hub - high.astype(f32)).astype(bf16)
     hub_ref[...] = (dot(high, wn_ref[...], NT) + dot(low, wn_ref[...], NT)) * scale
+
+
+def weights_kernel(core_ref, near_ref, far_ref, self_ref, neigh_ref):
+    width = self_ref.shape[0]
+    count = 2 * width // 16
+    near, far = near_ref[:count].astype(f32), far_ref[:count].astype(f32)
+    first_core = core_ref[0] == 0
+    whole = jnp.concatenate([jnp.where(first_core, near, far), jnp.where(first_core, far, near)], axis=1)
+    whole = whole.reshape(2 * width, width)
+    self_ref[...] = whole[:width]
+    neigh_ref[...] = whole[width:]
 
 
 def scatter_kernel(local_ref, grad_ref, out_ref):
@@ -349,21 +390,25 @@
     pay = pieces * slab + 8
     core = (lax.axis_index("row") % 2).astype(jnp.int32).reshape(1)
     rows = lax.axis_size("row")
+    half = hub_rows // 2
     table = parts * slab
     scale = 1.0 / (local_edges.shape[1] + hub_edges.shape[1] + remote_edges.shape[1])
     local_t, hub_t, remote_t = local_edges.T, hub_edges.T, remote_edges.T
     bias = out_bias.reshape(1, width)
     shape = jax.ShapeDtypeStruct
 
+    def sibling(value):
+        return lax.ppermute(value, "row", [(r, r ^ 1) for r in range(rows)])
+
     def exchange(value):
         return lax.all_to_all(value, AXES, split_axis=0, concat_axis=0, tiled=True)
 
     sending = call(
-        pick_kernel,
+        functools.partial(pick_kernel, rows),
         (send_rows, features, hub_features),
         [VMEM, VMEM, VMEM],
-        shape((parts, slab, width), bf16),
-        whole_block((parts, slab, width)),
+        shape((parts, slots + half, width), bf16),
+        whole_block((parts, slots + half, width)),
         "pick_rows",
         limit=MOST_VMEM,
         flops=2 * parts * slots * nodes * width,
@@ -376,9 +421,10 @@
     by_block = pl.BlockSpec((block, width), lambda i: (i, 0))
     packed = 2 * width + table
     local_sum, pack = call(
-        functools.partial(local_kernel, parts * slots),
-        (local_t, remote_t, hub_t, features, features, cotangent),
-        [pl.BlockSpec((edges.shape[0], block), lambda i: (0, i)) for edges in (local_t, remote_t, hub_t)]
+        functools.partial(local_kernel, parts * slots, hub_rows),
+        (core, local_t, remote_t, hub_t, features, features, cotangent),
+        [SMEM]
+        + [pl.BlockSpec((edges.shape[0], block), lambda i: (0, i)) for edges in (local_t, remote_t, hub_t)]
         + [whole_block((nodes, width)), by_block, by_block],
         [shape((nodes, width), f32), pltpu.HBM((nodes, packed), bf16)],
         [by_block, pl.BlockSpec((block, packed), lambda i: (i, 0))],
@@ -388,10 +434,22 @@
         moved=nodes * packed * 2,
     )
 
+    received, local_sum, pack = lax.optimization_barrier((received, local_sum, pack))
+    near_hubs = call(
+        functools.partial(half_kernel, slots),
+        [received],
+        [VMEM],
+        shape((parts * half, width), bf16),
+        VMEM,
+        "take_hubs",
+        moved=parts * half * width * 4,
+    )
+    far_hubs = sibling(near_hubs)
+
     activated, grad_pre, bound_terms, keep, give = call(
         functools.partial(middle_kernel, scale, slots),
-        [core, received, w_self, w_neigh, bias, local_sum, pack],
-        [SMEM] + [VMEM] * 5 + [HBM],
+        [core, received, near_hubs, far_hubs, w_self, w_neigh, bias, local_sum, pack],
+        [SMEM] + [VMEM] * 7 + [HBM],
         [pltpu.HBM((nodes, width), bf16)] * 2
         + [
             shape((parts, pieces * slots, LANES), bf16),
@@ -412,7 +470,7 @@
         flops=4 * nodes * table * width,
         moved=nodes * packed * 2,
     )
-    got = lax.ppermute(give, "row", [(r, r ^ 1) for r in range(rows)])
+    got = sibling(give)
     back = exchange(
         call(
             join_kernel,
@@ -436,16 +494,26 @@
         flops=8 * nodes * nodes * width,
         moved=nodes * width * 6,
     )
-    weight_rows, grad_bias, grad_hubs = call(
-        functools.partial(sums_kernel, scale, slots, hub_rows, rows),
+    back, scattered = lax.optimization_barrier((back, scattered))
+    weight_rows = call(
+        functools.partial(weight_sum_kernel, slots, hub_rows, rows),
+        (back,),
+        [VMEM],
+        shape((parts, 8, width), bf16),
+        VMEM,
+        "weight_sums",
+        moved=parts * pay * width * 2,
+    )
+    near_weights = exchange(weight_rows)
+    grad_bias, grad_hubs = call(
+        functools.partial(other_sums_kernel, scale, slots, hub_rows, rows),
         (back, w_neigh),
         [VMEM, VMEM],
-        [shape((parts, 16, width), bf16), shape((1, width), f32), shape((hub_rows, width), f32)],
-        [whole_block((parts, 16, width)), whole_block((1, width)), whole_block((hub_rows, width))],
-        "sums",
+        [shape((1, width), f32), shape((hub_rows, width), f32)],
+        [whole_block((1, width)), whole_block((hub_rows, width))],
+        "hub_sums",
         moved=parts * pay * width * 2,
     )
-    weights = exchange(weight_rows)
 
     height = 2 * TILE
     by_height = pl.BlockSpec((height, width), lambda i: (i, 0))
@@ -461,8 +529,17 @@
         flops=2 * nodes * parts * slots * width,
         moved=nodes * width * 10,
     )
-    weights = weights[: 2 * width // 16].reshape(2, width, width).astype(f32)
-    return (activated, grad_features, grad_hubs, weights[0], weights[1], grad_bias.reshape(width))
+    near_weights, grad_features = lax.optimization_barrier((near_weights, grad_features))
+    grad_w_self, grad_w_neigh = call(
+        weights_kernel,
+        [core, near_weights, sibling(near_weights)],
+        [SMEM, VMEM, VMEM],
+        [shape((width, width), f32)] * 2,
+        [whole_block((width, width))] * 2,
+        "weights",
+        moved=width * width * 12,
+    )
+    return (activated, grad_features, grad_hubs, grad_w_self, grad_w_neigh, grad_bias.reshape(width))
 
 
 def solution(mesh):

time: 70.6 us -> 68.9 us (0.976)
  blocking collectives: 19.8 us -> 0 us
  waiting for transfers between devices: 10.9 us -> 22.1 us
  starting transfers between devices: 9.95 us -> 12.9 us
  Pallas kernels: 25.5 us -> 27.8 us
  local copies, waits for them, and re-layouts: 3.32 us -> 4.91 us
    all_to_all x1 -> x0, blocking collectives: 19.8 us -> none  [exchange(): return lax.all_to_all(value, AXES, split_axis=0, concat_axis=0, tiled=True)]
    all_to_all x2 -> x3, waiting for transfers between devices: 9.24 us -> 18.8 us  [exchange(): return lax.all_to_all(value, AXES, split_axis=0, concat_axis=0, tiled=True)]
    all_to_all x2 -> x3, starting transfers between devices: 9.88 us -> 12.5 us  [exchange(): return lax.all_to_all(value, AXES, split_axis=0, concat_axis=0, tiled=True)]
    unnamed x20 -> x22, local copies, waits for them, and re-layouts: 2.48 us -> 4.91 us
    pallas_call x7 -> x10, Pallas kernels: 25.5 us -> 27.8 us  [call(): pl.pallas_call(kernel, grid=grid, in_specs=in_specs, out_specs=out_specs,...]
    ppermute x1 -> x3, waiting for transfers between devices: 1.62 us -> 3.27 us  [sibling(): return lax.ppermute(value, 'row', [(r, r ^ 1) for r in range(rows)])]
    slice x1 -> x0, local copies, waits for them, and re-layouts: 0.85 us -> none  [body(): weights[1]]
  transfers between devices with their start and end apart: 3 -> 6, of which waited for: 3 -> 6; matrix products, arithmetic and copies ran while one was open for 0% -> 0% of each run, Pallas kernels for 22% -> 23%
where the time goes in v8:
time: 68.9 us; the launch traced here: 68.4 us
  Pallas kernels  27.8 us (40%)
  waiting for transfers between devices  22.1 us (32%)
  starting transfers between devices  12.9 us (19%)
  local copies, waits for them, and re-layouts  4.91 us (7%)
  between operations  0.79 us (1%)
    pallas_call x10, Pallas kernels, call(): pl.pallas_call(kernel, grid=grid, in_specs=in_specs, out_specs=out_specs,...  27.8 us
    all_to_all x3, waiting for transfers between devices, exchange(): return lax.all_to_all(value, AXES, split_axis=0, concat_axis=0, tiled=True)  18.8 us
    all_to_all x3, starting transfers between devices, exchange(): return lax.all_to_all(value, AXES, split_axis=0, concat_axis=0, tiled=True)  12.5 us
    unnamed x22, local copies, waits for them, and re-layouts  4.91 us
    ppermute x3, waiting for transfers between devices, sibling(): return lax.ppermute(value, 'row', [(r, r ^ 1) for r in range(rows)])  3.27 us
  transfers between devices with their start and end apart: 6, of which 6 were waited for; matrix products, arithmetic and copies ran while one was open for 0% of the time, Pallas kernels for 23%

profile of v8, /device:TPU:0, one launch (start us, length us, event | category | flops | bytes accessed | tf_op | source)
XLA Modules:
  0.0 68.4 jit_solution(13936655381331666947)
XLA Ops:
  0.6 0.0 copy-start.8
  0.6 0.0 copy-start.10
  0.7 0.0 copy-start.9
  0.7 2.7 %pick_rows.1 = bf16[32,24,256]{2,1,0:T(8,128)(2,1)} custom-call(s32[1,512]{1,0:T(1,128)} %send_ref.3, bf16[2048,256]{1,0:T(8,128)(2,1)} %own_ref, bf16[16,256]{1,0:T(8,128)(2,1)} %hub_ref.1), custom_call_target="tpu_custom_call" | custom-call | flops 536870912 | bytes 1048576 | tf_op jit(solution)/shard_map/pick_rows/pallas_call | solution.py:355
  3.4 7.3 %all-to-all-start = ((bf16[32,24,256]{2,1,0:T(8,128)(2,1)}), bf16[32,24,256]{2,1,0:T(8,128)(2,1)S(1)}, u32[]{:S(2)}, u32[]{:S(2)}) async-start(bf16[32,24,256]{2,1,0:T(8,128)(2,1)} %pick_rows.1), calls=%async_computation | async-start | bytes 786432 | tf_op jit(solution)/shard_map/all_to_all | solution.py:404
  10.8 0.0 copy-start.6
  10.8 1.2 %copy-done.6 = bf16[2048,256]{1,0:T(8,128)(2,1)S(1)} copy-done((bf16[2048,256]{1,0:T(8,128)(2,1)S(1)}, bf16[2048,256]{1,0:T(8,128)(2,1)}, u32[]{:S(2)}) %copy-start.6) | copy-done | bytes 1048600
  12.0 1.2 %copy-done.7 = bf16[2048,256]{1,0:T(8,128)(2,1)S(1)} copy-done((bf16[2048,256]{1,0:T(8,128)(2,1)S(1)}, bf16[2048,256]{1,0:T(8,128)(2,1)}, u32[]{:S(2)}) %copy-start.7) | copy-done | bytes 1048600
  13.2 7.2 %local_gather.1 = (f32[2048,256]{1,0:T(8,128)S(1)}, bf16[2048,1536]{1,0:T(8,128)(2,1)}) custom-call(s32[1]{0:T(128)} %bitcast.core_ref, s32[4,2048]{1,0:T(4,128)S(1)} %bitcast.8, s32[4,2048]{1,0:T(4,128)S(1)} %bitcast.7, s32[2,2048]{1,0:T(2,128)S(1)} %bitcast.10, bf16[2048,256]{1,0:T(8,128)(2,1)S(1)} %copy-done.6, bf16[2048,256]{1,0:T(8,128)(2,1)S(1)} %copy-done.6, ...), custom_call_target="tpu_custom_call" | custom-call | flops 8589934592 | bytes 6291456 | tf_op jit(solution)/shard_map/local_gather/pallas_call | solution.py:355
  20.4 3.8 %all-to-all-done.table_ref = bf16[32,24,256]{2,1,0:T(8,128)(2,1)S(1)} async-done(((bf16[32,24,256]{2,1,0:T(8,128)(2,1)}), bf16[32,24,256]{2,1,0:T(8,128)(2,1)S(1)}, u32[]{:S(2)}, u32[]{:S(2)}) %all-to-all-start) | async-done | bytes 393248 | tf_op jit(solution)/shard_map/all_to_all | solution.py:404
  24.3 0.1 collective-permute-start
  24.3 1.3 %collective-permute-done.far_ref = bf16[256,256]{1,0:T(8,128)(2,1)S(1)} collective-permute-done((bf16[256,256]{1,0:T(8,128)(2,1)S(1)}, bf16[256,256]{1,0:T(8,128)(2,1)S(1)}, u32[]{:S(2)}, u32[]{:S(2)}) %collective-permute-start) | collective-permute-done | bytes 131104 | tf_op jit(solution)/shard_map/ppermute | solution.py:401
  25.7 0.0 copy-done.3
  25.7 6.6 %activate.1 = (bf16[2048,256]{1,0:T(8,128)(2,1)}, bf16[2048,256]{1,0:T(8,128)(2,1)}, bf16[32,32,128]{2,1,0:T(8,128)(2,1)S(1)}, f32[32,40,128]{2,1,0:T(8,128)S(1)}, bf16[32,40,128]{2,1,0:T(8,128)(2,1)S(1)}) custom-call(s32[1]{0:T(128)} %bitcast.core_ref, bf16[32,24,256]{2,1,0:T(8,128)(2,1)S(1)} %all-to-all-done.table_ref, ...), custom_call_target="tpu_custom_call" | custom-call | flops 2147483648 | bytes 6291456 | tf_op jit(solution)/shard_map/activate/pallas_call | solution.py:355
  32.3 0.2 collective-permute-start.1
  32.5 1.5 %collective-permute-done.1.got_ref = bf16[32,40,128]{2,1,0:T(8,128)(2,1)S(1)} collective-permute-done((bf16[32,40,128]{2,1,0:T(8,128)(2,1)S(1)}, bf16[32,40,128]{2,1,0:T(8,128)(2,1)S(1)}, u32[]{:S(2)}, u32[]{:S(2)}) %collective-permute-start.1) | collective-permute-done | bytes 327712 | tf_op jit(solution)/shard_map/ppermute | solution.py:401
  34.0 0.9 %join_siblings.1 = bf16[32,72,128]{2,1,0:T(8,128)(2,1)} custom-call(bf16[32,32,128]{2,1,0:T(8,128)(2,1)S(1)} %get-tuple-element.34.bound_ref, f32[32,40,128]{2,1,0:T(8,128)S(1)} %get-tuple-element.35.keep_ref, bf16[32,40,128]{2,1,0:T(8,128)(2,1)S(1)} %collective-permute-done.1.got_ref), custom_call_target="tpu_custom_call" | custom-call | bytes 1769472 | tf_op jit(solution)/shard_map/join_siblings/pallas_call | solution.py:355
  34.9 2.6 %all-to-all-start.1 = ((bf16[32,72,128]{2,1,0:T(8,128)(2,1)}), bf16[32,72,128]{2,1,0:T(8,128)(2,1)S(1)}, u32[]{:S(2)}, u32[]{:S(2)}) async-start(bf16[32,72,128]{2,1,0:T(8,128)(2,1)} %join_siblings.1), calls=%async_computation.1 | async-start | bytes 1179648 | tf_op jit(solution)/shard_map/all_to_all | solution.py:404
  37.5 0.0 copy-start.1
  37.5 1.2 %copy-done.1 = bf16[2048,256]{1,0:T(8,128)(2,1)S(1)} copy-done((bf16[2048,256]{1,0:T(8,128)(2,1)S(1)}, bf16[2048,256]{1,0:T(8,128)(2,1)}, u32[]{:S(2)}) %copy-start.1) | copy-done | bytes 1048600
  38.7 4.4 %local_scatter.1.scat_ref = f32[2048,256]{1,0:T(8,128)S(1)} custom-call(s32[4,2048]{1,0:T(4,128)S(1)} %bitcast.9, bf16[2048,256]{1,0:T(8,128)(2,1)S(1)} %copy-done.1), custom_call_target="tpu_custom_call" | custom-call | flops 8589934592 | bytes 3145728 | tf_op jit(solution)/shard_map/local_scatter/pallas_call | solution.py:355
  43.2 12.1 %all-to-all-done.1.back_ref = bf16[32,72,128]{2,1,0:T(8,128)(2,1)S(1)} async-done(((bf16[32,72,128]{2,1,0:T(8,128)(2,1)}), bf16[32,72,128]{2,1,0:T(8,128)(2,1)S(1)}, u32[]{:S(2)}, u32[]{:S(2)}) %all-to-all-start.1) | async-done | bytes 589856 | tf_op jit(solution)/shard_map/all_to_all | solution.py:404
  55.3 0.7 weight_sums.1
  55.9 2.6 %all-to-all-start.2 = ((bf16[32,8,256]{2,1,0:T(8,128)(2,1)}), bf16[32,8,256]{2,1,0:T(8,128)(2,1)S(1)}, u32[]{:S(2)}, u32[]{:S(2)}) async-start(bf16[32,8,256]{2,1,0:T(8,128)(2,1)} %weight_sums.1), calls=%async_computation.2 | async-start | bytes 262144 | tf_op jit(solution)/shard_map/all_to_all | solution.py:404
  58.5 0.0 copy-start.2
  58.5 1.2 %copy-done.2 = bf16[2048,256]{1,0:T(8,128)(2,1)S(1)} copy-done((bf16[2048,256]{1,0:T(8,128)(2,1)S(1)}, bf16[2048,256]{1,0:T(8,128)(2,1)}, u32[]{:S(2)}) %copy-start.2) | copy-done | bytes 1048600
  59.8 3.6 %return_scatter.1 = f32[2048,256]{1,0:T(8,128)} custom-call(s32[1,512]{1,0:T(1,128)S(1)} %copy-done.4, bf16[32,72,128]{2,1,0:T(8,128)(2,1)S(1)} %all-to-all-done.1.back_ref, f32[2048,256]{1,0:T(8,128)S(1)} %local_scatter.1.scat_ref, bf16[2048,256]{1,0:T(8,128)(2,1)S(1)} %copy-done.2, bf16[256,256]{1,0:T(8,128)(2,1)S(1)} %copy-done.3, ...), custom_call_target="tpu_custom_call" | custom-call | flops 536870912 | bytes 5242880 | tf_op jit(solution)/shard_map/return_scatter/pallas_call | solution.py:355
  63.4 2.9 %all-to-all-done.2.near_ref = bf16[32,8,256]{2,1,0:T(8,128)(2,1)S(1)} async-done(((bf16[32,8,256]{2,1,0:T(8,128)(2,1)}), bf16[32,8,256]{2,1,0:T(8,128)(2,1)S(1)}, u32[]{:S(2)}, u32[]{:S(2)}) %all-to-all-start.2) | async-done | bytes 131104 | tf_op jit(solution)/shard_map/all_to_all | solution.py:404
  66.3 0.1 collective-permute-start.2
  66.4 0.8 %hub_sums.1 = (f32[1,256]{1,0:T(1,128)}, f32[16,256]{1,0:T(8,128)}) custom-call(bf16[32,72,128]{2,1,0:T(8,128)(2,1)S(1)} %all-to-all-done.1.back_ref, bf16[256,256]{1,0:T(8,128)(2,1)S(1)} %copy-done), custom_call_target="tpu_custom_call" | custom-call | bytes 1179648 | tf_op jit(solution)/shard_map/hub_sums/pallas_call | solution.py:355
  67.2 0.4 collective-permute-done.2.far_ref
  67.6 0.8 %weights.1 = (f32[256,256]{1,0:T(8,128)}, f32[256,256]{1,0:T(8,128)}) custom-call(s32[1]{0:T(128)} %bitcast.core_ref, bf16[32,8,256]{2,1,0:T(8,128)(2,1)S(1)} %all-to-all-done.2.near_ref, bf16[32,8,256]{2,1,0:T(8,128)(2,1)S(1)} %collective-permute-done.2.far_ref), custom_call_target="tpu_custom_call" | custom-call | bytes 786432 | tf_op jit(solution)/shard_map/weights/pallas_call | solution.py:355
  (12 shorter events, 0.0 us)
Async XLA Ops:
  0.6 10.1 %copy-start.8 = (s32[2048,4]{0,1:T(4,128)S(1)}, s32[2048,4]{0,1:T(4,128)}, u32[]{:S(2)}) copy-start(s32[2048,4]{0,1:T(4,128)} %param.17) | copy-start | bytes 98308
  0.6 10.1 %copy-start.10 = (s32[2048,2]{0,1:T(2,128)S(1)}, s32[2048,2]{0,1:T(2,128)}, u32[]{:S(2)}) copy-start(s32[2048,2]{0,1:T(2,128)} %param.16) | copy-start | bytes 49156
  0.7 10.1 %copy-start.9 = (s32[2048,4]{0,1:T(4,128)S(1)}, s32[2048,4]{0,1:T(4,128)}, u32[]{:S(2)}) copy-start(s32[2048,4]{0,1:T(4,128)} %param.15) | copy-start | bytes 98308
  3.4 20.8 %all-to-all-start = ((bf16[32,24,256]{2,1,0:T(8,128)(2,1)}), bf16[32,24,256]{2,1,0:T(8,128)(2,1)S(1)}, u32[]{:S(2)}, u32[]{:S(2)}) async-start(bf16[32,24,256]{2,1,0:T(8,128)(2,1)} %pick_rows.1), calls=%async_computation | async-start | bytes 786432 | tf_op jit(solution)/shard_map/all_to_all | solution.py:404
  10.8 1.2 %copy-start.6 = (bf16[2048,256]{1,0:T(8,128)(2,1)S(1)}, bf16[2048,256]{1,0:T(8,128)(2,1)}, u32[]{:S(2)}) copy-start(bf16[2048,256]{1,0:T(8,128)(2,1)} %own_ref) | copy-start | bytes 3145732
  12.0 1.2 %copy-start.7 = (bf16[2048,256]{1,0:T(8,128)(2,1)S(1)}, bf16[2048,256]{1,0:T(8,128)(2,1)}, u32[]{:S(2)}) copy-start(bf16[2048,256]{1,0:T(8,128)(2,1)} %cot_ref.1) | copy-start | bytes 3145732
  13.2 12.5 %copy-start = (bf16[256,256]{1,0:T(8,128)(2,1)S(1)}, bf16[256,256]{1,0:T(8,128)(2,1)}, u32[]{:S(2)}) copy-start(bf16[256,256]{1,0:T(8,128)(2,1)} %wn_ref.5) | copy-start | bytes 393220
  13.2 12.5 %copy-start.3 = (bf16[256,256]{1,0:T(8,128)(2,1)S(1)}, bf16[256,256]{1,0:T(8,128)(2,1)}, u32[]{:S(2)}) copy-start(bf16[256,256]{1,0:T(8,128)(2,1)} %ws_ref.3) | copy-start | bytes 393220
  13.2 12.5 %copy-start.5 = (f32[256]{0:T(256)S(1)}, f32[256]{0:T(256)}, u32[]{:S(2)}) copy-start(f32[256]{0:T(256)} %param.14) | copy-start | bytes 3076
  24.3 1.4 %collective-permute-start = (bf16[256,256]{1,0:T(8,128)(2,1)S(1)}, bf16[256,256]{1,0:T(8,128)(2,1)S(1)}, u32[]{:S(2)}, u32[]{:S(2)}) collective-permute-start(bf16[256,256]{1,0:T(8,128)(2,1)S(1)} %take_hubs.1.near_ref), channel_id=1, source_target_pairs={{0,8},{8,0},{16,24},{24,16},{1,9},{9,1},{17,25},{25,17},{2,10},{10... | collective-permute-start | bytes 393224 | tf_op jit(solution)/shard_map/ppermute | solution.py:401
  32.3 1.7 %collective-permute-start.1 = (bf16[32,40,128]{2,1,0:T(8,128)(2,1)S(1)}, bf16[32,40,128]{2,1,0:T(8,128)(2,1)S(1)}, u32[]{:S(2)}, u32[]{:S(2)}) collective-permute-start(bf16[32,40,128]{2,1,0:T(8,128)(2,1)S(1)} %get-tuple-element.36), channel_id=1, source_target_pairs={{0,8},{8,0},{16,24},{24,16},{1,9},{9,1},{17,25},{25,17},{2,10},{10... | collective-permute-start | bytes 983048 | tf_op jit(solution)/shard_map/ppermute | solution.py:401
  34.9 20.4 %all-to-all-start.1 = ((bf16[32,72,128]{2,1,0:T(8,128)(2,1)}), bf16[32,72,128]{2,1,0:T(8,128)(2,1)S(1)}, u32[]{:S(2)}, u32[]{:S(2)}) async-start(bf16[32,72,128]{2,1,0:T(8,128)(2,1)} %join_siblings.1), calls=%async_computation.1 | async-start | bytes 1179648 | tf_op jit(solution)/shard_map/all_to_all | solution.py:404
  37.5 1.2 %copy-start.1 = (bf16[2048,256]{1,0:T(8,128)(2,1)S(1)}, bf16[2048,256]{1,0:T(8,128)(2,1)}, u32[]{:S(2)}) copy-start(bf16[2048,256]{1,0:T(8,128)(2,1)} %get-tuple-element.37.grad_ref) | copy-start | bytes 3145732
  38.7 19.8 %copy-start.4 = (s32[1,512]{1,0:T(1,128)S(1)}, s32[1,512]{1,0:T(1,128)}, u32[]{:S(2)}) copy-start(s32[1,512]{1,0:T(1,128)} %send_ref.3) | copy-start | bytes 6148
  55.9 10.3 %all-to-all-start.2 = ((bf16[32,8,256]{2,1,0:T(8,128)(2,1)}), bf16[32,8,256]{2,1,0:T(8,128)(2,1)S(1)}, u32[]{:S(2)}, u32[]{:S(2)}) async-start(bf16[32,8,256]{2,1,0:T(8,128)(2,1)} %weight_sums.1), calls=%async_computation.2 | async-start | bytes 262144 | tf_op jit(solution)/shard_map/all_to_all | solution.py:404
  58.5 1.2 %copy-start.2 = (bf16[2048,256]{1,0:T(8,128)(2,1)S(1)}, bf16[2048,256]{1,0:T(8,128)(2,1)}, u32[]{:S(2)}) copy-start(bf16[2048,256]{1,0:T(8,128)(2,1)} %get-tuple-element.37.grad_ref) | copy-start | bytes 3145732
  66.3 1.3 %collective-permute-start.2 = (bf16[32,8,256]{2,1,0:T(8,128)(2,1)S(1)}, bf16[32,8,256]{2,1,0:T(8,128)(2,1)S(1)}, u32[]{:S(2)}, u32[]{:S(2)}) collective-permute-start(bf16[32,8,256]{2,1,0:T(8,128)(2,1)S(1)} %all-to-all-done.2.near_ref), channel_id=1, source_target_pairs={{0,8},{8,0},{16,24},{24,16},{1,9},{9,1},{17,25},{25,17},{2,10},{10... | collective-permute-start | bytes 393224 | tf_op jit(solution)/shard_map/ppermute | solution.py:401

commit v9 on v8

--- a/solution.py
+++ b/solution.py
@@ -225,34 +225,32 @@
     own = jnp.where(first_core, weights[:, :half], weights[:, half:])
     other = jnp.where(first_core, weights[:, half:], weights[:, :half])
     count = step // hub_rows
+    tall = pieces * hub_rows
+
+    def flat(value):
+        return jnp.concatenate([value[:, :, lanes(piece)] for piece in range(pieces)], axis=1).reshape(-1, LANES)
+
     for low in range(0, parts, count):
         if low > 0:
             own = other = jnp.zeros_like(own)
         first = step + bounds + low * half
         keep = jnp.concatenate([term_rows(first, count * half, half), own], axis=1)
-        give = jnp.concatenate([term_rows(first + hubs // 2, count * half, half), other], axis=1).astype(bf16)
-        at = slice(low, low + count)
-        for piece in range(pieces):
-            there = slice(piece * hub_rows, (piece + 1) * hub_rows)
-            keep_ref[at, there, :] = keep[:, :, lanes(piece)]
-            give_ref[at, there, :] = give[:, :, lanes(piece)]
+        give = jnp.concatenate([term_rows(first + hubs // 2, count * half, half), other], axis=1)
+        keep_ref[low * tall : (low + count) * tall, :] = flat(keep)
+        give_ref[low * tall : (low + count) * tall, :] = flat(give).astype(bf16)
     bias_total = dot(jnp.ones((16, nodes), bf16), grad_all[...])[:1]
     rows = bias_rows([bias_total[:, lanes(piece)] for piece in range(pieces)])
-    keep_ref[:, pieces * hub_rows :, :] = jnp.broadcast_to(rows[None], (parts, 8, LANES))
-    give_ref[:, pieces * hub_rows :, :] = jnp.broadcast_to(rows.astype(bf16)[None], (parts, 8, LANES))
+    keep_ref[parts * tall :, :] = rows
+    give_ref[parts * tall :, :] = rows.astype(bf16)
     for low in range(0, bounds, step):
-        bound_terms = term_rows(step + low, step, slots).astype(bf16)
-        for piece in range(pieces):
-            bound_ref[low // slots : (low + step) // slots, piece * slots : (piece + 1) * slots, :] = (
-                bound_terms[:, :, lanes(piece)]
-            )
+        bound_ref[low // slots : (low + step) // slots] = term_rows(step + low, step, slots).astype(bf16)
     for store in stores:
         store.wait()
 
 
 def bias_rows(parts):
-    line = lax.broadcasted_iota(jnp.int32, (8, LANES), 0)
-    rows = jnp.zeros((8, LANES), f32)
+    line = lax.broadcasted_iota(jnp.int32, (16, LANES), 0)
+    rows = jnp.zeros((16, LANES), f32)
     for piece, value in enumerate(parts):
         high = value.astype(bf16).astype(f32)
         rows = jnp.where(line == piece, high, rows)
@@ -260,61 +258,64 @@
     return rows
 
 
-def join_kernel(bound_ref, keep_ref, got_ref, out_ref):
-    parts, tall, _ = keep_ref.shape
-    place = bound_ref.shape[1]
-    pieces = (tall - 8) // 16
-    out_ref[:, :place, :] = bound_ref[...]
-    both = keep_ref[:, : tall - 8, :] + got_ref[:, : tall - 8, :].astype(f32)
-    out_ref[:, place : place + tall - 8, :] = both.astype(bf16)
-    tail = keep_ref[0, tall - 8 :, :] + got_ref[0, tall - 8 :, :].astype(f32)
-    rows = bias_rows([tail[piece : piece + 1] + tail[pieces + piece : pieces + piece + 1] for piece in range(pieces)])
-    out_ref[:, place + tall - 8 :, :] = jnp.broadcast_to(rows.astype(bf16)[None], (parts, 8, LANES))
-
-
-def chip_sums(slots, hub_rows, rows, back_ref):
-    parts, tall, _ = back_ref.shape
-    pieces = (tall - 8) // (slots + hub_rows)
-    whole = back_ref[:, pieces * slots :, :].astype(f32)
-    count = whole.shape[1]
-    whole = whole.reshape(rows // 2, 2, parts // rows, count, LANES)
-    return jnp.sum(jnp.sum(whole, axis=2), axis=0), pieces
-
-
-def both_halves(total, pieces, hub_rows, first):
+def bias_pieces(tail, pieces):
+    return [tail[piece : piece + 1] + tail[pieces + piece : pieces + piece + 1] for piece in range(pieces)]
+
+
+def halve_kernel(before, tall, pieces, bit_ref, keep_ref, got_ref, keep_out, give_out):
+    both = keep_ref[...] + got_ref[...].astype(f32)
+    count = both.shape[0] - 16
+    body = both[:count].reshape(before, 2, count // (2 * before * tall) * tall, LANES)
+    low_side = bit_ref[0] == 0
+    mine = jnp.where(low_side, body[:, 0], body[:, 1]).reshape(count // 2, LANES)
+    other = jnp.where(low_side, body[:, 1], body[:, 0]).reshape(count // 2, LANES)
+    rows = bias_rows(bias_pieces(both[count:], pieces))
+    keep_out[: count // 2, :] = mine
+    keep_out[count // 2 :, :] = rows
+    give_out[: count // 2, :] = other.astype(bf16)
+    give_out[count // 2 :, :] = rows.astype(bf16)
+
+
+def last_kernel(rows, hub_rows, pieces, core_ref, keep_ref, got_ref, weight_ref, keep_out, give_out, bias_ref):
     half = hub_rows // 2
-    columns = []
-    for piece in range(pieces):
-        place = piece * hub_rows + first
-        columns.append(jnp.concatenate([total[0, place : place + half], total[1, place : place + half]], axis=0))
-    return jnp.concatenate(columns, axis=1)
-
-
-def weight_sum_kernel(slots, hub_rows, rows, back_ref, out_ref):
-    total, pieces = chip_sums(slots, hub_rows, rows, back_ref)
-    weight = both_halves(total, pieces, hub_rows, hub_rows // 2)
-    out_ref[...] = by_core(weight.astype(bf16), rows, out_ref.shape[0] // rows)
-
-
-def other_sums_kernel(scale, slots, hub_rows, rows, back_ref, wn_ref, bias_ref, hub_ref):
-    total, pieces = chip_sums(slots, hub_rows, rows, back_ref)
-    tail = 0.5 * (total[0, pieces * hub_rows :] + total[1, pieces * hub_rows :])
-    bias_ref[...] = jnp.concatenate(
-        [tail[piece : piece + 1] + tail[pieces + piece : pieces + piece + 1] for piece in range(pieces)], axis=1
-    )
-    hub = both_halves(total, pieces, hub_rows, 0)
+    both = keep_ref[...] + got_ref[...].astype(f32)
+    count = both.shape[0] - 16
+    body = both[:count].reshape(2, pieces * hub_rows, LANES)
+
+    def table(core, first):
+        return jnp.concatenate(
+            [body[core, piece * hub_rows + first : piece * hub_rows + first + half] for piece in range(pieces)], axis=1
+        )
+
+    weight = jnp.concatenate([table(0, half), table(1, half)], axis=0)
+    weight_ref[...] = by_core(weight.astype(bf16), rows, weight_ref.shape[0] // rows)
+    first_core = core_ref[0] == 0
+    keep_out[...] = jnp.where(first_core, table(0, 0), table(1, 0))
+    give_out[...] = jnp.where(first_core, table(1, 0), table(0, 0))
+    bias_ref[...] = jnp.concatenate(bias_pieces(both[count:], pieces), axis=1)
+
+
+def hub_kernel(scale, core_ref, keep_ref, got_ref, wn_ref, hub_ref):
+    first_core = core_ref[0] == 0
+    keep, got = keep_ref[...], got_ref[...]
+    hub = jnp.concatenate([jnp.where(first_core, keep, got), jnp.where(first_core, got, keep)], axis=0)
     high = hub.astype(bf16)
     low = (hub - high.astype(f32)).astype(bf16)
     hub_ref[...] = (dot(high, wn_ref[...], NT) + dot(low, wn_ref[...], NT)) * scale
 
 
-def weights_kernel(core_ref, near_ref, far_ref, self_ref, neigh_ref):
+def weights_kernel(rows, core_ref, near_ref, far_ref, self_ref, neigh_ref):
     width = self_ref.shape[0]
-    count = 2 * width // 16
-    near, far = near_ref[:count].astype(f32), far_ref[:count].astype(f32)
+    parts = near_ref.shape[0]
+    cols = parts // rows
+    near, far = near_ref[...].astype(f32), far_ref[...].astype(f32)
     first_core = core_ref[0] == 0
-    whole = jnp.concatenate([jnp.where(first_core, near, far), jnp.where(first_core, far, near)], axis=1)
-    whole = whole.reshape(2 * width, width)
+    holders = (jnp.where(first_core, near, far), jnp.where(first_core, far, near))
+    blocks = []
+    for row in range(rows):
+        held, pair = holders[row % 2], row // 2 * 2 * cols
+        blocks.append(jnp.concatenate([held[pair : pair + cols], held[pair + cols : pair + 2 * cols]], axis=1))
+    whole = jnp.concatenate(blocks, axis=0)[: 2 * width // 16].reshape(2 * width, width)
     self_ref[...] = whole[:width]
     neigh_ref[...] = whole[width:]
 
@@ -334,13 +335,7 @@
     height, width = out_ref.shape
     first = pl.program_id(0) * height
     count = send_ref.shape[1]
-    returned = jnp.concatenate(
-        [
-            back_ref[:, piece * slots : (piece + 1) * slots, :].reshape(count, LANES)
-            for piece in range(width // LANES)
-        ],
-        axis=1,
-    )
+    returned = back_ref[...].reshape(count, width)
     total = scat_ref[...]
     for start in range(0, count, 512):
         stop = min(count, start + 512)
@@ -363,6 +358,14 @@
         cost_estimate=cost(flops, moved),
         name=name,
     )(*ins)
+
+
+def powers(low, high):
+    found = []
+    while low < high:
+        found.append(low)
+        low *= 2
+    return found
 
 
 def whole_block(shape):
@@ -387,7 +390,7 @@
     slots = send_rows.shape[1] // parts
     slab = slots + hub_rows
     pieces = width // LANES
-    pay = pieces * slab + 8
+    tall = pieces * hub_rows
     core = (lax.axis_index("row") % 2).astype(jnp.int32).reshape(1)
     rows = lax.axis_size("row")
     half = hub_rows // 2
@@ -452,9 +455,9 @@
         [SMEM] + [VMEM] * 7 + [HBM],
         [pltpu.HBM((nodes, width), bf16)] * 2
         + [
-            shape((parts, pieces * slots, LANES), bf16),
-            shape((parts, pieces * hub_rows + 8, LANES), f32),
-            shape((parts, pieces * hub_rows + 8, LANES), bf16),
+            shape((parts, slots, width), bf16),
+            shape((parts * tall + 16, LANES), f32),
+            shape((parts * tall + 16, LANES), bf16),
         ],
         [HBM] * 2 + [VMEM] * 3,
         "activate",
@@ -471,17 +474,7 @@
         moved=nodes * packed * 2,
     )
     got = sibling(give)
-    back = exchange(
-        call(
-            join_kernel,
-            [bound_terms, keep, got],
-            [VMEM] * 3,
-            shape((parts, pay, LANES), bf16),
-            VMEM,
-            "join_siblings",
-            moved=parts * pay * LANES * 6,
-        )
-    )
+    back = exchange(bound_terms)
 
     scattered = call(
         scatter_kernel,
@@ -494,25 +487,48 @@
         flops=8 * nodes * nodes * width,
         moved=nodes * width * 6,
     )
-    back, scattered = lax.optimization_barrier((back, scattered))
-    weight_rows = call(
-        functools.partial(weight_sum_kernel, slots, hub_rows, rows),
-        (back,),
-        [VMEM],
-        shape((parts, 8, width), bf16),
+    cols = parts // rows
+    bits = [("row", bit) for bit in powers(2, rows)[::-1]] + [("col", bit) for bit in powers(1, cols)]
+    count = parts
+    for stage, (axis, bit) in enumerate(bits):
+        before = 1 if axis == "row" else 2 * (cols // (2 * bit))
+        side = (lax.axis_index(axis) // bit % 2).astype(jnp.int32).reshape(1)
+        count //= 2
+        keep, give = call(
+            functools.partial(halve_kernel, before, tall, pieces),
+            [side, keep, got],
+            [SMEM, VMEM, VMEM],
+            [shape((count * tall + 16, LANES), f32), shape((count * tall + 16, LANES), bf16)],
+            [VMEM, VMEM],
+            "halve",
+            moved=count * tall * LANES * 8,
+        )
+        got = lax.ppermute(give, axis, [(i, i ^ bit) for i in range(lax.axis_size(axis))])
+        if stage == 0:
+            got, scattered = lax.optimization_barrier((got, scattered))
+    weight_rows, hub_keep, hub_give, grad_bias = call(
+        functools.partial(last_kernel, rows, hub_rows, pieces),
+        [core, keep, got],
+        [SMEM, VMEM, VMEM],
+        [
+            shape((parts, 8, width), bf16),
+            shape((half, width), f32),
+            shape((half, width), f32),
+            shape((1, width), f32),
+        ],
+        [VMEM] * 4,
+        "weight_sums",
+        moved=parts * 8 * width * 2,
+    )
+    near_weights = exchange(weight_rows)
+    grad_hubs = call(
+        functools.partial(hub_kernel, scale),
+        [core, hub_keep, sibling(hub_give), w_neigh],
+        [SMEM, VMEM, VMEM, VMEM],
+        shape((hub_rows, width), f32),
         VMEM,
-        "weight_sums",
-        moved=parts * pay * width * 2,
-    )
-    near_weights = exchange(weight_rows)
-    grad_bias, grad_hubs = call(
-        functools.partial(other_sums_kernel, scale, slots, hub_rows, rows),
-        (back, w_neigh),
-        [VMEM, VMEM],
-        [shape((1, width), f32), shape((hub_rows, width), f32)],
-        [whole_block((1, width)), whole_block((hub_rows, width))],
         "hub_sums",
-        moved=parts * pay * width * 2,
+        moved=width * width * 2,
     )
 
     height = 2 * TILE
@@ -520,7 +536,7 @@
     grad_features = call(
         functools.partial(final_kernel, scale, slots),
         (send_rows, back, scattered, grad_pre, w_self, w_neigh),
-        [whole_block(send_rows.shape), whole_block((parts, pay, LANES)), by_height, by_height]
+        [whole_block(send_rows.shape), whole_block((parts, slots, width)), by_height, by_height]
         + [whole_block((width, width))] * 2,
         shape((nodes, width), f32),
         by_height,
@@ -531,7 +547,7 @@
     )
     near_weights, grad_features = lax.optimization_barrier((near_weights, grad_features))
     grad_w_self, grad_w_neigh = call(
-        weights_kernel,
+        functools.partial(weights_kernel, rows),
         [core, near_weights, sibling(near_weights)],
         [SMEM, VMEM, VMEM],
         [shape((width, width), f32)] * 2,

time: 68.9 us -> 74.4 us (1.080)
  starting transfers between devices: 12.9 us -> 23.5 us
  waiting for transfers between devices: 22.1 us -> 16.1 us
  local copies, waits for them, and re-layouts: 4.91 us -> 5.68 us
    all_to_all x3, waiting for transfers between devices: 18.8 us -> 6.67 us  [exchange(): return lax.all_to_all(value, AXES, split_axis=0, concat_axis=0, tiled=True)]
    ppermute x0 -> x4, starting transfers between devices: none -> 7.62 us  [body(): lax.ppermute(give, axis, [(i, i ^ bit) for i in range(lax.axis_size(axis))])]
    ppermute x0 -> x4, waiting for transfers between devices: none -> 7.24 us  [body(): lax.ppermute(give, axis, [(i, i ^ bit) for i in range(lax.axis_size(axis))])]
    all_to_all x3, starting transfers between devices: 12.5 us -> 15.1 us  [exchange(): return lax.all_to_all(value, AXES, split_axis=0, concat_axis=0, tiled=True)]
    ppermute x3 -> x4, waiting for transfers between devices: 3.27 us -> 2.19 us  [sibling(): return lax.ppermute(value, 'row', [(r, r ^ 1) for r in range(rows)])]
    unnamed x22 -> x24, local copies, waits for them, and re-layouts: 4.91 us -> 5.68 us
    pallas_call x10 -> x13, Pallas kernels: 27.8 us -> 27.8 us  [call(): pl.pallas_call(kernel, grid=grid, in_specs=in_specs, out_specs=out_specs,...]
  transfers between devices with their start and end apart: 6 -> 11, of which waited for: 6 -> 7; matrix products, arithmetic and copies ran while one was open for 0% -> 0% of each run, Pallas kernels for 23% -> 23%
where the time goes in v9:
time: 74.4 us; the launch traced here: 73.8 us
  Pallas kernels  27.8 us (37%)
  starting transfers between devices  23.5 us (32%)
  waiting for transfers between devices  16.1 us (22%)
  local copies, waits for them, and re-layouts  5.68 us (8%)
  between operations  0.82 us (1%)
    pallas_call x13, Pallas kernels, call(): pl.pallas_call(kernel, grid=grid, in_specs=in_specs, out_specs=out_specs,...  27.8 us
    all_to_all x3, starting transfers between devices, exchange(): return lax.all_to_all(value, AXES, split_axis=0, concat_axis=0, tiled=True)  15.1 us
    ppermute x4, starting transfers between devices, body(): lax.ppermute(give, axis, [(i, i ^ bit) for i in range(lax.axis_size(axis))])  7.62 us
    ppermute x4, waiting for transfers between devices, body(): lax.ppermute(give, axis, [(i, i ^ bit) for i in range(lax.axis_size(axis))])  7.24 us
    all_to_all x3, waiting for transfers between devices, exchange(): return lax.all_to_all(value, AXES, split_axis=0, concat_axis=0, tiled=True)  6.67 us
    unnamed x24, local copies, waits for them, and re-layouts  5.68 us
    ppermute x4, waiting for transfers between devices, sibling(): return lax.ppermute(value, 'row', [(r, r ^ 1) for r in range(rows)])  2.19 us
  transfers between devices with their start and end apart: 11, of which 7 were waited for; matrix products, arithmetic and copies ran while one was open for 0% of the time, Pallas kernels for 23%

profile of v9, /device:TPU:0, one launch (start us, length us, event | category | flops | bytes accessed | tf_op | source)
XLA Modules:
  0.0 73.8 jit_solution(13214920775123862628)
XLA Ops:
  0.7 2.7 %pick_rows.1 = bf16[32,24,256]{2,1,0:T(8,128)(2,1)} custom-call(s32[1,512]{1,0:T(1,128)} %send_ref.3, bf16[2048,256]{1,0:T(8,128)(2,1)} %own_ref, bf16[16,256]{1,0:T(8,128)(2,1)} %hub_ref.1), custom_call_target="tpu_custom_call" | custom-call | flops 536870912 | bytes 1048576 | tf_op jit(solution)/shard_map/pick_rows/pallas_call | solution.py:350
  3.4 7.3 %all-to-all-start = ((bf16[32,24,256]{2,1,0:T(8,128)(2,1)}), bf16[32,24,256]{2,1,0:T(8,128)(2,1)S(1)}, u32[]{:S(2)}, u32[]{:S(2)}) async-start(bf16[32,24,256]{2,1,0:T(8,128)(2,1)} %pick_rows.1), calls=%async_computation | async-start | bytes 786432 | tf_op jit(solution)/shard_map/all_to_all | solution.py:407
  10.8 1.2 %copy-done.6 = bf16[2048,256]{1,0:T(8,128)(2,1)S(1)} copy-done((bf16[2048,256]{1,0:T(8,128)(2,1)S(1)}, bf16[2048,256]{1,0:T(8,128)(2,1)}, u32[]{:S(2)}) %copy-start.6) | copy-done | bytes 1048600
  12.0 1.2 %copy-done.7 = bf16[2048,256]{1,0:T(8,128)(2,1)S(1)} copy-done((bf16[2048,256]{1,0:T(8,128)(2,1)S(1)}, bf16[2048,256]{1,0:T(8,128)(2,1)}, u32[]{:S(2)}) %copy-start.7) | copy-done | bytes 1048600
  13.2 7.2 %local_gather.1 = (f32[2048,256]{1,0:T(8,128)S(1)}, bf16[2048,1536]{1,0:T(8,128)(2,1)}) custom-call(s32[1]{0:T(128)} %bitcast.core_ref, s32[4,2048]{1,0:T(4,128)S(1)} %bitcast.12, s32[4,2048]{1,0:T(4,128)S(1)} %bitcast.11, s32[2,2048]{1,0:T(2,128)S(1)} %bitcast.14, bf16[2048,256]{1,0:T(8,128)(2,1)S(1)} %copy-done.6, bf16[2048,256]{1,0:T(8,128)(2,1)S(1)} %copy-done.6, ...), custom_call_target="tpu_custom_call" | custom-call | flops 8589934592 | bytes 6291456 | tf_op jit(solution)/shard_map/local_gather/pallas_call | solution.py:350
  20.5 3.8 %all-to-all-done.table_ref = bf16[32,24,256]{2,1,0:T(8,128)(2,1)S(1)} async-done(((bf16[32,24,256]{2,1,0:T(8,128)(2,1)}), bf16[32,24,256]{2,1,0:T(8,128)(2,1)S(1)}, u32[]{:S(2)}, u32[]{:S(2)}) %all-to-all-start) | async-done | bytes 393248 | tf_op jit(solution)/shard_map/all_to_all | solution.py:407
  24.3 0.1 collective-permute-start
  24.3 1.3 %collective-permute-done.far_ref = bf16[256,256]{1,0:T(8,128)(2,1)S(1)} collective-permute-done((bf16[256,256]{1,0:T(8,128)(2,1)S(1)}, bf16[256,256]{1,0:T(8,128)(2,1)S(1)}, u32[]{:S(2)}, u32[]{:S(2)}) %collective-permute-start) | collective-permute-done | bytes 131104 | tf_op jit(solution)/shard_map/ppermute | solution.py:404
  25.7 7.3 %activate.1 = (bf16[2048,256]{1,0:T(8,128)(2,1)}, bf16[2048,256]{1,0:T(8,128)(2,1)}, bf16[32,16,256]{2,1,0:T(8,128)(2,1)}, f32[1040,128]{1,0:T(8,128)S(1)}, bf16[1040,128]{1,0:T(8,128)(2,1)S(1)}) custom-call(s32[1]{0:T(128)} %bitcast.core_ref, bf16[32,24,256]{2,1,0:T(8,128)(2,1)S(1)} %all-to-all-done.table_ref, bf16[256,256]{1,0:T(8,128)(2,1)S(1)} %take_hubs.1.near_ref, ...), custom_call_target="tpu_custom_call" | custom-call | flops 2147483648 | bytes 6291456 | tf_op jit(solution)/shard_map/activate/pallas_call | solution.py:350
  33.0 0.2 collective-permute-start.1
  33.2 2.6 %all-to-all-start.2 = ((bf16[32,16,256]{2,1,0:T(8,128)(2,1)}), bf16[32,16,256]{2,1,0:T(8,128)(2,1)S(1)}, u32[]{:S(2)}, u32[]{:S(2)}) async-start(bf16[32,16,256]{2,1,0:T(8,128)(2,1)} %get-tuple-element.57), calls=%async_computation.2 | async-start | bytes 524288 | tf_op jit(solution)/shard_map/all_to_all | solution.py:407
  35.8 0.1 halve.4
  35.9 1.7 %collective-permute-start.2 = (bf16[528,128]{1,0:T(8,128)(2,1)S(1)}, bf16[528,128]{1,0:T(8,128)(2,1)S(1)}, u32[]{:S(2)}, u32[]{:S(2)}) collective-permute-start(bf16[528,128]{1,0:T(8,128)(2,1)S(1)} %get-tuple-element.47), channel_id=1, source_target_pairs={{0,16},{8,24},{16,0},{24,8},{1,17},{9,25},{17,1},{25,9},{2,18},{10... | collective-permute-start | bytes 405512 | tf_op jit(solution)/shard_map/ppermute | solution.py:506
  37.6 1.2 %copy-done.1 = bf16[2048,256]{1,0:T(8,128)(2,1)S(1)} copy-done((bf16[2048,256]{1,0:T(8,128)(2,1)S(1)}, bf16[2048,256]{1,0:T(8,128)(2,1)}, u32[]{:S(2)}) %copy-start.1) | copy-done | bytes 1048600
  38.8 0.8 %copy-done.10 = s32[2048,4]{0,1:T(4,128)S(1)} copy-done((s32[2048,4]{0,1:T(4,128)S(1)}, s32[2048,4]{0,1:T(4,128)}, u32[]{:S(2)}) %copy-start.10) | copy-done | bytes 32792
  39.6 4.4 %local_scatter.1.scat_ref = f32[2048,256]{1,0:T(8,128)S(1)} custom-call(s32[4,2048]{1,0:T(4,128)S(1)} %bitcast.13, bf16[2048,256]{1,0:T(8,128)(2,1)S(1)} %copy-done.1), custom_call_target="tpu_custom_call" | custom-call | flops 8589934592 | bytes 3145728 | tf_op jit(solution)/shard_map/local_scatter/pallas_call | solution.py:350
  44.1 1.5 %collective-permute-start.3 = (bf16[272,128]{1,0:T(8,128)(2,1)S(1)}, bf16[272,128]{1,0:T(8,128)(2,1)S(1)}, u32[]{:S(2)}, u32[]{:S(2)}) collective-permute-start(bf16[272,128]{1,0:T(8,128)(2,1)S(1)} %get-tuple-element.51), channel_id=1, source_target_pairs={{0,1},{1,0},{2,3},{3,2},{4,5},{5,4},{6,7},{7,6},{8,9},{9,8},{10,11... | collective-permute-start | bytes 208904 | tf_op jit(solution)/shard_map/ppermute | solution.py:506
  45.6 2.8 %collective-permute-done.3.got_ref = bf16[272,128]{1,0:T(8,128)(2,1)S(1)} collective-permute-done((bf16[272,128]{1,0:T(8,128)(2,1)S(1)}, bf16[272,128]{1,0:T(8,128)(2,1)S(1)}, u32[]{:S(2)}, u32[]{:S(2)}) %collective-permute-start.3) | collective-permute-done | bytes 69664 | tf_op jit(solution)/shard_map/ppermute | solution.py:506
  48.5 1.6 %collective-permute-start.4 = (bf16[144,128]{1,0:T(8,128)(2,1)S(1)}, bf16[144,128]{1,0:T(8,128)(2,1)S(1)}, u32[]{:S(2)}, u32[]{:S(2)}) collective-permute-start(bf16[144,128]{1,0:T(8,128)(2,1)S(1)} %get-tuple-element.53), channel_id=1, source_target_pairs={{0,2},{1,3},{2,0},{3,1},{4,6},{5,7},{6,4},{7,5},{8,10},{9,11},{10,... | collective-permute-start | bytes 110600 | tf_op jit(solution)/shard_map/ppermute | solution.py:506
  50.1 2.4 %collective-permute-done.4.got_ref = bf16[144,128]{1,0:T(8,128)(2,1)S(1)} collective-permute-done((bf16[144,128]{1,0:T(8,128)(2,1)S(1)}, bf16[144,128]{1,0:T(8,128)(2,1)S(1)}, u32[]{:S(2)}, u32[]{:S(2)}) %collective-permute-start.4) | collective-permute-done | bytes 36896 | tf_op jit(solution)/shard_map/ppermute | solution.py:506
  52.5 2.7 %collective-permute-start.5 = (bf16[80,128]{1,0:T(8,128)(2,1)S(1)}, bf16[80,128]{1,0:T(8,128)(2,1)S(1)}, u32[]{:S(2)}, u32[]{:S(2)}) collective-permute-start(bf16[80,128]{1,0:T(8,128)(2,1)S(1)} %get-tuple-element.55), channel_id=1, source_target_pairs={{0,4},{1,5},{2,6},{3,7},{4,0},{5,1},{6,2},{7,3},{8,12},{9,13},{10,... | collective-permute-start | bytes 61448 | tf_op jit(solution)/shard_map/ppermute | solution.py:506
  55.3 2.0 %collective-permute-done.5.got_ref = bf16[80,128]{1,0:T(8,128)(2,1)S(1)} collective-permute-done((bf16[80,128]{1,0:T(8,128)(2,1)S(1)}, bf16[80,128]{1,0:T(8,128)(2,1)S(1)}, u32[]{:S(2)}, u32[]{:S(2)}) %collective-permute-start.5) | collective-permute-done | bytes 20512 | tf_op jit(solution)/shard_map/ppermute | solution.py:506
  57.3 0.7 weight_sums.1
  57.9 5.2 %all-to-all-start.1 = ((bf16[32,8,256]{2,1,0:T(8,128)(2,1)}), bf16[32,8,256]{2,1,0:T(8,128)(2,1)S(1)}, u32[]{:S(2)}, u32[]{:S(2)}) async-start(bf16[32,8,256]{2,1,0:T(8,128)(2,1)} %get-tuple-element.56), calls=%async_computation.1 | async-start | bytes 262144 | tf_op jit(solution)/shard_map/all_to_all | solution.py:407
  63.2 1.2 %copy-done.2 = bf16[2048,256]{1,0:T(8,128)(2,1)S(1)} copy-done((bf16[2048,256]{1,0:T(8,128)(2,1)S(1)}, bf16[2048,256]{1,0:T(8,128)(2,1)}, u32[]{:S(2)}) %copy-start.2) | copy-done | bytes 1048600
  64.4 3.6 %return_scatter.1 = f32[2048,256]{1,0:T(8,128)} custom-call(s32[1,512]{1,0:T(1,128)S(1)} %copy-done.4, bf16[32,16,256]{2,1,0:T(8,128)(2,1)S(1)} %all-to-all-done.2.back_ref, f32[2048,256]{1,0:T(8,128)S(1)} %local_scatter.1.scat_ref, bf16[2048,256]{1,0:T(8,128)(2,1)S(1)} %copy-done.2, bf16[256,256]{1,0:T(8,128)(2,1)S(1)} %copy-done.3, ...), custom_call_target="tpu_custom_call" | custom-call | flops 536870912 | bytes 5242880 | tf_op jit(solution)/shard_map/return_scatter/pallas_call | solution.py:350
  68.0 2.9 %all-to-all-done.1.near_ref = bf16[32,8,256]{2,1,0:T(8,128)(2,1)S(1)} async-done(((bf16[32,8,256]{2,1,0:T(8,128)(2,1)}), bf16[32,8,256]{2,1,0:T(8,128)(2,1)S(1)}, u32[]{:S(2)}, u32[]{:S(2)}) %all-to-all-start.1) | async-done | bytes 131104 | tf_op jit(solution)/shard_map/all_to_all | solution.py:407
  70.9 0.1 collective-permute-start.7
  71.0 0.4 collective-permute-start.6
  71.4 0.8 %collective-permute-done.6.got_ref = f32[8,256]{1,0:T(8,128)S(1)} collective-permute-done((f32[8,256]{1,0:T(8,128)S(1)}, f32[8,256]{1,0:T(8,128)S(1)}, u32[]{:S(2)}, u32[]{:S(2)}) %collective-permute-start.6) | collective-permute-done | bytes 8224 | tf_op jit(solution)/shard_map/ppermute | solution.py:404
  72.2 0.8 %hub_sums.1 = f32[16,256]{1,0:T(8,128)} custom-call(s32[1]{0:T(128)} %bitcast.core_ref, f32[8,256]{1,0:T(8,128)S(1)} %get-tuple-element.60.keep_ref, f32[8,256]{1,0:T(8,128)S(1)} %collective-permute-done.6.got_ref, bf16[256,256]{1,0:T(8,128)(2,1)S(1)} %copy-done), custom_call_target="tpu_custom_call" | custom-call | bytes 131072 | tf_op jit(solution)/shard_map/hub_sums/pallas_call | solution.py:350
  73.0 0.8 %weights.1 = (f32[256,256]{1,0:T(8,128)}, f32[256,256]{1,0:T(8,128)}) custom-call(s32[1]{0:T(128)} %bitcast.core_ref, bf16[32,8,256]{2,1,0:T(8,128)(2,1)S(1)} %all-to-all-done.1.near_ref, bf16[32,8,256]{2,1,0:T(8,128)(2,1)S(1)} %collective-permute-done.7.far_ref), custom_call_target="tpu_custom_call" | custom-call | bytes 786432 | tf_op jit(solution)/shard_map/weights/pallas_call | solution.py:350
  (27 shorter events, 0.2 us)
Async XLA Ops:
  0.6 10.1 %copy-start.8 = (s32[2048,4]{0,1:T(4,128)S(1)}, s32[2048,4]{0,1:T(4,128)}, u32[]{:S(2)}) copy-start(s32[2048,4]{0,1:T(4,128)} %param.17) | copy-start | bytes 98308
  0.6 10.1 %copy-start.11 = (s32[2048,2]{0,1:T(2,128)S(1)}, s32[2048,2]{0,1:T(2,128)}, u32[]{:S(2)}) copy-start(s32[2048,2]{0,1:T(2,128)} %param.16) | copy-start | bytes 49156
  0.7 10.1 %copy-start.9 = (s32[2048,4]{0,1:T(4,128)S(1)}, s32[2048,4]{0,1:T(4,128)}, u32[]{:S(2)}) copy-start(s32[2048,4]{0,1:T(4,128)} %param.15) | copy-start | bytes 98308
  3.4 20.8 %all-to-all-start = ((bf16[32,24,256]{2,1,0:T(8,128)(2,1)}), bf16[32,24,256]{2,1,0:T(8,128)(2,1)S(1)}, u32[]{:S(2)}, u32[]{:S(2)}) async-start(bf16[32,24,256]{2,1,0:T(8,128)(2,1)} %pick_rows.1), calls=%async_computation | async-start | bytes 786432 | tf_op jit(solution)/shard_map/all_to_all | solution.py:407
  10.8 1.2 %copy-start.6 = (bf16[2048,256]{1,0:T(8,128)(2,1)S(1)}, bf16[2048,256]{1,0:T(8,128)(2,1)}, u32[]{:S(2)}) copy-start(bf16[2048,256]{1,0:T(8,128)(2,1)} %own_ref) | copy-start | bytes 3145732
  12.0 1.2 %copy-start.7 = (bf16[2048,256]{1,0:T(8,128)(2,1)S(1)}, bf16[2048,256]{1,0:T(8,128)(2,1)}, u32[]{:S(2)}) copy-start(bf16[2048,256]{1,0:T(8,128)(2,1)} %cot_ref.1) | copy-start | bytes 3145732
  13.2 12.5 %copy-start = (bf16[256,256]{1,0:T(8,128)(2,1)S(1)}, bf16[256,256]{1,0:T(8,128)(2,1)}, u32[]{:S(2)}) copy-start(bf16[256,256]{1,0:T(8,128)(2,1)} %wn_ref.5) | copy-start | bytes 393220
  13.2 12.5 %copy-start.3 = (bf16[256,256]{1,0:T(8,128)(2,1)S(1)}, bf16[256,256]{1,0:T(8,128)(2,1)}, u32[]{:S(2)}) copy-start(bf16[256,256]{1,0:T(8,128)(2,1)} %ws_ref.3) | copy-start | bytes 393220
  13.2 12.5 %copy-start.5 = (f32[256]{0:T(256)S(1)}, f32[256]{0:T(256)}, u32[]{:S(2)}) copy-start(f32[256]{0:T(256)} %param.14) | copy-start | bytes 3076
  24.3 1.4 %collective-permute-start = (bf16[256,256]{1,0:T(8,128)(2,1)S(1)}, bf16[256,256]{1,0:T(8,128)(2,1)S(1)}, u32[]{:S(2)}, u32[]{:S(2)}) collective-permute-start(bf16[256,256]{1,0:T(8,128)(2,1)S(1)} %take_hubs.1.near_ref), channel_id=1, source_target_pairs={{0,8},{8,0},{16,24},{24,16},{1,9},{9,1},{17,25},{25,17},{2,10},{10... | collective-permute-start | bytes 393224 | tf_op jit(solution)/shard_map/ppermute | solution.py:404
  33.0 2.8 %collective-permute-start.1 = (bf16[1040,128]{1,0:T(8,128)(2,1)S(1)}, bf16[1040,128]{1,0:T(8,128)(2,1)S(1)}, u32[]{:S(2)}, u32[]{:S(2)}) collective-permute-start(bf16[1040,128]{1,0:T(8,128)(2,1)S(1)} %get-tuple-element.45), channel_id=1, source_target_pairs={{0,8},{8,0},{16,24},{24,16},{1,9},{9,1},{17,25},{25,17},{2,10},{10... | collective-permute-start | bytes 798728 | tf_op jit(solution)/shard_map/ppermute | solution.py:404
  33.2 24.7 %all-to-all-start.2 = ((bf16[32,16,256]{2,1,0:T(8,128)(2,1)}), bf16[32,16,256]{2,1,0:T(8,128)(2,1)S(1)}, u32[]{:S(2)}, u32[]{:S(2)}) async-start(bf16[32,16,256]{2,1,0:T(8,128)(2,1)} %get-tuple-element.57), calls=%async_computation.2 | async-start | bytes 524288 | tf_op jit(solution)/shard_map/all_to_all | solution.py:407
  35.9 8.1 %collective-permute-start.2 = (bf16[528,128]{1,0:T(8,128)(2,1)S(1)}, bf16[528,128]{1,0:T(8,128)(2,1)S(1)}, u32[]{:S(2)}, u32[]{:S(2)}) collective-permute-start(bf16[528,128]{1,0:T(8,128)(2,1)S(1)} %get-tuple-element.47), channel_id=1, source_target_pairs={{0,16},{8,24},{16,0},{24,8},{1,17},{9,25},{17,1},{25,9},{2,18},{10... | collective-permute-start | bytes 405512 | tf_op jit(solution)/shard_map/ppermute | solution.py:506
  37.6 1.2 %copy-start.1 = (bf16[2048,256]{1,0:T(8,128)(2,1)S(1)}, bf16[2048,256]{1,0:T(8,128)(2,1)}, u32[]{:S(2)}) copy-start(bf16[2048,256]{1,0:T(8,128)(2,1)} %get-tuple-element.48.grad_ref) | copy-start | bytes 3145732
  38.8 0.8 %copy-start.10 = (s32[2048,4]{0,1:T(4,128)S(1)}, s32[2048,4]{0,1:T(4,128)}, u32[]{:S(2)}) copy-start(s32[2048,4]{0,1:T(4,128)} %param.15) | copy-start | bytes 98308
  39.6 23.6 %copy-start.4 = (s32[1,512]{1,0:T(1,128)S(1)}, s32[1,512]{1,0:T(1,128)}, u32[]{:S(2)}) copy-start(s32[1,512]{1,0:T(1,128)} %send_ref.3) | copy-start | bytes 6148
  44.1 4.4 %collective-permute-start.3 = (bf16[272,128]{1,0:T(8,128)(2,1)S(1)}, bf16[272,128]{1,0:T(8,128)(2,1)S(1)}, u32[]{:S(2)}, u32[]{:S(2)}) collective-permute-start(bf16[272,128]{1,0:T(8,128)(2,1)S(1)} %get-tuple-element.51), channel_id=1, source_target_pairs={{0,1},{1,0},{2,3},{3,2},{4,5},{5,4},{6,7},{7,6},{8,9},{9,8},{10,11... | collective-permute-start | bytes 208904 | tf_op jit(solution)/shard_map/ppermute | solution.py:506
  48.5 4.0 %collective-permute-start.4 = (bf16[144,128]{1,0:T(8,128)(2,1)S(1)}, bf16[144,128]{1,0:T(8,128)(2,1)S(1)}, u32[]{:S(2)}, u32[]{:S(2)}) collective-permute-start(bf16[144,128]{1,0:T(8,128)(2,1)S(1)} %get-tuple-element.53), channel_id=1, source_target_pairs={{0,2},{1,3},{2,0},{3,1},{4,6},{5,7},{6,4},{7,5},{8,10},{9,11},{10,... | collective-permute-start | bytes 110600 | tf_op jit(solution)/shard_map/ppermute | solution.py:506
  52.5 4.7 %collective-permute-start.5 = (bf16[80,128]{1,0:T(8,128)(2,1)S(1)}, bf16[80,128]{1,0:T(8,128)(2,1)S(1)}, u32[]{:S(2)}, u32[]{:S(2)}) collective-permute-start(bf16[80,128]{1,0:T(8,128)(2,1)S(1)} %get-tuple-element.55), channel_id=1, source_target_pairs={{0,4},{1,5},{2,6},{3,7},{4,0},{5,1},{6,2},{7,3},{8,12},{9,13},{10,... | collective-permute-start | bytes 61448 | tf_op jit(solution)/shard_map/ppermute | solution.py:506
  57.9 12.9 %all-to-all-start.1 = ((bf16[32,8,256]{2,1,0:T(8,128)(2,1)}), bf16[32,8,256]{2,1,0:T(8,128)(2,1)S(1)}, u32[]{:S(2)}, u32[]{:S(2)}) async-start(bf16[32,8,256]{2,1,0:T(8,128)(2,1)} %get-tuple-element.56), calls=%async_computation.1 | async-start | bytes 262144 | tf_op jit(solution)/shard_map/all_to_all | solution.py:407
  63.1 1.2 %copy-start.2 = (bf16[2048,256]{1,0:T(8,128)(2,1)S(1)}, bf16[2048,256]{1,0:T(8,128)(2,1)}, u32[]{:S(2)}) copy-start(bf16[2048,256]{1,0:T(8,128)(2,1)} %get-tuple-element.48.grad_ref) | copy-start | bytes 3145732
  70.9 2.2 %collective-permute-start.7 = (bf16[32,8,256]{2,1,0:T(8,128)(2,1)S(1)}, bf16[32,8,256]{2,1,0:T(8,128)(2,1)S(1)}, u32[]{:S(2)}, u32[]{:S(2)}) collective-permute-start(bf16[32,8,256]{2,1,0:T(8,128)(2,1)S(1)} %all-to-all-done.1.near_ref), channel_id=1, source_target_pairs={{0,8},{8,0},{16,24},{24,16},{1,9},{9,1},{17,25},{25,17},{2,10},{10... | collective-permute-start | bytes 393224 | tf_op jit(solution)/shard_map/ppermute | solution.py:404
  71.0 1.2 %collective-permute-start.6 = (f32[8,256]{1,0:T(8,128)S(1)}, f32[8,256]{1,0:T(8,128)S(1)}, u32[]{:S(2)}, u32[]{:S(2)}) collective-permute-start(f32[8,256]{1,0:T(8,128)S(1)} %get-tuple-element.61), channel_id=1, source_target_pairs={{0,8},{8,0},{16,24},{24,16},{1,9},{9,1},{17,25},{25,17},{2,10},{10... | collective-permute-start | bytes 24584 | tf_op jit(solution)/shard_map/ppermute | solution.py:404

commit v10 on v8

--- a/solution.py
+++ b/solution.py
@@ -159,7 +159,7 @@
     half = slab - slots
     hub_rows = 2 * half
     bounds, hubs = parts * slots, parts * hub_rows
-    size = 2 * TILE
+    size = TILE
     blocks = nodes // size
     features, counts = slice(width, 2 * width), 3 * width
 
@@ -169,8 +169,8 @@
     def loads(block):
         at = here(block)
         return [
+            pltpu.make_async_copy(pack_hbm.at[at, 2 * width :], pack.at[at, counts:], in_sem.at[1, block]),
             pltpu.make_async_copy(pack_hbm.at[at, : 2 * width], pack.at[at, : 2 * width], in_sem.at[0, block]),
-            pltpu.make_async_copy(pack_hbm.at[at, 2 * width :], pack.at[at, counts:], in_sem.at[1, block]),
         ]
 
     coming = [loads(block) for block in range(blocks)]
@@ -464,8 +464,8 @@
             pltpu.VMEM((nodes, width), bf16),
             pltpu.VMEM((nodes, width), bf16),
             pltpu.VMEM((width, 2 * width + table), f32),
-            pltpu.SemaphoreType.DMA((2, nodes // (2 * TILE))),
-            pltpu.SemaphoreType.DMA((2, nodes // (2 * TILE))),
+            pltpu.SemaphoreType.DMA((2, nodes // TILE)),
+            pltpu.SemaphoreType.DMA((2, nodes // TILE)),
         ],
         flops=4 * nodes * table * width,
         moved=nodes * packed * 2,

time: 68.9 us -> 69.8 us (1.013)
  Pallas kernels: 27.8 us -> 28.7 us
    pallas_call x10, Pallas kernels: 27.8 us -> 28.7 us  [call(): pl.pallas_call(kernel, grid=grid, in_specs=in_specs, out_specs=out_specs,...]
where the time goes in v10:
time: 69.8 us; the launch traced here: 69.3 us
  Pallas kernels  28.7 us (41%)
  waiting for transfers between devices  22.1 us (32%)
  starting transfers between devices  12.9 us (18%)
  local copies, waits for them, and re-layouts  4.91 us (7%)
  between operations  0.79 us (1%)
    pallas_call x10, Pallas kernels, call(): pl.pallas_call(kernel, grid=grid, in_specs=in_specs, out_specs=out_specs,...  28.7 us
    all_to_all x3, waiting for transfers between devices, exchange(): return lax.all_to_all(value, AXES, split_axis=0, concat_axis=0, tiled=True)  18.8 us
    all_to_all x3, starting transfers between devices, exchange(): return lax.all_to_all(value, AXES, split_axis=0, concat_axis=0, tiled=True)  12.5 us
    unnamed x22, local copies, waits for them, and re-layouts  4.91 us
    ppermute x3, waiting for transfers between devices, sibling(): return lax.ppermute(value, 'row', [(r, r ^ 1) for r in range(rows)])  3.27 us
  transfers between devices with their start and end apart: 6, of which 6 were waited for; matrix products, arithmetic and copies ran while one was open for 0% of the time, Pallas kernels for 23%

profile of v10, /device:TPU:0, one launch (start us, length us, event | category | flops | bytes accessed | tf_op | source)
XLA Modules:
  0.0 69.3 jit_solution(1301204633569304547)
XLA Ops:
  0.6 0.0 copy-start.8
  0.6 0.0 copy-start.10
  0.7 0.0 copy-start.9
  0.7 2.7 %pick_rows.1 = bf16[32,24,256]{2,1,0:T(8,128)(2,1)} custom-call(s32[1,512]{1,0:T(1,128)} %send_ref.3, bf16[2048,256]{1,0:T(8,128)(2,1)} %own_ref, bf16[16,256]{1,0:T(8,128)(2,1)} %hub_ref.1), custom_call_target="tpu_custom_call" | custom-call | flops 536870912 | bytes 1048576 | tf_op jit(solution)/shard_map/pick_rows/pallas_call | solution.py:355
  3.4 7.3 %all-to-all-start = ((bf16[32,24,256]{2,1,0:T(8,128)(2,1)}), bf16[32,24,256]{2,1,0:T(8,128)(2,1)S(1)}, u32[]{:S(2)}, u32[]{:S(2)}) async-start(bf16[32,24,256]{2,1,0:T(8,128)(2,1)} %pick_rows.1), calls=%async_computation | async-start | bytes 786432 | tf_op jit(solution)/shard_map/all_to_all | solution.py:404
  10.8 0.0 copy-start.6
  10.8 1.2 %copy-done.6 = bf16[2048,256]{1,0:T(8,128)(2,1)S(1)} copy-done((bf16[2048,256]{1,0:T(8,128)(2,1)S(1)}, bf16[2048,256]{1,0:T(8,128)(2,1)}, u32[]{:S(2)}) %copy-start.6) | copy-done | bytes 1048600
  12.0 1.2 %copy-done.7 = bf16[2048,256]{1,0:T(8,128)(2,1)S(1)} copy-done((bf16[2048,256]{1,0:T(8,128)(2,1)S(1)}, bf16[2048,256]{1,0:T(8,128)(2,1)}, u32[]{:S(2)}) %copy-start.7) | copy-done | bytes 1048600
  13.2 7.2 %local_gather.1 = (f32[2048,256]{1,0:T(8,128)S(1)}, bf16[2048,1536]{1,0:T(8,128)(2,1)}) custom-call(s32[1]{0:T(128)} %bitcast.core_ref, s32[4,2048]{1,0:T(4,128)S(1)} %bitcast.8, s32[4,2048]{1,0:T(4,128)S(1)} %bitcast.7, s32[2,2048]{1,0:T(2,128)S(1)} %bitcast.10, bf16[2048,256]{1,0:T(8,128)(2,1)S(1)} %copy-done.6, bf16[2048,256]{1,0:T(8,128)(2,1)S(1)} %copy-done.6, ...), custom_call_target="tpu_custom_call" | custom-call | flops 8589934592 | bytes 6291456 | tf_op jit(solution)/shard_map/local_gather/pallas_call | solution.py:355
  20.4 3.8 %all-to-all-done.table_ref = bf16[32,24,256]{2,1,0:T(8,128)(2,1)S(1)} async-done(((bf16[32,24,256]{2,1,0:T(8,128)(2,1)}), bf16[32,24,256]{2,1,0:T(8,128)(2,1)S(1)}, u32[]{:S(2)}, u32[]{:S(2)}) %all-to-all-start) | async-done | bytes 393248 | tf_op jit(solution)/shard_map/all_to_all | solution.py:404
  24.3 0.1 collective-permute-start
  24.3 1.3 %collective-permute-done.far_ref = bf16[256,256]{1,0:T(8,128)(2,1)S(1)} collective-permute-done((bf16[256,256]{1,0:T(8,128)(2,1)S(1)}, bf16[256,256]{1,0:T(8,128)(2,1)S(1)}, u32[]{:S(2)}, u32[]{:S(2)}) %collective-permute-start) | collective-permute-done | bytes 131104 | tf_op jit(solution)/shard_map/ppermute | solution.py:401
  25.7 0.0 copy-done.3
  25.7 7.5 %activate.1 = (bf16[2048,256]{1,0:T(8,128)(2,1)}, bf16[2048,256]{1,0:T(8,128)(2,1)}, bf16[32,32,128]{2,1,0:T(8,128)(2,1)S(1)}, f32[32,40,128]{2,1,0:T(8,128)S(1)}, bf16[32,40,128]{2,1,0:T(8,128)(2,1)S(1)}) custom-call(s32[1]{0:T(128)} %bitcast.core_ref, bf16[32,24,256]{2,1,0:T(8,128)(2,1)S(1)} %all-to-all-done.table_ref, ...), custom_call_target="tpu_custom_call" | custom-call | flops 2147483648 | bytes 6291456 | tf_op jit(solution)/shard_map/activate/pallas_call | solution.py:355
  33.2 0.2 collective-permute-start.1
  33.4 1.5 %collective-permute-done.1.got_ref = bf16[32,40,128]{2,1,0:T(8,128)(2,1)S(1)} collective-permute-done((bf16[32,40,128]{2,1,0:T(8,128)(2,1)S(1)}, bf16[32,40,128]{2,1,0:T(8,128)(2,1)S(1)}, u32[]{:S(2)}, u32[]{:S(2)}) %collective-permute-start.1) | collective-permute-done | bytes 327712 | tf_op jit(solution)/shard_map/ppermute | solution.py:401
  34.9 0.9 %join_siblings.1 = bf16[32,72,128]{2,1,0:T(8,128)(2,1)} custom-call(bf16[32,32,128]{2,1,0:T(8,128)(2,1)S(1)} %get-tuple-element.34.bound_ref, f32[32,40,128]{2,1,0:T(8,128)S(1)} %get-tuple-element.35.keep_ref, bf16[32,40,128]{2,1,0:T(8,128)(2,1)S(1)} %collective-permute-done.1.got_ref), custom_call_target="tpu_custom_call" | custom-call | bytes 1769472 | tf_op jit(solution)/shard_map/join_siblings/pallas_call | solution.py:355
  35.8 2.6 %all-to-all-start.1 = ((bf16[32,72,128]{2,1,0:T(8,128)(2,1)}), bf16[32,72,128]{2,1,0:T(8,128)(2,1)S(1)}, u32[]{:S(2)}, u32[]{:S(2)}) async-start(bf16[32,72,128]{2,1,0:T(8,128)(2,1)} %join_siblings.1), calls=%async_computation.1 | async-start | bytes 1179648 | tf_op jit(solution)/shard_map/all_to_all | solution.py:404
  38.4 0.0 copy-start.1
  38.4 1.2 %copy-done.1 = bf16[2048,256]{1,0:T(8,128)(2,1)S(1)} copy-done((bf16[2048,256]{1,0:T(8,128)(2,1)S(1)}, bf16[2048,256]{1,0:T(8,128)(2,1)}, u32[]{:S(2)}) %copy-start.1) | copy-done | bytes 1048600
  39.7 4.4 %local_scatter.1.scat_ref = f32[2048,256]{1,0:T(8,128)S(1)} custom-call(s32[4,2048]{1,0:T(4,128)S(1)} %bitcast.9, bf16[2048,256]{1,0:T(8,128)(2,1)S(1)} %copy-done.1), custom_call_target="tpu_custom_call" | custom-call | flops 8589934592 | bytes 3145728 | tf_op jit(solution)/shard_map/local_scatter/pallas_call | solution.py:355
  44.1 12.1 %all-to-all-done.1.back_ref = bf16[32,72,128]{2,1,0:T(8,128)(2,1)S(1)} async-done(((bf16[32,72,128]{2,1,0:T(8,128)(2,1)}), bf16[32,72,128]{2,1,0:T(8,128)(2,1)S(1)}, u32[]{:S(2)}, u32[]{:S(2)}) %all-to-all-start.1) | async-done | bytes 589856 | tf_op jit(solution)/shard_map/all_to_all | solution.py:404
  56.2 0.7 weight_sums.1
  56.9 2.6 %all-to-all-start.2 = ((bf16[32,8,256]{2,1,0:T(8,128)(2,1)}), bf16[32,8,256]{2,1,0:T(8,128)(2,1)S(1)}, u32[]{:S(2)}, u32[]{:S(2)}) async-start(bf16[32,8,256]{2,1,0:T(8,128)(2,1)} %weight_sums.1), calls=%async_computation.2 | async-start | bytes 262144 | tf_op jit(solution)/shard_map/all_to_all | solution.py:404
  59.5 0.0 copy-start.2
  59.5 1.2 %copy-done.2 = bf16[2048,256]{1,0:T(8,128)(2,1)S(1)} copy-done((bf16[2048,256]{1,0:T(8,128)(2,1)S(1)}, bf16[2048,256]{1,0:T(8,128)(2,1)}, u32[]{:S(2)}) %copy-start.2) | copy-done | bytes 1048600
  60.7 3.6 %return_scatter.1 = f32[2048,256]{1,0:T(8,128)} custom-call(s32[1,512]{1,0:T(1,128)S(1)} %copy-done.4, bf16[32,72,128]{2,1,0:T(8,128)(2,1)S(1)} %all-to-all-done.1.back_ref, f32[2048,256]{1,0:T(8,128)S(1)} %local_scatter.1.scat_ref, bf16[2048,256]{1,0:T(8,128)(2,1)S(1)} %copy-done.2, bf16[256,256]{1,0:T(8,128)(2,1)S(1)} %copy-done.3, ...), custom_call_target="tpu_custom_call" | custom-call | flops 536870912 | bytes 5242880 | tf_op jit(solution)/shard_map/return_scatter/pallas_call | solution.py:355
  64.3 2.9 %all-to-all-done.2.near_ref = bf16[32,8,256]{2,1,0:T(8,128)(2,1)S(1)} async-done(((bf16[32,8,256]{2,1,0:T(8,128)(2,1)}), bf16[32,8,256]{2,1,0:T(8,128)(2,1)S(1)}, u32[]{:S(2)}, u32[]{:S(2)}) %all-to-all-start.2) | async-done | bytes 131104 | tf_op jit(solution)/shard_map/all_to_all | solution.py:404
  67.2 0.1 collective-permute-start.2
  67.3 0.8 %hub_sums.1 = (f32[1,256]{1,0:T(1,128)}, f32[16,256]{1,0:T(8,128)}) custom-call(bf16[32,72,128]{2,1,0:T(8,128)(2,1)S(1)} %all-to-all-done.1.back_ref, bf16[256,256]{1,0:T(8,128)(2,1)S(1)} %copy-done), custom_call_target="tpu_custom_call" | custom-call | bytes 1179648 | tf_op jit(solution)/shard_map/hub_sums/pallas_call | solution.py:355
  68.1 0.4 collective-permute-done.2.far_ref
  68.5 0.8 %weights.1 = (f32[256,256]{1,0:T(8,128)}, f32[256,256]{1,0:T(8,128)}) custom-call(s32[1]{0:T(128)} %bitcast.core_ref, bf16[32,8,256]{2,1,0:T(8,128)(2,1)S(1)} %all-to-all-done.2.near_ref, bf16[32,8,256]{2,1,0:T(8,128)(2,1)S(1)} %collective-permute-done.2.far_ref), custom_call_target="tpu_custom_call" | custom-call | bytes 786432 | tf_op jit(solution)/shard_map/weights/pallas_call | solution.py:355
  (12 shorter events, 0.0 us)
Async XLA Ops:
  0.6 10.1 %copy-start.8 = (s32[2048,4]{0,1:T(4,128)S(1)}, s32[2048,4]{0,1:T(4,128)}, u32[]{:S(2)}) copy-start(s32[2048,4]{0,1:T(4,128)} %param.17) | copy-start | bytes 98308
  0.6 10.1 %copy-start.10 = (s32[2048,2]{0,1:T(2,128)S(1)}, s32[2048,2]{0,1:T(2,128)}, u32[]{:S(2)}) copy-start(s32[2048,2]{0,1:T(2,128)} %param.16) | copy-start | bytes 49156
  0.7 10.1 %copy-start.9 = (s32[2048,4]{0,1:T(4,128)S(1)}, s32[2048,4]{0,1:T(4,128)}, u32[]{:S(2)}) copy-start(s32[2048,4]{0,1:T(4,128)} %param.15) | copy-start | bytes 98308
  3.4 20.8 %all-to-all-start = ((bf16[32,24,256]{2,1,0:T(8,128)(2,1)}), bf16[32,24,256]{2,1,0:T(8,128)(2,1)S(1)}, u32[]{:S(2)}, u32[]{:S(2)}) async-start(bf16[32,24,256]{2,1,0:T(8,128)(2,1)} %pick_rows.1), calls=%async_computation | async-start | bytes 786432 | tf_op jit(solution)/shard_map/all_to_all | solution.py:404
  10.8 1.2 %copy-start.6 = (bf16[2048,256]{1,0:T(8,128)(2,1)S(1)}, bf16[2048,256]{1,0:T(8,128)(2,1)}, u32[]{:S(2)}) copy-start(bf16[2048,256]{1,0:T(8,128)(2,1)} %own_ref) | copy-start | bytes 3145732
  12.0 1.2 %copy-start.7 = (bf16[2048,256]{1,0:T(8,128)(2,1)S(1)}, bf16[2048,256]{1,0:T(8,128)(2,1)}, u32[]{:S(2)}) copy-start(bf16[2048,256]{1,0:T(8,128)(2,1)} %cot_ref.1) | copy-start | bytes 3145732
  13.2 12.5 %copy-start = (bf16[256,256]{1,0:T(8,128)(2,1)S(1)}, bf16[256,256]{1,0:T(8,128)(2,1)}, u32[]{:S(2)}) copy-start(bf16[256,256]{1,0:T(8,128)(2,1)} %wn_ref.5) | copy-start | bytes 393220
  13.2 12.5 %copy-start.3 = (bf16[256,256]{1,0:T(8,128)(2,1)S(1)}, bf16[256,256]{1,0:T(8,128)(2,1)}, u32[]{:S(2)}) copy-start(bf16[256,256]{1,0:T(8,128)(2,1)} %ws_ref.3) | copy-start | bytes 393220
  13.2 12.5 %copy-start.5 = (f32[256]{0:T(256)S(1)}, f32[256]{0:T(256)}, u32[]{:S(2)}) copy-start(f32[256]{0:T(256)} %param.14) | copy-start | bytes 3076
  24.3 1.4 %collective-permute-start = (bf16[256,256]{1,0:T(8,128)(2,1)S(1)}, bf16[256,256]{1,0:T(8,128)(2,1)S(1)}, u32[]{:S(2)}, u32[]{:S(2)}) collective-permute-start(bf16[256,256]{1,0:T(8,128)(2,1)S(1)} %take_hubs.1.near_ref), channel_id=1, source_target_pairs={{0,8},{8,0},{16,24},{24,16},{1,9},{9,1},{17,25},{25,17},{2,10},{10... | collective-permute-start | bytes 393224 | tf_op jit(solution)/shard_map/ppermute | solution.py:401
  33.2 1.7 %collective-permute-start.1 = (bf16[32,40,128]{2,1,0:T(8,128)(2,1)S(1)}, bf16[32,40,128]{2,1,0:T(8,128)(2,1)S(1)}, u32[]{:S(2)}, u32[]{:S(2)}) collective-permute-start(bf16[32,40,128]{2,1,0:T(8,128)(2,1)S(1)} %get-tuple-element.36), channel_id=1, source_target_pairs={{0,8},{8,0},{16,24},{24,16},{1,9},{9,1},{17,25},{25,17},{2,10},{10... | collective-permute-start | bytes 983048 | tf_op jit(solution)/shard_map/ppermute | solution.py:401
  35.8 20.4 %all-to-all-start.1 = ((bf16[32,72,128]{2,1,0:T(8,128)(2,1)}), bf16[32,72,128]{2,1,0:T(8,128)(2,1)S(1)}, u32[]{:S(2)}, u32[]{:S(2)}) async-start(bf16[32,72,128]{2,1,0:T(8,128)(2,1)} %join_siblings.1), calls=%async_computation.1 | async-start | bytes 1179648 | tf_op jit(solution)/shard_map/all_to_all | solution.py:404
  38.4 1.2 %copy-start.1 = (bf16[2048,256]{1,0:T(8,128)(2,1)S(1)}, bf16[2048,256]{1,0:T(8,128)(2,1)}, u32[]{:S(2)}) copy-start(bf16[2048,256]{1,0:T(8,128)(2,1)} %get-tuple-element.37.grad_ref) | copy-start | bytes 3145732
  39.7 19.8 %copy-start.4 = (s32[1,512]{1,0:T(1,128)S(1)}, s32[1,512]{1,0:T(1,128)}, u32[]{:S(2)}) copy-start(s32[1,512]{1,0:T(1,128)} %send_ref.3) | copy-start | bytes 6148
  56.9 10.3 %all-to-all-start.2 = ((bf16[32,8,256]{2,1,0:T(8,128)(2,1)}), bf16[32,8,256]{2,1,0:T(8,128)(2,1)S(1)}, u32[]{:S(2)}, u32[]{:S(2)}) async-start(bf16[32,8,256]{2,1,0:T(8,128)(2,1)} %weight_sums.1), calls=%async_computation.2 | async-start | bytes 262144 | tf_op jit(solution)/shard_map/all_to_all | solution.py:404
  59.5 1.2 %copy-start.2 = (bf16[2048,256]{1,0:T(8,128)(2,1)S(1)}, bf16[2048,256]{1,0:T(8,128)(2,1)}, u32[]{:S(2)}) copy-start(bf16[2048,256]{1,0:T(8,128)(2,1)} %get-tuple-element.37.grad_ref) | copy-start | bytes 3145732
  67.2 1.3 %collective-permute-start.2 = (bf16[32,8,256]{2,1,0:T(8,128)(2,1)S(1)}, bf16[32,8,256]{2,1,0:T(8,128)(2,1)S(1)}, u32[]{:S(2)}, u32[]{:S(2)}) collective-permute-start(bf16[32,8,256]{2,1,0:T(8,128)(2,1)S(1)} %all-to-all-done.2.near_ref), channel_id=1, source_target_pairs={{0,8},{8,0},{16,24},{24,16},{1,9},{9,1},{17,25},{25,17},{2,10},{10... | collective-permute-start | bytes 393224 | tf_op jit(solution)/shard_map/ppermute | solution.py:401

commit v11 on v8

--- a/solution.py
+++ b/solution.py
@@ -103,7 +103,7 @@
     out_ref[...] = table_ref[:, slots:, :].astype(f32).reshape(out_ref.shape).astype(bf16)
 
 
-def local_kernel(split, hub_rows, core_ref, local_ref, remote_ref, hub_ref, feat_ref, own_ref, cot_ref, sum_ref, pack_ref):
+def local_kernel(split, hub_rows, core_ref, local_ref, remote_ref, hub_ref, feat_ref, own_ref, cot_ref, sum_ref, pack_ref, turned_ref):
     nodes, width = feat_ref.shape
     columns = [along_rows(row) for row in index_rows(local_ref, 0, TILE)]
     total = None
@@ -126,7 +126,9 @@
     for index, share in ((index_rows(remote_ref, 0, TILE), split), (hubs, counts - split)):
         columns = [along_rows(row) for row in index]
         for first in range(0, share, TILE):
+            there = slice(place - 2 * width + first, place - 2 * width + first + TILE)
             pack_ref[:, place + first : place + first + TILE] = hits_by_row(columns, first, TILE)
+            turned_ref[there, :] = hits_by_column(index, first, TILE)
         place += share
 
 
@@ -142,16 +144,19 @@
     bias_ref,
     sum_ref,
     pack_hbm,
+    by_col_hbm,
     act_hbm,
     grad_hbm,
     bound_ref,
     keep_ref,
     give_ref,
     pack,
+    by_col,
     act,
     grad_all,
     terms,
     in_sem,
+    col_sem,
     out_sem,
 ):
     nodes, width = sum_ref.shape
@@ -177,6 +182,8 @@
     for group in coming:
         for copy in group:
             copy.start()
+    col_load = pltpu.make_async_copy(by_col_hbm, by_col, col_sem)
+    col_load.start()
     table = jnp.concatenate(
         [table_ref[:, :slots, :].reshape(bounds, width), near_ref[...], far_ref[...]], axis=0
     )
@@ -192,7 +199,7 @@
                 copy.wait()
             following = sum_ref[here(block), :] + dot(pack[here(block), counts:], table)
         if block > 1:
-            part = dot(turned, pack[here(block - 2), width:])
+            part = dot(turned, pack[here(block - 2), width:counts])
             terms[...] = part if block == 2 else terms[...] + part
         if 0 < block <= blocks:
             at = here(block - 1)
@@ -214,21 +221,24 @@
     pieces = width // LANES
     step = 2 * width
 
+    grad = grad_all[...]
+    col_load.wait()
+
     def term_rows(first, count, rows):
-        return jnp.transpose(terms[:, first : first + count]).reshape(count // rows, rows, width)
+        return dot(by_col[first : first + count, :], grad).reshape(count // rows, rows, width)
 
     def lanes(piece):
         return slice(piece * LANES, (piece + 1) * LANES)
 
     first_core = core_ref[0] == 0
-    weights = term_rows(0, step, hub_rows)
+    weights = jnp.transpose(terms[...]).reshape(step // hub_rows, hub_rows, width)
     own = jnp.where(first_core, weights[:, :half], weights[:, half:])
     other = jnp.where(first_core, weights[:, half:], weights[:, :half])
     count = step // hub_rows
     for low in range(0, parts, count):
         if low > 0:
             own = other = jnp.zeros_like(own)
-        first = step + bounds + low * half
+        first = bounds + low * half
         keep = jnp.concatenate([term_rows(first, count * half, half), own], axis=1)
         give = jnp.concatenate([term_rows(first + hubs // 2, count * half, half), other], axis=1).astype(bf16)
         at = slice(low, low + count)
@@ -236,12 +246,12 @@
             there = slice(piece * hub_rows, (piece + 1) * hub_rows)
             keep_ref[at, there, :] = keep[:, :, lanes(piece)]
             give_ref[at, there, :] = give[:, :, lanes(piece)]
-    bias_total = dot(jnp.ones((16, nodes), bf16), grad_all[...])[:1]
+    bias_total = dot(jnp.ones((16, nodes), bf16), grad)[:1]
     rows = bias_rows([bias_total[:, lanes(piece)] for piece in range(pieces)])
     keep_ref[:, pieces * hub_rows :, :] = jnp.broadcast_to(rows[None], (parts, 8, LANES))
     give_ref[:, pieces * hub_rows :, :] = jnp.broadcast_to(rows.astype(bf16)[None], (parts, 8, LANES))
     for low in range(0, bounds, step):
-        bound_terms = term_rows(step + low, step, slots).astype(bf16)
+        bound_terms = term_rows(low, step, slots).astype(bf16)
         for piece in range(pieces):
             bound_ref[low // slots : (low + step) // slots, piece * slots : (piece + 1) * slots, :] = (
                 bound_terms[:, :, lanes(piece)]
@@ -420,14 +430,18 @@
     block = TILE
     by_block = pl.BlockSpec((block, width), lambda i: (i, 0))
     packed = 2 * width + table
-    local_sum, pack = call(
+    local_sum, pack, turned_counts = call(
         functools.partial(local_kernel, parts * slots, hub_rows),
         (core, local_t, remote_t, hub_t, features, features, cotangent),
         [SMEM]
         + [pl.BlockSpec((edges.shape[0], block), lambda i: (0, i)) for edges in (local_t, remote_t, hub_t)]
         + [whole_block((nodes, width)), by_block, by_block],
-        [shape((nodes, width), f32), pltpu.HBM((nodes, packed), bf16)],
-        [by_block, pl.BlockSpec((block, packed), lambda i: (i, 0))],
+        [shape((nodes, width), f32), pltpu.HBM((nodes, packed), bf16), pltpu.HBM((table, nodes), bf16)],
+        [
+            by_block,
+            pl.BlockSpec((block, packed), lambda i: (i, 0)),
+            pl.BlockSpec((table, block), lambda i: (0, i)),
+        ],
         "local_gather",
         grid=(nodes // block,),
         flops=8 * nodes * nodes * width,
@@ -448,8 +462,8 @@
 
     activated, grad_pre, bound_terms, keep, give = call(
         functools.partial(middle_kernel, scale, slots),
-        [core, received, near_hubs, far_hubs, w_self, w_neigh, bias, local_sum, pack],
-        [SMEM] + [VMEM] * 7 + [HBM],
+        [core, received, near_hubs, far_hubs, w_self, w_neigh, bias, local_sum, pack, turned_counts],
+        [SMEM] + [VMEM] * 7 + [HBM] * 2,
         [pltpu.HBM((nodes, width), bf16)] * 2
         + [
             shape((parts, pieces * slots, LANES), bf16),
@@ -461,10 +475,12 @@
         limit=MUCH_VMEM,
         scratch=[
             pltpu.VMEM((nodes, packed + width), bf16),
+            pltpu.VMEM((table, nodes), bf16),
             pltpu.VMEM((nodes, width), bf16),
             pltpu.VMEM((nodes, width), bf16),
-            pltpu.VMEM((width, 2 * width + table), f32),
+            pltpu.VMEM((width, 2 * width), f32),
             pltpu.SemaphoreType.DMA((2, nodes // (2 * TILE))),
+            pltpu.SemaphoreType.DMA,
             pltpu.SemaphoreType.DMA((2, nodes // (2 * TILE))),
         ],
         flops=4 * nodes * table * width,

time: 68.9 us -> 70.9 us (1.029)
  Pallas kernels: 27.8 us -> 30.3 us
  waiting for transfers between devices: 22.1 us -> 20.6 us
  starting transfers between devices: 12.9 us -> 13.7 us
    pallas_call x10, Pallas kernels: 27.8 us -> 30.3 us  [call(): pl.pallas_call(kernel, grid=grid, in_specs=in_specs, out_specs=out_specs,...]
    all_to_all x3, waiting for transfers between devices: 18.8 us -> 17.4 us  [exchange(): return lax.all_to_all(value, AXES, split_axis=0, concat_axis=0, tiled=True)]
    all_to_all x3, starting transfers between devices: 12.5 us -> 13.3 us  [exchange(): return lax.all_to_all(value, AXES, split_axis=0, concat_axis=0, tiled=True)]
  transfers between devices with their start and end apart: 6 -> 6, of which waited for: 6 -> 6; matrix products, arithmetic and copies ran while one was open for 0% -> 0% of each run, Pallas kernels for 23% -> 25%
where the time goes in v11:
time: 70.9 us; the launch traced here: 70.4 us
  Pallas kernels  30.3 us (43%)
  waiting for transfers between devices  20.6 us (29%)
  starting transfers between devices  13.7 us (19%)
  local copies, waits for them, and re-layouts  4.91 us (7%)
  between operations  0.79 us (1%)
    pallas_call x10, Pallas kernels, call(): pl.pallas_call(kernel, grid=grid, in_specs=in_specs, out_specs=out_specs,...  30.3 us
    all_to_all x3, waiting for transfers between devices, exchange(): return lax.all_to_all(value, AXES, split_axis=0, concat_axis=0, tiled=True)  17.4 us
    all_to_all x3, starting transfers between devices, exchange(): return lax.all_to_all(value, AXES, split_axis=0, concat_axis=0, tiled=True)  13.3 us
    unnamed x22, local copies, waits for them, and re-layouts  4.91 us
    ppermute x3, waiting for transfers between devices, sibling(): return lax.ppermute(value, 'row', [(r, r ^ 1) for r in range(rows)])  3.26 us
  transfers between devices with their start and end apart: 6, of which 6 were waited for; matrix products, arithmetic and copies ran while one was open for 0% of the time, Pallas kernels for 25%

profile of v11, /device:TPU:0, one launch (start us, length us, event | category | flops | bytes accessed | tf_op | source)
XLA Modules:
  0.0 70.4 jit_solution(8832705781530366837)
XLA Ops:
  0.6 0.0 copy-start.8
  0.6 0.0 copy-start.10
  0.7 0.0 copy-start.9
  0.7 2.7 %pick_rows.1 = bf16[32,24,256]{2,1,0:T(8,128)(2,1)} custom-call(s32[1,512]{1,0:T(1,128)} %send_ref.3, bf16[2048,256]{1,0:T(8,128)(2,1)} %own_ref, bf16[16,256]{1,0:T(8,128)(2,1)} %hub_ref.1), custom_call_target="tpu_custom_call" | custom-call | flops 536870912 | bytes 1048576 | tf_op jit(solution)/shard_map/pick_rows/pallas_call | solution.py:365
  3.4 7.3 %all-to-all-start = ((bf16[32,24,256]{2,1,0:T(8,128)(2,1)}), bf16[32,24,256]{2,1,0:T(8,128)(2,1)S(1)}, u32[]{:S(2)}, u32[]{:S(2)}) async-start(bf16[32,24,256]{2,1,0:T(8,128)(2,1)} %pick_rows.1), calls=%async_computation | async-start | bytes 786432 | tf_op jit(solution)/shard_map/all_to_all | solution.py:414
  10.8 0.0 copy-start.6
  10.8 1.2 %copy-done.6 = bf16[2048,256]{1,0:T(8,128)(2,1)S(1)} copy-done((bf16[2048,256]{1,0:T(8,128)(2,1)S(1)}, bf16[2048,256]{1,0:T(8,128)(2,1)}, u32[]{:S(2)}) %copy-start.6) | copy-done | bytes 1048600
  12.0 1.2 %copy-done.7 = bf16[2048,256]{1,0:T(8,128)(2,1)S(1)} copy-done((bf16[2048,256]{1,0:T(8,128)(2,1)S(1)}, bf16[2048,256]{1,0:T(8,128)(2,1)}, u32[]{:S(2)}) %copy-start.7) | copy-done | bytes 1048600
  13.2 8.6 %local_gather.1 = (f32[2048,256]{1,0:T(8,128)S(1)}, bf16[2048,1536]{1,0:T(8,128)(2,1)}, bf16[1024,2048]{1,0:T(8,128)(2,1)}) custom-call(s32[1]{0:T(128)} %bitcast.core_ref, s32[4,2048]{1,0:T(4,128)S(1)} %bitcast.8, s32[4,2048]{1,0:T(4,128)S(1)} %bitcast.7, s32[2,2048]{1,0:T(2,128)S(1)} %bitcast.10, bf16[2048,256]{1,0:T(8,128)(2,1)S(1)} %copy-done.6, ...), custom_call_target="tpu_custom_call" | custom-call | flops 8589934592 | bytes 6291456 | tf_op jit(solution)/shard_map/local_gather/pallas_call | solution.py:365
  21.9 2.4 %all-to-all-done.table_ref = bf16[32,24,256]{2,1,0:T(8,128)(2,1)S(1)} async-done(((bf16[32,24,256]{2,1,0:T(8,128)(2,1)}), bf16[32,24,256]{2,1,0:T(8,128)(2,1)S(1)}, u32[]{:S(2)}, u32[]{:S(2)}) %all-to-all-start) | async-done | bytes 393248 | tf_op jit(solution)/shard_map/all_to_all | solution.py:414
  24.3 0.1 collective-permute-start
  24.3 1.3 %collective-permute-done.far_ref = bf16[256,256]{1,0:T(8,128)(2,1)S(1)} collective-permute-done((bf16[256,256]{1,0:T(8,128)(2,1)S(1)}, bf16[256,256]{1,0:T(8,128)(2,1)S(1)}, u32[]{:S(2)}, u32[]{:S(2)}) %collective-permute-start) | collective-permute-done | bytes 131104 | tf_op jit(solution)/shard_map/ppermute | solution.py:411
  25.7 0.0 copy-done.3
  25.7 7.7 %activate.1 = (bf16[2048,256]{1,0:T(8,128)(2,1)}, bf16[2048,256]{1,0:T(8,128)(2,1)}, bf16[32,32,128]{2,1,0:T(8,128)(2,1)S(1)}, f32[32,40,128]{2,1,0:T(8,128)S(1)}, bf16[32,40,128]{2,1,0:T(8,128)(2,1)S(1)}) custom-call(s32[1]{0:T(128)} %bitcast.core_ref, bf16[32,24,256]{2,1,0:T(8,128)(2,1)S(1)} %all-to-all-done.table_ref, ...), custom_call_target="tpu_custom_call" | custom-call | flops 2147483648 | bytes 6291456 | tf_op jit(solution)/shard_map/activate/pallas_call | solution.py:365
  33.4 0.2 collective-permute-start.1
  33.6 1.5 %collective-permute-done.1.got_ref = bf16[32,40,128]{2,1,0:T(8,128)(2,1)S(1)} collective-permute-done((bf16[32,40,128]{2,1,0:T(8,128)(2,1)S(1)}, bf16[32,40,128]{2,1,0:T(8,128)(2,1)S(1)}, u32[]{:S(2)}, u32[]{:S(2)}) %collective-permute-start.1) | collective-permute-done | bytes 327712 | tf_op jit(solution)/shard_map/ppermute | solution.py:411
  35.1 0.9 %join_siblings.1 = bf16[32,72,128]{2,1,0:T(8,128)(2,1)} custom-call(bf16[32,32,128]{2,1,0:T(8,128)(2,1)S(1)} %get-tuple-element.36.bound_ref, f32[32,40,128]{2,1,0:T(8,128)S(1)} %get-tuple-element.37.keep_ref, bf16[32,40,128]{2,1,0:T(8,128)(2,1)S(1)} %collective-permute-done.1.got_ref), custom_call_target="tpu_custom_call" | custom-call | bytes 1769472 | tf_op jit(solution)/shard_map/join_siblings/pallas_call | solution.py:365
  36.0 3.4 %all-to-all-start.1 = ((bf16[32,72,128]{2,1,0:T(8,128)(2,1)}), bf16[32,72,128]{2,1,0:T(8,128)(2,1)S(1)}, u32[]{:S(2)}, u32[]{:S(2)}) async-start(bf16[32,72,128]{2,1,0:T(8,128)(2,1)} %join_siblings.1), calls=%async_computation.1 | async-start | bytes 1179648 | tf_op jit(solution)/shard_map/all_to_all | solution.py:414
  39.5 0.0 copy-start.1
  39.5 1.2 %copy-done.1 = bf16[2048,256]{1,0:T(8,128)(2,1)S(1)} copy-done((bf16[2048,256]{1,0:T(8,128)(2,1)S(1)}, bf16[2048,256]{1,0:T(8,128)(2,1)}, u32[]{:S(2)}) %copy-start.1) | copy-done | bytes 1048600
  40.7 4.4 %local_scatter.1.scat_ref = f32[2048,256]{1,0:T(8,128)S(1)} custom-call(s32[4,2048]{1,0:T(4,128)S(1)} %bitcast.9, bf16[2048,256]{1,0:T(8,128)(2,1)S(1)} %copy-done.1), custom_call_target="tpu_custom_call" | custom-call | flops 8589934592 | bytes 3145728 | tf_op jit(solution)/shard_map/local_scatter/pallas_call | solution.py:365
  45.1 12.1 %all-to-all-done.1.back_ref = bf16[32,72,128]{2,1,0:T(8,128)(2,1)S(1)} async-done(((bf16[32,72,128]{2,1,0:T(8,128)(2,1)}), bf16[32,72,128]{2,1,0:T(8,128)(2,1)S(1)}, u32[]{:S(2)}, u32[]{:S(2)}) %all-to-all-start.1) | async-done | bytes 589856 | tf_op jit(solution)/shard_map/all_to_all | solution.py:414
  57.2 0.7 weight_sums.1
  57.9 2.6 %all-to-all-start.2 = ((bf16[32,8,256]{2,1,0:T(8,128)(2,1)}), bf16[32,8,256]{2,1,0:T(8,128)(2,1)S(1)}, u32[]{:S(2)}, u32[]{:S(2)}) async-start(bf16[32,8,256]{2,1,0:T(8,128)(2,1)} %weight_sums.1), calls=%async_computation.2 | async-start | bytes 262144 | tf_op jit(solution)/shard_map/all_to_all | solution.py:414
  60.5 0.0 copy-start.2
  60.5 1.2 %copy-done.2 = bf16[2048,256]{1,0:T(8,128)(2,1)S(1)} copy-done((bf16[2048,256]{1,0:T(8,128)(2,1)S(1)}, bf16[2048,256]{1,0:T(8,128)(2,1)}, u32[]{:S(2)}) %copy-start.2) | copy-done | bytes 1048600
  61.7 3.6 %return_scatter.1 = f32[2048,256]{1,0:T(8,128)} custom-call(s32[1,512]{1,0:T(1,128)S(1)} %copy-done.4, bf16[32,72,128]{2,1,0:T(8,128)(2,1)S(1)} %all-to-all-done.1.back_ref, f32[2048,256]{1,0:T(8,128)S(1)} %local_scatter.1.scat_ref, bf16[2048,256]{1,0:T(8,128)(2,1)S(1)} %copy-done.2, bf16[256,256]{1,0:T(8,128)(2,1)S(1)} %copy-done.3, ...), custom_call_target="tpu_custom_call" | custom-call | flops 536870912 | bytes 5242880 | tf_op jit(solution)/shard_map/return_scatter/pallas_call | solution.py:365
  65.3 2.9 %all-to-all-done.2.near_ref = bf16[32,8,256]{2,1,0:T(8,128)(2,1)S(1)} async-done(((bf16[32,8,256]{2,1,0:T(8,128)(2,1)}), bf16[32,8,256]{2,1,0:T(8,128)(2,1)S(1)}, u32[]{:S(2)}, u32[]{:S(2)}) %all-to-all-start.2) | async-done | bytes 131104 | tf_op jit(solution)/shard_map/all_to_all | solution.py:414
  68.2 0.1 collective-permute-start.2
  68.3 0.8 %hub_sums.1 = (f32[1,256]{1,0:T(1,128)}, f32[16,256]{1,0:T(8,128)}) custom-call(bf16[32,72,128]{2,1,0:T(8,128)(2,1)S(1)} %all-to-all-done.1.back_ref, bf16[256,256]{1,0:T(8,128)(2,1)S(1)} %copy-done), custom_call_target="tpu_custom_call" | custom-call | bytes 1179648 | tf_op jit(solution)/shard_map/hub_sums/pallas_call | solution.py:365
  69.1 0.4 collective-permute-done.2.far_ref
  69.6 0.8 %weights.1 = (f32[256,256]{1,0:T(8,128)}, f32[256,256]{1,0:T(8,128)}) custom-call(s32[1]{0:T(128)} %bitcast.core_ref, bf16[32,8,256]{2,1,0:T(8,128)(2,1)S(1)} %all-to-all-done.2.near_ref, bf16[32,8,256]{2,1,0:T(8,128)(2,1)S(1)} %collective-permute-done.2.far_ref), custom_call_target="tpu_custom_call" | custom-call | bytes 786432 | tf_op jit(solution)/shard_map/weights/pallas_call | solution.py:365
  (12 shorter events, 0.0 us)
Async XLA Ops:
  0.6 10.1 %copy-start.8 = (s32[2048,4]{0,1:T(4,128)S(1)}, s32[2048,4]{0,1:T(4,128)}, u32[]{:S(2)}) copy-start(s32[2048,4]{0,1:T(4,128)} %param.17) | copy-start | bytes 98308
  0.6 10.1 %copy-start.10 = (s32[2048,2]{0,1:T(2,128)S(1)}, s32[2048,2]{0,1:T(2,128)}, u32[]{:S(2)}) copy-start(s32[2048,2]{0,1:T(2,128)} %param.16) | copy-start | bytes 49156
  0.7 10.1 %copy-start.9 = (s32[2048,4]{0,1:T(4,128)S(1)}, s32[2048,4]{0,1:T(4,128)}, u32[]{:S(2)}) copy-start(s32[2048,4]{0,1:T(4,128)} %param.15) | copy-start | bytes 98308
  3.4 20.8 %all-to-all-start = ((bf16[32,24,256]{2,1,0:T(8,128)(2,1)}), bf16[32,24,256]{2,1,0:T(8,128)(2,1)S(1)}, u32[]{:S(2)}, u32[]{:S(2)}) async-start(bf16[32,24,256]{2,1,0:T(8,128)(2,1)} %pick_rows.1), calls=%async_computation | async-start | bytes 786432 | tf_op jit(solution)/shard_map/all_to_all | solution.py:414
  10.8 1.2 %copy-start.6 = (bf16[2048,256]{1,0:T(8,128)(2,1)S(1)}, bf16[2048,256]{1,0:T(8,128)(2,1)}, u32[]{:S(2)}) copy-start(bf16[2048,256]{1,0:T(8,128)(2,1)} %own_ref) | copy-start | bytes 3145732
  12.0 1.2 %copy-start.7 = (bf16[2048,256]{1,0:T(8,128)(2,1)S(1)}, bf16[2048,256]{1,0:T(8,128)(2,1)}, u32[]{:S(2)}) copy-start(bf16[2048,256]{1,0:T(8,128)(2,1)} %cot_ref.1) | copy-start | bytes 3145732
  13.2 12.5 %copy-start = (bf16[256,256]{1,0:T(8,128)(2,1)S(1)}, bf16[256,256]{1,0:T(8,128)(2,1)}, u32[]{:S(2)}) copy-start(bf16[256,256]{1,0:T(8,128)(2,1)} %wn_ref.5) | copy-start | bytes 393220
  13.2 12.5 %copy-start.3 = (bf16[256,256]{1,0:T(8,128)(2,1)S(1)}, bf16[256,256]{1,0:T(8,128)(2,1)}, u32[]{:S(2)}) copy-start(bf16[256,256]{1,0:T(8,128)(2,1)} %ws_ref.3) | copy-start | bytes 393220
  13.2 12.5 %copy-start.5 = (f32[256]{0:T(256)S(1)}, f32[256]{0:T(256)}, u32[]{:S(2)}) copy-start(f32[256]{0:T(256)} %param.14) | copy-start | bytes 3076
  24.3 1.4 %collective-permute-start = (bf16[256,256]{1,0:T(8,128)(2,1)S(1)}, bf16[256,256]{1,0:T(8,128)(2,1)S(1)}, u32[]{:S(2)}, u32[]{:S(2)}) collective-permute-start(bf16[256,256]{1,0:T(8,128)(2,1)S(1)} %take_hubs.1.near_ref), channel_id=1, source_target_pairs={{0,8},{8,0},{16,24},{24,16},{1,9},{9,1},{17,25},{25,17},{2,10},{10... | collective-permute-start | bytes 393224 | tf_op jit(solution)/shard_map/ppermute | solution.py:411
  33.4 1.7 %collective-permute-start.1 = (bf16[32,40,128]{2,1,0:T(8,128)(2,1)S(1)}, bf16[32,40,128]{2,1,0:T(8,128)(2,1)S(1)}, u32[]{:S(2)}, u32[]{:S(2)}) collective-permute-start(bf16[32,40,128]{2,1,0:T(8,128)(2,1)S(1)} %get-tuple-element.38), channel_id=1, source_target_pairs={{0,8},{8,0},{16,24},{24,16},{1,9},{9,1},{17,25},{25,17},{2,10},{10... | collective-permute-start | bytes 983048 | tf_op jit(solution)/shard_map/ppermute | solution.py:411
  36.0 21.2 %all-to-all-start.1 = ((bf16[32,72,128]{2,1,0:T(8,128)(2,1)}), bf16[32,72,128]{2,1,0:T(8,128)(2,1)S(1)}, u32[]{:S(2)}, u32[]{:S(2)}) async-start(bf16[32,72,128]{2,1,0:T(8,128)(2,1)} %join_siblings.1), calls=%async_computation.1 | async-start | bytes 1179648 | tf_op jit(solution)/shard_map/all_to_all | solution.py:414
  39.5 1.2 %copy-start.1 = (bf16[2048,256]{1,0:T(8,128)(2,1)S(1)}, bf16[2048,256]{1,0:T(8,128)(2,1)}, u32[]{:S(2)}) copy-start(bf16[2048,256]{1,0:T(8,128)(2,1)} %get-tuple-element.39.grad_ref) | copy-start | bytes 3145732
  40.7 19.8 %copy-start.4 = (s32[1,512]{1,0:T(1,128)S(1)}, s32[1,512]{1,0:T(1,128)}, u32[]{:S(2)}) copy-start(s32[1,512]{1,0:T(1,128)} %send_ref.3) | copy-start | bytes 6148
  57.9 10.3 %all-to-all-start.2 = ((bf16[32,8,256]{2,1,0:T(8,128)(2,1)}), bf16[32,8,256]{2,1,0:T(8,128)(2,1)S(1)}, u32[]{:S(2)}, u32[]{:S(2)}) async-start(bf16[32,8,256]{2,1,0:T(8,128)(2,1)} %weight_sums.1), calls=%async_computation.2 | async-start | bytes 262144 | tf_op jit(solution)/shard_map/all_to_all | solution.py:414
  60.5 1.2 %copy-start.2 = (bf16[2048,256]{1,0:T(8,128)(2,1)S(1)}, bf16[2048,256]{1,0:T(8,128)(2,1)}, u32[]{:S(2)}) copy-start(bf16[2048,256]{1,0:T(8,128)(2,1)} %get-tuple-element.39.grad_ref) | copy-start | bytes 3145732
  68.2 1.3 %collective-permute-start.2 = (bf16[32,8,256]{2,1,0:T(8,128)(2,1)S(1)}, bf16[32,8,256]{2,1,0:T(8,128)(2,1)S(1)}, u32[]{:S(2)}, u32[]{:S(2)}) collective-permute-start(bf16[32,8,256]{2,1,0:T(8,128)(2,1)S(1)} %all-to-all-done.2.near_ref), channel_id=1, source_target_pairs={{0,8},{8,0},{16,24},{24,16},{1,9},{9,1},{17,25},{25,17},{2,10},{10... | collective-permute-start | bytes 393224 | tf_op jit(solution)/shard_map/ppermute | solution.py:411

commit v12 on v8

--- a/solution.py
+++ b/solution.py
@@ -488,13 +488,12 @@
         (local_t, grad_pre),
         [whole_block(local_t.shape), whole_block((nodes, width))],
         shape((nodes, width), f32),
-        pl.BlockSpec((block, width), lambda i: (i, 0)),
+        pl.BlockSpec((2 * TILE, width), lambda i: (i, 0)),
         "local_scatter",
-        grid=(nodes // block,),
+        grid=(nodes // (2 * TILE),),
         flops=8 * nodes * nodes * width,
         moved=nodes * width * 6,
     )
-    back, scattered = lax.optimization_barrier((back, scattered))
     weight_rows = call(
         functools.partial(weight_sum_kernel, slots, hub_rows, rows),
         (back,),

time: 68.9 us -> 67.4 us (0.978)
  blocking collectives: 0 us -> 19.8 us
  waiting for transfers between devices: 22.1 us -> 7.42 us
  starting transfers between devices: 12.9 us -> 10.3 us
  local copies, waits for them, and re-layouts: 4.91 us -> 2.48 us
  Pallas kernels: 27.8 us -> 26.3 us
    all_to_all x0 -> x1, blocking collectives: none -> 19.8 us  [exchange(): return lax.all_to_all(value, AXES, split_axis=0, concat_axis=0, tiled=True)]
    all_to_all x3 -> x2, waiting for transfers between devices: 18.8 us -> 4.15 us  [exchange(): return lax.all_to_all(value, AXES, split_axis=0, concat_axis=0, tiled=True)]
    all_to_all x3 -> x2, starting transfers between devices: 12.5 us -> 9.87 us  [exchange(): return lax.all_to_all(value, AXES, split_axis=0, concat_axis=0, tiled=True)]
    unnamed x22 -> x20, local copies, waits for them, and re-layouts: 4.91 us -> 2.48 us
    pallas_call x10, Pallas kernels: 27.8 us -> 26.3 us  [call(): pl.pallas_call(kernel, grid=grid, in_specs=in_specs, out_specs=out_specs,...]
  transfers between devices with their start and end apart: 6 -> 5, of which waited for: 6 -> 5; matrix products, arithmetic and copies ran while one was open for 0% -> 0% of each run, Pallas kernels for 23% -> 23%
where the time goes in v12:
time: 67.4 us; the launch traced here: 67.1 us
  Pallas kernels  26.3 us (39%)
  blocking collectives  19.8 us (29%)
  starting transfers between devices  10.3 us (15%)
  waiting for transfers between devices  7.42 us (11%)
  local copies, waits for them, and re-layouts  2.48 us (4%)
  between operations  0.79 us (1%)
    pallas_call x10, Pallas kernels, call(): pl.pallas_call(kernel, grid=grid, in_specs=in_specs, out_specs=out_specs,...  26.3 us
    all_to_all x1, blocking collectives, exchange(): return lax.all_to_all(value, AXES, split_axis=0, concat_axis=0, tiled=True)  19.8 us
    all_to_all x2, starting transfers between devices, exchange(): return lax.all_to_all(value, AXES, split_axis=0, concat_axis=0, tiled=True)  9.87 us
    all_to_all x2, waiting for transfers between devices, exchange(): return lax.all_to_all(value, AXES, split_axis=0, concat_axis=0, tiled=True)  4.15 us
    ppermute x3, waiting for transfers between devices, sibling(): return lax.ppermute(value, 'row', [(r, r ^ 1) for r in range(rows)])  3.27 us
    unnamed x20, local copies, waits for them, and re-layouts  2.48 us
  transfers between devices with their start and end apart: 5, of which 5 were waited for; matrix products, arithmetic and copies ran while one was open for 0% of the time, Pallas kernels for 23%

profile of v12, /device:TPU:0, one launch (start us, length us, event | category | flops | bytes accessed | tf_op | source)
XLA Modules:
  0.0 67.1 jit_solution(3776971298406073061)
XLA Ops:
  0.6 0.0 copy-start.7
  0.6 0.0 copy-start.9
  0.7 2.7 %pick_rows.1 = bf16[32,24,256]{2,1,0:T(8,128)(2,1)} custom-call(s32[1,512]{1,0:T(1,128)} %send_ref.3, bf16[2048,256]{1,0:T(8,128)(2,1)} %own_ref, bf16[16,256]{1,0:T(8,128)(2,1)} %hub_ref.1), custom_call_target="tpu_custom_call" | custom-call | flops 536870912 | bytes 1048576 | tf_op jit(solution)/shard_map/pick_rows/pallas_call | solution.py:355
  3.4 7.3 %all-to-all-start = ((bf16[32,24,256]{2,1,0:T(8,128)(2,1)}), bf16[32,24,256]{2,1,0:T(8,128)(2,1)S(1)}, u32[]{:S(2)}, u32[]{:S(2)}) async-start(bf16[32,24,256]{2,1,0:T(8,128)(2,1)} %pick_rows.1), calls=%async_computation | async-start | bytes 786432 | tf_op jit(solution)/shard_map/all_to_all | solution.py:404
  10.7 0.0 copy-done.7
  10.7 0.0 copy-done.9
  10.7 0.0 copy-done.8
  10.8 0.0 copy-start.5
  10.8 1.2 %copy-done.5 = bf16[2048,256]{1,0:T(8,128)(2,1)S(1)} copy-done((bf16[2048,256]{1,0:T(8,128)(2,1)S(1)}, bf16[2048,256]{1,0:T(8,128)(2,1)}, u32[]{:S(2)}) %copy-start.5) | copy-done | bytes 1048600
  12.0 1.2 %copy-done.6 = bf16[2048,256]{1,0:T(8,128)(2,1)S(1)} copy-done((bf16[2048,256]{1,0:T(8,128)(2,1)S(1)}, bf16[2048,256]{1,0:T(8,128)(2,1)}, u32[]{:S(2)}) %copy-start.6) | copy-done | bytes 1048600
  13.2 7.2 %local_gather.1 = (f32[2048,256]{1,0:T(8,128)S(1)}, bf16[2048,1536]{1,0:T(8,128)(2,1)}) custom-call(s32[1]{0:T(128)} %bitcast.core_ref, s32[4,2048]{1,0:T(4,128)S(1)} %bitcast.8, s32[4,2048]{1,0:T(4,128)S(1)} %bitcast.7, s32[2,2048]{1,0:T(2,128)S(1)} %bitcast.10, bf16[2048,256]{1,0:T(8,128)(2,1)S(1)} %copy-done.5, bf16[2048,256]{1,0:T(8,128)(2,1)S(1)} %copy-done.5, ...), custom_call_target="tpu_custom_call" | custom-call | flops 8589934592 | bytes 6291456 | tf_op jit(solution)/shard_map/local_gather/pallas_call | solution.py:355
  20.4 3.8 %all-to-all-done.table_ref = bf16[32,24,256]{2,1,0:T(8,128)(2,1)S(1)} async-done(((bf16[32,24,256]{2,1,0:T(8,128)(2,1)}), bf16[32,24,256]{2,1,0:T(8,128)(2,1)S(1)}, u32[]{:S(2)}, u32[]{:S(2)}) %all-to-all-start) | async-done | bytes 393248 | tf_op jit(solution)/shard_map/all_to_all | solution.py:404
  24.3 0.1 collective-permute-start
  24.3 1.3 %collective-permute-done.far_ref = bf16[256,256]{1,0:T(8,128)(2,1)S(1)} collective-permute-done((bf16[256,256]{1,0:T(8,128)(2,1)S(1)}, bf16[256,256]{1,0:T(8,128)(2,1)S(1)}, u32[]{:S(2)}, u32[]{:S(2)}) %collective-permute-start) | collective-permute-done | bytes 131104 | tf_op jit(solution)/shard_map/ppermute | solution.py:401
  25.7 0.0 copy-done
  25.7 6.6 %activate.1 = (bf16[2048,256]{1,0:T(8,128)(2,1)}, bf16[2048,256]{1,0:T(8,128)(2,1)}, bf16[32,32,128]{2,1,0:T(8,128)(2,1)S(1)}, f32[32,40,128]{2,1,0:T(8,128)S(1)}, bf16[32,40,128]{2,1,0:T(8,128)(2,1)S(1)}) custom-call(s32[1]{0:T(128)} %bitcast.core_ref, bf16[32,24,256]{2,1,0:T(8,128)(2,1)S(1)} %all-to-all-done.table_ref, ...), custom_call_target="tpu_custom_call" | custom-call | flops 2147483648 | bytes 6291456 | tf_op jit(solution)/shard_map/activate/pallas_call | solution.py:355
  32.3 0.0 copy-start.1
  32.3 0.2 collective-permute-start.1
  32.5 1.5 %collective-permute-done.1.got_ref = bf16[32,40,128]{2,1,0:T(8,128)(2,1)S(1)} collective-permute-done((bf16[32,40,128]{2,1,0:T(8,128)(2,1)S(1)}, bf16[32,40,128]{2,1,0:T(8,128)(2,1)S(1)}, u32[]{:S(2)}, u32[]{:S(2)}) %collective-permute-start.1) | collective-permute-done | bytes 327712 | tf_op jit(solution)/shard_map/ppermute | solution.py:401
  34.0 0.1 join_siblings.1
  34.1 19.8 %all_to_all.15.back_ref = bf16[32,72,128]{2,1,0:T(8,128)(2,1)S(1)} all-to-all(bf16[32,72,128]{2,1,0:T(8,128)(2,1)S(1)} %join_siblings.1), channel_id=1, replica_groups=mesh['row'=4,'col'=8] {'row','col'}, dimensions={0} | all-to-all | bytes 1179648 | tf_op jit(solution)/shard_map/all_to_all | solution.py:404
  53.9 0.7 %weight_sums.1 = bf16[32,8,256]{2,1,0:T(8,128)(2,1)} custom-call(bf16[32,72,128]{2,1,0:T(8,128)(2,1)S(1)} %all_to_all.15.back_ref), custom_call_target="tpu_custom_call" | custom-call | bytes 1179648 | tf_op jit(solution)/shard_map/weight_sums/pallas_call | solution.py:355
  54.6 2.6 %all-to-all-start.2 = ((bf16[32,8,256]{2,1,0:T(8,128)(2,1)}), bf16[32,8,256]{2,1,0:T(8,128)(2,1)S(1)}, u32[]{:S(2)}, u32[]{:S(2)}) async-start(bf16[32,8,256]{2,1,0:T(8,128)(2,1)} %weight_sums.1), calls=%async_computation.2 | async-start | bytes 262144 | tf_op jit(solution)/shard_map/all_to_all | solution.py:404
  57.2 0.0 copy-done.1
  57.2 0.0 copy-start.3
  57.2 3.7 %local_scatter.1.scat_ref = f32[2048,256]{1,0:T(8,128)S(1)} custom-call(s32[4,2048]{1,0:T(4,128)S(1)} %bitcast.9, bf16[2048,256]{1,0:T(8,128)(2,1)S(1)} %copy-done.1), custom_call_target="tpu_custom_call" | custom-call | flops 8589934592 | bytes 3145728 | tf_op jit(solution)/shard_map/local_scatter/pallas_call | solution.py:355
  60.9 3.6 %return_scatter.1 = f32[2048,256]{1,0:T(8,128)} custom-call(s32[1,512]{1,0:T(1,128)S(1)} %copy-done.3, bf16[32,72,128]{2,1,0:T(8,128)(2,1)S(1)} %all_to_all.15.back_ref, f32[2048,256]{1,0:T(8,128)S(1)} %local_scatter.1.scat_ref, bf16[2048,256]{1,0:T(8,128)(2,1)S(1)} %copy-done.1, bf16[256,256]{1,0:T(8,128)(2,1)S(1)} %copy-done.2, bf16[256,256]{1,0:T(8,128)(2,1)S(1)} %copy-done), custom_call_target="tpu_custom_call" | custom-call | flops 536870912 | bytes 5242880 | tf_op jit(solution)/shard_map/return_scatter/pallas_call | solution.py:355
  64.6 0.3 all-to-all-done.2.near_ref
  64.9 0.1 collective-permute-start.2
  65.0 0.8 %hub_sums.1 = (f32[1,256]{1,0:T(1,128)}, f32[16,256]{1,0:T(8,128)}) custom-call(bf16[32,72,128]{2,1,0:T(8,128)(2,1)S(1)} %all_to_all.15.back_ref, bf16[256,256]{1,0:T(8,128)(2,1)S(1)} %copy-done), custom_call_target="tpu_custom_call" | custom-call | bytes 1179648 | tf_op jit(solution)/shard_map/hub_sums/pallas_call | solution.py:355
  65.8 0.4 collective-permute-done.2.far_ref
  66.3 0.8 %weights.1 = (f32[256,256]{1,0:T(8,128)}, f32[256,256]{1,0:T(8,128)}) custom-call(s32[1]{0:T(128)} %bitcast.core_ref, bf16[32,8,256]{2,1,0:T(8,128)(2,1)S(1)} %all-to-all-done.2.near_ref, bf16[32,8,256]{2,1,0:T(8,128)(2,1)S(1)} %collective-permute-done.2.far_ref), custom_call_target="tpu_custom_call" | custom-call | bytes 786432 | tf_op jit(solution)/shard_map/weights/pallas_call | solution.py:355
  (9 shorter events, 0.0 us)
Async XLA Ops:
  0.6 10.1 %copy-start.7 = (s32[2048,4]{0,1:T(4,128)S(1)}, s32[2048,4]{0,1:T(4,128)}, u32[]{:S(2)}) copy-start(s32[2048,4]{0,1:T(4,128)} %param.17) | copy-start | bytes 98308
  0.6 10.1 %copy-start.9 = (s32[2048,2]{0,1:T(2,128)S(1)}, s32[2048,2]{0,1:T(2,128)}, u32[]{:S(2)}) copy-start(s32[2048,2]{0,1:T(2,128)} %param.16) | copy-start | bytes 49156
  0.7 10.1 %copy-start.8 = (s32[2048,4]{0,1:T(4,128)S(1)}, s32[2048,4]{0,1:T(4,128)}, u32[]{:S(2)}) copy-start(s32[2048,4]{0,1:T(4,128)} %param.15) | copy-start | bytes 98308
  3.4 20.8 %all-to-all-start = ((bf16[32,24,256]{2,1,0:T(8,128)(2,1)}), bf16[32,24,256]{2,1,0:T(8,128)(2,1)S(1)}, u32[]{:S(2)}, u32[]{:S(2)}) async-start(bf16[32,24,256]{2,1,0:T(8,128)(2,1)} %pick_rows.1), calls=%async_computation | async-start | bytes 786432 | tf_op jit(solution)/shard_map/all_to_all | solution.py:404
  10.8 1.2 %copy-start.5 = (bf16[2048,256]{1,0:T(8,128)(2,1)S(1)}, bf16[2048,256]{1,0:T(8,128)(2,1)}, u32[]{:S(2)}) copy-start(bf16[2048,256]{1,0:T(8,128)(2,1)} %own_ref) | copy-start | bytes 3145732
  12.0 1.2 %copy-start.6 = (bf16[2048,256]{1,0:T(8,128)(2,1)S(1)}, bf16[2048,256]{1,0:T(8,128)(2,1)}, u32[]{:S(2)}) copy-start(bf16[2048,256]{1,0:T(8,128)(2,1)} %cot_ref.1) | copy-start | bytes 3145732
  13.2 12.5 %copy-start = (bf16[256,256]{1,0:T(8,128)(2,1)S(1)}, bf16[256,256]{1,0:T(8,128)(2,1)}, u32[]{:S(2)}) copy-start(bf16[256,256]{1,0:T(8,128)(2,1)} %wn_ref.5) | copy-start | bytes 393220
  13.2 12.5 %copy-start.2 = (bf16[256,256]{1,0:T(8,128)(2,1)S(1)}, bf16[256,256]{1,0:T(8,128)(2,1)}, u32[]{:S(2)}) copy-start(bf16[256,256]{1,0:T(8,128)(2,1)} %ws_ref.3) | copy-start | bytes 393220
  13.2 12.5 %copy-start.4 = (f32[256]{0:T(256)S(1)}, f32[256]{0:T(256)}, u32[]{:S(2)}) copy-start(f32[256]{0:T(256)} %param.14) | copy-start | bytes 3076
  24.3 1.4 %collective-permute-start = (bf16[256,256]{1,0:T(8,128)(2,1)S(1)}, bf16[256,256]{1,0:T(8,128)(2,1)S(1)}, u32[]{:S(2)}, u32[]{:S(2)}) collective-permute-start(bf16[256,256]{1,0:T(8,128)(2,1)S(1)} %take_hubs.1.near_ref), channel_id=1, source_target_pairs={{0,8},{8,0},{16,24},{24,16},{1,9},{9,1},{17,25},{25,17},{2,10},{10... | collective-permute-start | bytes 393224 | tf_op jit(solution)/shard_map/ppermute | solution.py:401
  32.3 24.9 %copy-start.1 = (bf16[2048,256]{1,0:T(8,128)(2,1)S(1)}, bf16[2048,256]{1,0:T(8,128)(2,1)}, u32[]{:S(2)}) copy-start(bf16[2048,256]{1,0:T(8,128)(2,1)} %get-tuple-element.35.grad_ref) | copy-start | bytes 3145732
  32.3 1.7 %collective-permute-start.1 = (bf16[32,40,128]{2,1,0:T(8,128)(2,1)S(1)}, bf16[32,40,128]{2,1,0:T(8,128)(2,1)S(1)}, u32[]{:S(2)}, u32[]{:S(2)}) collective-permute-start(bf16[32,40,128]{2,1,0:T(8,128)(2,1)S(1)} %get-tuple-element.34), channel_id=1, source_target_pairs={{0,8},{8,0},{16,24},{24,16},{1,9},{9,1},{17,25},{25,17},{2,10},{10... | collective-permute-start | bytes 983048 | tf_op jit(solution)/shard_map/ppermute | solution.py:401
  54.6 10.3 %all-to-all-start.2 = ((bf16[32,8,256]{2,1,0:T(8,128)(2,1)}), bf16[32,8,256]{2,1,0:T(8,128)(2,1)S(1)}, u32[]{:S(2)}, u32[]{:S(2)}) async-start(bf16[32,8,256]{2,1,0:T(8,128)(2,1)} %weight_sums.1), calls=%async_computation.2 | async-start | bytes 262144 | tf_op jit(solution)/shard_map/all_to_all | solution.py:404
  57.2 3.7 %copy-start.3 = (s32[1,512]{1,0:T(1,128)S(1)}, s32[1,512]{1,0:T(1,128)}, u32[]{:S(2)}) copy-start(s32[1,512]{1,0:T(1,128)} %send_ref.3) | copy-start | bytes 6148
  64.9 1.3 %collective-permute-start.2 = (bf16[32,8,256]{2,1,0:T(8,128)(2,1)S(1)}, bf16[32,8,256]{2,1,0:T(8,128)(2,1)S(1)}, u32[]{:S(2)}, u32[]{:S(2)}) collective-permute-start(bf16[32,8,256]{2,1,0:T(8,128)(2,1)S(1)} %all-to-all-done.2.near_ref), channel_id=1, source_target_pairs={{0,8},{8,0},{16,24},{24,16},{1,9},{9,1},{17,25},{25,17},{2,10},{10... | collective-permute-start | bytes 393224 | tf_op jit(solution)/shard_map/ppermute | solution.py:401

commit v13 on v12

--- a/solution.py
+++ b/solution.py
@@ -159,12 +159,12 @@
     half = slab - slots
     hub_rows = 2 * half
     bounds, hubs = parts * slots, parts * hub_rows
-    size = 2 * TILE
-    blocks = nodes // size
+    edges = [0] + list(range(TILE, nodes, 2 * TILE)) + [nodes]
+    blocks = len(edges) - 1
     features, counts = slice(width, 2 * width), 3 * width
 
     def here(block):
-        return slice(block * size, (block + 1) * size)
+        return slice(edges[block], edges[block + 1])
 
     def loads(block):
         at = here(block)
@@ -464,8 +464,8 @@
             pltpu.VMEM((nodes, width), bf16),
             pltpu.VMEM((nodes, width), bf16),
             pltpu.VMEM((width, 2 * width + table), f32),
-            pltpu.SemaphoreType.DMA((2, nodes // (2 * TILE))),
-            pltpu.SemaphoreType.DMA((2, nodes // (2 * TILE))),
+            pltpu.SemaphoreType.DMA((2, nodes // (2 * TILE) + 1)),
+            pltpu.SemaphoreType.DMA((2, nodes // (2 * TILE) + 1)),
         ],
         flops=4 * nodes * table * width,
         moved=nodes * packed * 2,

time: 67.4 us -> 68.1 us (1.010)
  Pallas kernels: 26.3 us -> 27 us
where the time goes in v13:
time: 68.1 us; the launch traced here: 67.8 us
  Pallas kernels  27 us (40%)
  blocking collectives  19.8 us (29%)
  starting transfers between devices  10.3 us (15%)
  waiting for transfers between devices  7.41 us (11%)
  local copies, waits for them, and re-layouts  2.48 us (4%)
  between operations  0.79 us (1%)
    pallas_call x10, Pallas kernels, call(): pl.pallas_call(kernel, grid=grid, in_specs=in_specs, out_specs=out_specs,...  27 us
    all_to_all x1, blocking collectives, exchange(): return lax.all_to_all(value, AXES, split_axis=0, concat_axis=0, tiled=True)  19.8 us
    all_to_all x2, starting transfers between devices, exchange(): return lax.all_to_all(value, AXES, split_axis=0, concat_axis=0, tiled=True)  9.87 us
    all_to_all x2, waiting for transfers between devices, exchange(): return lax.all_to_all(value, AXES, split_axis=0, concat_axis=0, tiled=True)  4.15 us
    ppermute x3, waiting for transfers between devices, sibling(): return lax.ppermute(value, 'row', [(r, r ^ 1) for r in range(rows)])  3.26 us
    unnamed x20, local copies, waits for them, and re-layouts  2.48 us
  transfers between devices with their start and end apart: 5, of which 5 were waited for; matrix products, arithmetic and copies ran while one was open for 0% of the time, Pallas kernels for 23%

profile of v13, /device:TPU:0, one launch (start us, length us, event | category | flops | bytes accessed | tf_op | source)
XLA Modules:
  0.0 67.8 jit_solution(13227437762894819130)
XLA Ops:
  0.6 0.0 copy-start.7
  0.6 0.0 copy-start.9
  0.7 0.0 copy-start.8
  0.7 2.7 %pick_rows.1 = bf16[32,24,256]{2,1,0:T(8,128)(2,1)} custom-call(s32[1,512]{1,0:T(1,128)} %send_ref.3, bf16[2048,256]{1,0:T(8,128)(2,1)} %own_ref, bf16[16,256]{1,0:T(8,128)(2,1)} %hub_ref.1), custom_call_target="tpu_custom_call" | custom-call | flops 536870912 | bytes 1048576 | tf_op jit(solution)/shard_map/pick_rows/pallas_call | solution.py:355
  3.4 7.3 %all-to-all-start = ((bf16[32,24,256]{2,1,0:T(8,128)(2,1)}), bf16[32,24,256]{2,1,0:T(8,128)(2,1)S(1)}, u32[]{:S(2)}, u32[]{:S(2)}) async-start(bf16[32,24,256]{2,1,0:T(8,128)(2,1)} %pick_rows.1), calls=%async_computation | async-start | bytes 786432 | tf_op jit(solution)/shard_map/all_to_all | solution.py:404
  10.7 0.0 copy-done.7
  10.7 0.0 copy-done.9
  10.7 0.0 copy-done.8
  10.8 0.0 copy-start.5
  10.8 1.2 %copy-done.5 = bf16[2048,256]{1,0:T(8,128)(2,1)S(1)} copy-done((bf16[2048,256]{1,0:T(8,128)(2,1)S(1)}, bf16[2048,256]{1,0:T(8,128)(2,1)}, u32[]{:S(2)}) %copy-start.5) | copy-done | bytes 1048600
  12.0 1.2 %copy-done.6 = bf16[2048,256]{1,0:T(8,128)(2,1)S(1)} copy-done((bf16[2048,256]{1,0:T(8,128)(2,1)S(1)}, bf16[2048,256]{1,0:T(8,128)(2,1)}, u32[]{:S(2)}) %copy-start.6) | copy-done | bytes 1048600
  13.2 7.2 %local_gather.1 = (f32[2048,256]{1,0:T(8,128)S(1)}, bf16[2048,1536]{1,0:T(8,128)(2,1)}) custom-call(s32[1]{0:T(128)} %bitcast.core_ref, s32[4,2048]{1,0:T(4,128)S(1)} %bitcast.8, s32[4,2048]{1,0:T(4,128)S(1)} %bitcast.7, s32[2,2048]{1,0:T(2,128)S(1)} %bitcast.10, bf16[2048,256]{1,0:T(8,128)(2,1)S(1)} %copy-done.5, bf16[2048,256]{1,0:T(8,128)(2,1)S(1)} %copy-done.5, ...), custom_call_target="tpu_custom_call" | custom-call | flops 8589934592 | bytes 6291456 | tf_op jit(solution)/shard_map/local_gather/pallas_call | solution.py:355
  20.4 3.8 %all-to-all-done.table_ref = bf16[32,24,256]{2,1,0:T(8,128)(2,1)S(1)} async-done(((bf16[32,24,256]{2,1,0:T(8,128)(2,1)}), bf16[32,24,256]{2,1,0:T(8,128)(2,1)S(1)}, u32[]{:S(2)}, u32[]{:S(2)}) %all-to-all-start) | async-done | bytes 393248 | tf_op jit(solution)/shard_map/all_to_all | solution.py:404
  24.3 0.1 collective-permute-start
  24.3 1.3 %collective-permute-done.far_ref = bf16[256,256]{1,0:T(8,128)(2,1)S(1)} collective-permute-done((bf16[256,256]{1,0:T(8,128)(2,1)S(1)}, bf16[256,256]{1,0:T(8,128)(2,1)S(1)}, u32[]{:S(2)}, u32[]{:S(2)}) %collective-permute-start) | collective-permute-done | bytes 131104 | tf_op jit(solution)/shard_map/ppermute | solution.py:401
  25.7 0.0 copy-done.2
  25.7 7.3 %activate.1 = (bf16[2048,256]{1,0:T(8,128)(2,1)}, bf16[2048,256]{1,0:T(8,128)(2,1)}, bf16[32,32,128]{2,1,0:T(8,128)(2,1)S(1)}, f32[32,40,128]{2,1,0:T(8,128)S(1)}, bf16[32,40,128]{2,1,0:T(8,128)(2,1)S(1)}) custom-call(s32[1]{0:T(128)} %bitcast.core_ref, bf16[32,24,256]{2,1,0:T(8,128)(2,1)S(1)} %all-to-all-done.table_ref, ...), custom_call_target="tpu_custom_call" | custom-call | flops 2147483648 | bytes 6291456 | tf_op jit(solution)/shard_map/activate/pallas_call | solution.py:355
  33.0 0.0 copy-start.1
  33.0 0.2 collective-permute-start.1
  33.2 1.5 %collective-permute-done.1.got_ref = bf16[32,40,128]{2,1,0:T(8,128)(2,1)S(1)} collective-permute-done((bf16[32,40,128]{2,1,0:T(8,128)(2,1)S(1)}, bf16[32,40,128]{2,1,0:T(8,128)(2,1)S(1)}, u32[]{:S(2)}, u32[]{:S(2)}) %collective-permute-start.1) | collective-permute-done | bytes 327712 | tf_op jit(solution)/shard_map/ppermute | solution.py:401
  34.7 0.1 join_siblings.1
  34.8 19.8 %all_to_all.15.back_ref = bf16[32,72,128]{2,1,0:T(8,128)(2,1)S(1)} all-to-all(bf16[32,72,128]{2,1,0:T(8,128)(2,1)S(1)} %join_siblings.1), channel_id=1, replica_groups=mesh['row'=4,'col'=8] {'row','col'}, dimensions={0} | all-to-all | bytes 1179648 | tf_op jit(solution)/shard_map/all_to_all | solution.py:404
  54.6 0.7 %weight_sums.1 = bf16[32,8,256]{2,1,0:T(8,128)(2,1)} custom-call(bf16[32,72,128]{2,1,0:T(8,128)(2,1)S(1)} %all_to_all.15.back_ref), custom_call_target="tpu_custom_call" | custom-call | bytes 1179648 | tf_op jit(solution)/shard_map/weight_sums/pallas_call | solution.py:355
  55.3 2.6 %all-to-all-start.2 = ((bf16[32,8,256]{2,1,0:T(8,128)(2,1)}), bf16[32,8,256]{2,1,0:T(8,128)(2,1)S(1)}, u32[]{:S(2)}, u32[]{:S(2)}) async-start(bf16[32,8,256]{2,1,0:T(8,128)(2,1)} %weight_sums.1), calls=%async_computation.2 | async-start | bytes 262144 | tf_op jit(solution)/shard_map/all_to_all | solution.py:404
  57.9 0.0 copy-start.3
  57.9 3.7 %local_scatter.1.scat_ref = f32[2048,256]{1,0:T(8,128)S(1)} custom-call(s32[4,2048]{1,0:T(4,128)S(1)} %bitcast.9, bf16[2048,256]{1,0:T(8,128)(2,1)S(1)} %copy-done.1), custom_call_target="tpu_custom_call" | custom-call | flops 8589934592 | bytes 3145728 | tf_op jit(solution)/shard_map/local_scatter/pallas_call | solution.py:355
  61.6 3.6 %return_scatter.1 = f32[2048,256]{1,0:T(8,128)} custom-call(s32[1,512]{1,0:T(1,128)S(1)} %copy-done.3, bf16[32,72,128]{2,1,0:T(8,128)(2,1)S(1)} %all_to_all.15.back_ref, f32[2048,256]{1,0:T(8,128)S(1)} %local_scatter.1.scat_ref, bf16[2048,256]{1,0:T(8,128)(2,1)S(1)} %copy-done.1, bf16[256,256]{1,0:T(8,128)(2,1)S(1)} %copy-done.2, bf16[256,256]{1,0:T(8,128)(2,1)S(1)} %copy-done), custom_call_target="tpu_custom_call" | custom-call | flops 536870912 | bytes 5242880 | tf_op jit(solution)/shard_map/return_scatter/pallas_call | solution.py:355
  65.3 0.3 all-to-all-done.2.near_ref
  65.6 0.1 collective-permute-start.2
  65.7 0.8 %hub_sums.1 = (f32[1,256]{1,0:T(1,128)}, f32[16,256]{1,0:T(8,128)}) custom-call(bf16[32,72,128]{2,1,0:T(8,128)(2,1)S(1)} %all_to_all.15.back_ref, bf16[256,256]{1,0:T(8,128)(2,1)S(1)} %copy-done), custom_call_target="tpu_custom_call" | custom-call | bytes 1179648 | tf_op jit(solution)/shard_map/hub_sums/pallas_call | solution.py:355
  66.5 0.4 collective-permute-done.2.far_ref
  67.0 0.8 %weights.1 = (f32[256,256]{1,0:T(8,128)}, f32[256,256]{1,0:T(8,128)}) custom-call(s32[1]{0:T(128)} %bitcast.core_ref, bf16[32,8,256]{2,1,0:T(8,128)(2,1)S(1)} %all-to-all-done.2.near_ref, bf16[32,8,256]{2,1,0:T(8,128)(2,1)S(1)} %collective-permute-done.2.far_ref), custom_call_target="tpu_custom_call" | custom-call | bytes 786432 | tf_op jit(solution)/shard_map/weights/pallas_call | solution.py:355
  (9 shorter events, 0.0 us)
Async XLA Ops:
  0.6 10.1 %copy-start.7 = (s32[2048,4]{0,1:T(4,128)S(1)}, s32[2048,4]{0,1:T(4,128)}, u32[]{:S(2)}) copy-start(s32[2048,4]{0,1:T(4,128)} %param.17) | copy-start | bytes 98308
  0.6 10.1 %copy-start.9 = (s32[2048,2]{0,1:T(2,128)S(1)}, s32[2048,2]{0,1:T(2,128)}, u32[]{:S(2)}) copy-start(s32[2048,2]{0,1:T(2,128)} %param.16) | copy-start | bytes 49156
  0.7 10.1 %copy-start.8 = (s32[2048,4]{0,1:T(4,128)S(1)}, s32[2048,4]{0,1:T(4,128)}, u32[]{:S(2)}) copy-start(s32[2048,4]{0,1:T(4,128)} %param.15) | copy-start | bytes 98308
  3.4 20.8 %all-to-all-start = ((bf16[32,24,256]{2,1,0:T(8,128)(2,1)}), bf16[32,24,256]{2,1,0:T(8,128)(2,1)S(1)}, u32[]{:S(2)}, u32[]{:S(2)}) async-start(bf16[32,24,256]{2,1,0:T(8,128)(2,1)} %pick_rows.1), calls=%async_computation | async-start | bytes 786432 | tf_op jit(solution)/shard_map/all_to_all | solution.py:404
  10.8 1.2 %copy-start.5 = (bf16[2048,256]{1,0:T(8,128)(2,1)S(1)}, bf16[2048,256]{1,0:T(8,128)(2,1)}, u32[]{:S(2)}) copy-start(bf16[2048,256]{1,0:T(8,128)(2,1)} %own_ref) | copy-start | bytes 3145732
  12.0 1.2 %copy-start.6 = (bf16[2048,256]{1,0:T(8,128)(2,1)S(1)}, bf16[2048,256]{1,0:T(8,128)(2,1)}, u32[]{:S(2)}) copy-start(bf16[2048,256]{1,0:T(8,128)(2,1)} %cot_ref.1) | copy-start | bytes 3145732
  13.2 12.5 %copy-start = (bf16[256,256]{1,0:T(8,128)(2,1)S(1)}, bf16[256,256]{1,0:T(8,128)(2,1)}, u32[]{:S(2)}) copy-start(bf16[256,256]{1,0:T(8,128)(2,1)} %wn_ref.5) | copy-start | bytes 393220
  13.2 12.5 %copy-start.2 = (bf16[256,256]{1,0:T(8,128)(2,1)S(1)}, bf16[256,256]{1,0:T(8,128)(2,1)}, u32[]{:S(2)}) copy-start(bf16[256,256]{1,0:T(8,128)(2,1)} %ws_ref.3) | copy-start | bytes 393220
  13.2 12.5 %copy-start.4 = (f32[256]{0:T(256)S(1)}, f32[256]{0:T(256)}, u32[]{:S(2)}) copy-start(f32[256]{0:T(256)} %param.14) | copy-start | bytes 3076
  24.3 1.4 %collective-permute-start = (bf16[256,256]{1,0:T(8,128)(2,1)S(1)}, bf16[256,256]{1,0:T(8,128)(2,1)S(1)}, u32[]{:S(2)}, u32[]{:S(2)}) collective-permute-start(bf16[256,256]{1,0:T(8,128)(2,1)S(1)} %take_hubs.1.near_ref), channel_id=1, source_target_pairs={{0,8},{8,0},{16,24},{24,16},{1,9},{9,1},{17,25},{25,17},{2,10},{10... | collective-permute-start | bytes 393224 | tf_op jit(solution)/shard_map/ppermute | solution.py:401
  33.0 24.9 %copy-start.1 = (bf16[2048,256]{1,0:T(8,128)(2,1)S(1)}, bf16[2048,256]{1,0:T(8,128)(2,1)}, u32[]{:S(2)}) copy-start(bf16[2048,256]{1,0:T(8,128)(2,1)} %get-tuple-element.35.grad_ref) | copy-start | bytes 3145732
  33.0 1.7 %collective-permute-start.1 = (bf16[32,40,128]{2,1,0:T(8,128)(2,1)S(1)}, bf16[32,40,128]{2,1,0:T(8,128)(2,1)S(1)}, u32[]{:S(2)}, u32[]{:S(2)}) collective-permute-start(bf16[32,40,128]{2,1,0:T(8,128)(2,1)S(1)} %get-tuple-element.34), channel_id=1, source_target_pairs={{0,8},{8,0},{16,24},{24,16},{1,9},{9,1},{17,25},{25,17},{2,10},{10... | collective-permute-start | bytes 983048 | tf_op jit(solution)/shard_map/ppermute | solution.py:401
  55.3 10.3 %all-to-all-start.2 = ((bf16[32,8,256]{2,1,0:T(8,128)(2,1)}), bf16[32,8,256]{2,1,0:T(8,128)(2,1)S(1)}, u32[]{:S(2)}, u32[]{:S(2)}) async-start(bf16[32,8,256]{2,1,0:T(8,128)(2,1)} %weight_sums.1), calls=%async_computation.2 | async-start | bytes 262144 | tf_op jit(solution)/shard_map/all_to_all | solution.py:404
  57.9 3.8 %copy-start.3 = (s32[1,512]{1,0:T(1,128)S(1)}, s32[1,512]{1,0:T(1,128)}, u32[]{:S(2)}) copy-start(s32[1,512]{1,0:T(1,128)} %send_ref.3) | copy-start | bytes 6148
  65.6 1.3 %collective-permute-start.2 = (bf16[32,8,256]{2,1,0:T(8,128)(2,1)S(1)}, bf16[32,8,256]{2,1,0:T(8,128)(2,1)S(1)}, u32[]{:S(2)}, u32[]{:S(2)}) collective-permute-start(bf16[32,8,256]{2,1,0:T(8,128)(2,1)S(1)} %all-to-all-done.2.near_ref), channel_id=1, source_target_pairs={{0,8},{8,0},{16,24},{24,16},{1,9},{9,1},{17,25},{25,17},{2,10},{10... | collective-permute-start | bytes 393224 | tf_op jit(solution)/shard_map/ppermute | solution.py:401

commit v14 on v13

--- a/solution.py
+++ b/solution.py
@@ -159,7 +159,7 @@
     half = slab - slots
     hub_rows = 2 * half
     bounds, hubs = parts * slots, parts * hub_rows
-    edges = [0] + list(range(TILE, nodes, 2 * TILE)) + [nodes]
+    edges = [0, nodes // 4, nodes * 5 // 8, nodes]
     blocks = len(edges) - 1
     features, counts = slice(width, 2 * width), 3 * width
 
@@ -464,8 +464,8 @@
             pltpu.VMEM((nodes, width), bf16),
             pltpu.VMEM((nodes, width), bf16),
             pltpu.VMEM((width, 2 * width + table), f32),
-            pltpu.SemaphoreType.DMA((2, nodes // (2 * TILE) + 1)),
-            pltpu.SemaphoreType.DMA((2, nodes // (2 * TILE) + 1)),
+            pltpu.SemaphoreType.DMA((2, 3)),
+            pltpu.SemaphoreType.DMA((2, 3)),
         ],
         flops=4 * nodes * table * width,
         moved=nodes * packed * 2,

time: 68.1 us -> 68.5 us (level)
  no operation moved by 1% of the time
where the time goes in v14:
time: 68.5 us; the launch traced here: 68.2 us
  Pallas kernels  27.4 us (40%)
  blocking collectives  19.8 us (29%)
  starting transfers between devices  10.3 us (15%)
  waiting for transfers between devices  7.42 us (11%)
  local copies, waits for them, and re-layouts  2.48 us (4%)
  between operations  0.79 us (1%)
    pallas_call x10, Pallas kernels, call(): pl.pallas_call(kernel, grid=grid, in_specs=in_specs, out_specs=out_specs,...  27.4 us
    all_to_all x1, blocking collectives, exchange(): return lax.all_to_all(value, AXES, split_axis=0, concat_axis=0, tiled=True)  19.8 us
    all_to_all x2, starting transfers between devices, exchange(): return lax.all_to_all(value, AXES, split_axis=0, concat_axis=0, tiled=True)  9.87 us
    all_to_all x2, waiting for transfers between devices, exchange(): return lax.all_to_all(value, AXES, split_axis=0, concat_axis=0, tiled=True)  4.15 us
    ppermute x3, waiting for transfers between devices, sibling(): return lax.ppermute(value, 'row', [(r, r ^ 1) for r in range(rows)])  3.27 us
    unnamed x20, local copies, waits for them, and re-layouts  2.48 us
  transfers between devices with their start and end apart: 5, of which 5 were waited for; matrix products, arithmetic and copies ran while one was open for 0% of the time, Pallas kernels for 23%

profile of v14, /device:TPU:0, one launch (start us, length us, event | category | flops | bytes accessed | tf_op | source)
XLA Modules:
  0.0 68.2 jit_solution(11263126039678262932)
XLA Ops:
  0.6 0.0 copy-start.7
  0.6 0.0 copy-start.9
  0.7 0.0 copy-start.8
  0.7 2.7 %pick_rows.1 = bf16[32,24,256]{2,1,0:T(8,128)(2,1)} custom-call(s32[1,512]{1,0:T(1,128)} %send_ref.3, bf16[2048,256]{1,0:T(8,128)(2,1)} %own_ref, bf16[16,256]{1,0:T(8,128)(2,1)} %hub_ref.1), custom_call_target="tpu_custom_call" | custom-call | flops 536870912 | bytes 1048576 | tf_op jit(solution)/shard_map/pick_rows/pallas_call | solution.py:355
  3.4 7.3 %all-to-all-start = ((bf16[32,24,256]{2,1,0:T(8,128)(2,1)}), bf16[32,24,256]{2,1,0:T(8,128)(2,1)S(1)}, u32[]{:S(2)}, u32[]{:S(2)}) async-start(bf16[32,24,256]{2,1,0:T(8,128)(2,1)} %pick_rows.1), calls=%async_computation | async-start | bytes 786432 | tf_op jit(solution)/shard_map/all_to_all | solution.py:404
  10.7 0.0 copy-done.7
  10.7 0.0 copy-done.9
  10.7 0.0 copy-done.8
  10.8 0.0 copy-start.5
  10.8 1.2 %copy-done.5 = bf16[2048,256]{1,0:T(8,128)(2,1)S(1)} copy-done((bf16[2048,256]{1,0:T(8,128)(2,1)S(1)}, bf16[2048,256]{1,0:T(8,128)(2,1)}, u32[]{:S(2)}) %copy-start.5) | copy-done | bytes 1048600
  12.0 1.2 %copy-done.6 = bf16[2048,256]{1,0:T(8,128)(2,1)S(1)} copy-done((bf16[2048,256]{1,0:T(8,128)(2,1)S(1)}, bf16[2048,256]{1,0:T(8,128)(2,1)}, u32[]{:S(2)}) %copy-start.6) | copy-done | bytes 1048600
  13.2 7.2 %local_gather.1 = (f32[2048,256]{1,0:T(8,128)S(1)}, bf16[2048,1536]{1,0:T(8,128)(2,1)}) custom-call(s32[1]{0:T(128)} %bitcast.core_ref, s32[4,2048]{1,0:T(4,128)S(1)} %bitcast.8, s32[4,2048]{1,0:T(4,128)S(1)} %bitcast.7, s32[2,2048]{1,0:T(2,128)S(1)} %bitcast.10, bf16[2048,256]{1,0:T(8,128)(2,1)S(1)} %copy-done.5, bf16[2048,256]{1,0:T(8,128)(2,1)S(1)} %copy-done.5, ...), custom_call_target="tpu_custom_call" | custom-call | flops 8589934592 | bytes 6291456 | tf_op jit(solution)/shard_map/local_gather/pallas_call | solution.py:355
  20.4 3.8 %all-to-all-done.table_ref = bf16[32,24,256]{2,1,0:T(8,128)(2,1)S(1)} async-done(((bf16[32,24,256]{2,1,0:T(8,128)(2,1)}), bf16[32,24,256]{2,1,0:T(8,128)(2,1)S(1)}, u32[]{:S(2)}, u32[]{:S(2)}) %all-to-all-start) | async-done | bytes 393248 | tf_op jit(solution)/shard_map/all_to_all | solution.py:404
  24.3 0.1 collective-permute-start
  24.3 1.3 %collective-permute-done.far_ref = bf16[256,256]{1,0:T(8,128)(2,1)S(1)} collective-permute-done((bf16[256,256]{1,0:T(8,128)(2,1)S(1)}, bf16[256,256]{1,0:T(8,128)(2,1)S(1)}, u32[]{:S(2)}, u32[]{:S(2)}) %collective-permute-start) | collective-permute-done | bytes 131104 | tf_op jit(solution)/shard_map/ppermute | solution.py:401
  25.7 7.7 %activate.1 = (bf16[2048,256]{1,0:T(8,128)(2,1)}, bf16[2048,256]{1,0:T(8,128)(2,1)}, bf16[32,32,128]{2,1,0:T(8,128)(2,1)S(1)}, f32[32,40,128]{2,1,0:T(8,128)S(1)}, bf16[32,40,128]{2,1,0:T(8,128)(2,1)S(1)}) custom-call(s32[1]{0:T(128)} %bitcast.core_ref, bf16[32,24,256]{2,1,0:T(8,128)(2,1)S(1)} %all-to-all-done.table_ref, ...), custom_call_target="tpu_custom_call" | custom-call | flops 2147483648 | bytes 6291456 | tf_op jit(solution)/shard_map/activate/pallas_call | solution.py:355
  33.4 0.0 copy-start.1
  33.4 0.2 collective-permute-start.1
  33.6 1.5 %collective-permute-done.1.got_ref = bf16[32,40,128]{2,1,0:T(8,128)(2,1)S(1)} collective-permute-done((bf16[32,40,128]{2,1,0:T(8,128)(2,1)S(1)}, bf16[32,40,128]{2,1,0:T(8,128)(2,1)S(1)}, u32[]{:S(2)}, u32[]{:S(2)}) %collective-permute-start.1) | collective-permute-done | bytes 327712 | tf_op jit(solution)/shard_map/ppermute | solution.py:401
  35.1 0.1 join_siblings.1
  35.2 19.8 %all_to_all.15.back_ref = bf16[32,72,128]{2,1,0:T(8,128)(2,1)S(1)} all-to-all(bf16[32,72,128]{2,1,0:T(8,128)(2,1)S(1)} %join_siblings.1), channel_id=1, replica_groups=mesh['row'=4,'col'=8] {'row','col'}, dimensions={0} | all-to-all | bytes 1179648 | tf_op jit(solution)/shard_map/all_to_all | solution.py:404
  55.0 0.7 weight_sums.1
  55.7 2.6 %all-to-all-start.2 = ((bf16[32,8,256]{2,1,0:T(8,128)(2,1)}), bf16[32,8,256]{2,1,0:T(8,128)(2,1)S(1)}, u32[]{:S(2)}, u32[]{:S(2)}) async-start(bf16[32,8,256]{2,1,0:T(8,128)(2,1)} %weight_sums.1), calls=%async_computation.2 | async-start | bytes 262144 | tf_op jit(solution)/shard_map/all_to_all | solution.py:404
  58.3 0.0 copy-start.3
  58.3 3.7 %local_scatter.1.scat_ref = f32[2048,256]{1,0:T(8,128)S(1)} custom-call(s32[4,2048]{1,0:T(4,128)S(1)} %bitcast.9, bf16[2048,256]{1,0:T(8,128)(2,1)S(1)} %copy-done.1), custom_call_target="tpu_custom_call" | custom-call | flops 8589934592 | bytes 3145728 | tf_op jit(solution)/shard_map/local_scatter/pallas_call | solution.py:355
  62.0 0.0 copy-done.3
  62.0 3.6 %return_scatter.1 = f32[2048,256]{1,0:T(8,128)} custom-call(s32[1,512]{1,0:T(1,128)S(1)} %copy-done.3, bf16[32,72,128]{2,1,0:T(8,128)(2,1)S(1)} %all_to_all.15.back_ref, f32[2048,256]{1,0:T(8,128)S(1)} %local_scatter.1.scat_ref, bf16[2048,256]{1,0:T(8,128)(2,1)S(1)} %copy-done.1, bf16[256,256]{1,0:T(8,128)(2,1)S(1)} %copy-done.2, bf16[256,256]{1,0:T(8,128)(2,1)S(1)} %copy-done), custom_call_target="tpu_custom_call" | custom-call | flops 536870912 | bytes 5242880 | tf_op jit(solution)/shard_map/return_scatter/pallas_call | solution.py:355
  65.7 0.3 all-to-all-done.2.near_ref
  66.0 0.1 collective-permute-start.2
  66.1 0.8 %hub_sums.1 = (f32[1,256]{1,0:T(1,128)}, f32[16,256]{1,0:T(8,128)}) custom-call(bf16[32,72,128]{2,1,0:T(8,128)(2,1)S(1)} %all_to_all.15.back_ref, bf16[256,256]{1,0:T(8,128)(2,1)S(1)} %copy-done), custom_call_target="tpu_custom_call" | custom-call | bytes 1179648 | tf_op jit(solution)/shard_map/hub_sums/pallas_call | solution.py:355
  66.9 0.4 collective-permute-done.2.far_ref
  67.3 0.8 %weights.1 = (f32[256,256]{1,0:T(8,128)}, f32[256,256]{1,0:T(8,128)}) custom-call(s32[1]{0:T(128)} %bitcast.core_ref, bf16[32,8,256]{2,1,0:T(8,128)(2,1)S(1)} %all-to-all-done.2.near_ref, bf16[32,8,256]{2,1,0:T(8,128)(2,1)S(1)} %collective-permute-done.2.far_ref), custom_call_target="tpu_custom_call" | custom-call | bytes 786432 | tf_op jit(solution)/shard_map/weights/pallas_call | solution.py:355
  (9 shorter events, 0.0 us)
Async XLA Ops:
  0.6 10.1 %copy-start.7 = (s32[2048,4]{0,1:T(4,128)S(1)}, s32[2048,4]{0,1:T(4,128)}, u32[]{:S(2)}) copy-start(s32[2048,4]{0,1:T(4,128)} %param.17) | copy-start | bytes 98308
  0.6 10.1 %copy-start.9 = (s32[2048,2]{0,1:T(2,128)S(1)}, s32[2048,2]{0,1:T(2,128)}, u32[]{:S(2)}) copy-start(s32[2048,2]{0,1:T(2,128)} %param.16) | copy-start | bytes 49156
  0.7 10.1 %copy-start.8 = (s32[2048,4]{0,1:T(4,128)S(1)}, s32[2048,4]{0,1:T(4,128)}, u32[]{:S(2)}) copy-start(s32[2048,4]{0,1:T(4,128)} %param.15) | copy-start | bytes 98308
  3.4 20.8 %all-to-all-start = ((bf16[32,24,256]{2,1,0:T(8,128)(2,1)}), bf16[32,24,256]{2,1,0:T(8,128)(2,1)S(1)}, u32[]{:S(2)}, u32[]{:S(2)}) async-start(bf16[32,24,256]{2,1,0:T(8,128)(2,1)} %pick_rows.1), calls=%async_computation | async-start | bytes 786432 | tf_op jit(solution)/shard_map/all_to_all | solution.py:404
  10.8 1.2 %copy-start.5 = (bf16[2048,256]{1,0:T(8,128)(2,1)S(1)}, bf16[2048,256]{1,0:T(8,128)(2,1)}, u32[]{:S(2)}) copy-start(bf16[2048,256]{1,0:T(8,128)(2,1)} %own_ref) | copy-start | bytes 3145732
  12.0 1.2 %copy-start.6 = (bf16[2048,256]{1,0:T(8,128)(2,1)S(1)}, bf16[2048,256]{1,0:T(8,128)(2,1)}, u32[]{:S(2)}) copy-start(bf16[2048,256]{1,0:T(8,128)(2,1)} %cot_ref.1) | copy-start | bytes 3145732
  13.2 12.5 %copy-start = (bf16[256,256]{1,0:T(8,128)(2,1)S(1)}, bf16[256,256]{1,0:T(8,128)(2,1)}, u32[]{:S(2)}) copy-start(bf16[256,256]{1,0:T(8,128)(2,1)} %wn_ref.5) | copy-start | bytes 393220
  13.2 12.5 %copy-start.2 = (bf16[256,256]{1,0:T(8,128)(2,1)S(1)}, bf16[256,256]{1,0:T(8,128)(2,1)}, u32[]{:S(2)}) copy-start(bf16[256,256]{1,0:T(8,128)(2,1)} %ws_ref.3) | copy-start | bytes 393220
  13.2 12.5 %copy-start.4 = (f32[256]{0:T(256)S(1)}, f32[256]{0:T(256)}, u32[]{:S(2)}) copy-start(f32[256]{0:T(256)} %param.14) | copy-start | bytes 3076
  24.3 1.4 %collective-permute-start = (bf16[256,256]{1,0:T(8,128)(2,1)S(1)}, bf16[256,256]{1,0:T(8,128)(2,1)S(1)}, u32[]{:S(2)}, u32[]{:S(2)}) collective-permute-start(bf16[256,256]{1,0:T(8,128)(2,1)S(1)} %take_hubs.1.near_ref), channel_id=1, source_target_pairs={{0,8},{8,0},{16,24},{24,16},{1,9},{9,1},{17,25},{25,17},{2,10},{10... | collective-permute-start | bytes 393224 | tf_op jit(solution)/shard_map/ppermute | solution.py:401
  33.4 24.9 %copy-start.1 = (bf16[2048,256]{1,0:T(8,128)(2,1)S(1)}, bf16[2048,256]{1,0:T(8,128)(2,1)}, u32[]{:S(2)}) copy-start(bf16[2048,256]{1,0:T(8,128)(2,1)} %get-tuple-element.35.grad_ref) | copy-start | bytes 3145732
  33.4 1.7 %collective-permute-start.1 = (bf16[32,40,128]{2,1,0:T(8,128)(2,1)S(1)}, bf16[32,40,128]{2,1,0:T(8,128)(2,1)S(1)}, u32[]{:S(2)}, u32[]{:S(2)}) collective-permute-start(bf16[32,40,128]{2,1,0:T(8,128)(2,1)S(1)} %get-tuple-element.34), channel_id=1, source_target_pairs={{0,8},{8,0},{16,24},{24,16},{1,9},{9,1},{17,25},{25,17},{2,10},{10... | collective-permute-start | bytes 983048 | tf_op jit(solution)/shard_map/ppermute | solution.py:401
  55.7 10.3 %all-to-all-start.2 = ((bf16[32,8,256]{2,1,0:T(8,128)(2,1)}), bf16[32,8,256]{2,1,0:T(8,128)(2,1)S(1)}, u32[]{:S(2)}, u32[]{:S(2)}) async-start(bf16[32,8,256]{2,1,0:T(8,128)(2,1)} %weight_sums.1), calls=%async_computation.2 | async-start | bytes 262144 | tf_op jit(solution)/shard_map/all_to_all | solution.py:404
  58.3 3.8 %copy-start.3 = (s32[1,512]{1,0:T(1,128)S(1)}, s32[1,512]{1,0:T(1,128)}, u32[]{:S(2)}) copy-start(s32[1,512]{1,0:T(1,128)} %send_ref.3) | copy-start | bytes 6148
  66.0 1.3 %collective-permute-start.2 = (bf16[32,8,256]{2,1,0:T(8,128)(2,1)S(1)}, bf16[32,8,256]{2,1,0:T(8,128)(2,1)S(1)}, u32[]{:S(2)}, u32[]{:S(2)}) collective-permute-start(bf16[32,8,256]{2,1,0:T(8,128)(2,1)S(1)} %all-to-all-done.2.near_ref), channel_id=1, source_target_pairs={{0,8},{8,0},{16,24},{24,16},{1,9},{9,1},{17,25},{25,17},{2,10},{10... | collective-permute-start | bytes 393224 | tf_op jit(solution)/shard_map/ppermute | solution.py:401

commit v15 on v12

--- a/solution.py
+++ b/solution.py
@@ -488,9 +488,9 @@
         (local_t, grad_pre),
         [whole_block(local_t.shape), whole_block((nodes, width))],
         shape((nodes, width), f32),
-        pl.BlockSpec((2 * TILE, width), lambda i: (i, 0)),
+        pl.BlockSpec((4 * TILE, width), lambda i: (i, 0)),
         "local_scatter",
-        grid=(nodes // (2 * TILE),),
+        grid=(nodes // (4 * TILE),),
         flops=8 * nodes * nodes * width,
         moved=nodes * width * 6,
     )

time: 67.4 us -> 67.4 us (level)
  transfers between devices with their start and end apart: 5 -> 5, of which waited for: 5 -> 5; matrix products, arithmetic and copies ran while one was open for 0% -> 0% of each run, Pallas kernels for 23% -> 22%
where the time goes in v15:
time: 67.4 us; the launch traced here: 67.1 us
  Pallas kernels  26 us (39%)
  blocking collectives  19.8 us (29%)
  starting transfers between devices  10.3 us (15%)
  waiting for transfers between devices  7.74 us (11%)
  local copies, waits for them, and re-layouts  2.48 us (4%)
  between operations  0.79 us (1%)
    pallas_call x10, Pallas kernels, call(): pl.pallas_call(kernel, grid=grid, in_specs=in_specs, out_specs=out_specs,...  26 us
    all_to_all x1, blocking collectives, exchange(): return lax.all_to_all(value, AXES, split_axis=0, concat_axis=0, tiled=True)  19.8 us
    all_to_all x2, starting transfers between devices, exchange(): return lax.all_to_all(value, AXES, split_axis=0, concat_axis=0, tiled=True)  9.87 us
    all_to_all x2, waiting for transfers between devices, exchange(): return lax.all_to_all(value, AXES, split_axis=0, concat_axis=0, tiled=True)  4.47 us
    ppermute x3, waiting for transfers between devices, sibling(): return lax.ppermute(value, 'row', [(r, r ^ 1) for r in range(rows)])  3.27 us
    unnamed x20, local copies, waits for them, and re-layouts  2.48 us
  transfers between devices with their start and end apart: 5, of which 5 were waited for; matrix products, arithmetic and copies ran while one was open for 0% of the time, Pallas kernels for 22%

profile of v15, /device:TPU:0, one launch (start us, length us, event | category | flops | bytes accessed | tf_op | source)
XLA Modules:
  0.0 67.1 jit_solution(551331379332080488)
XLA Ops:
  0.6 0.0 copy-start.7
  0.6 0.0 copy-start.9
  0.7 0.0 copy-start.8
  0.7 2.7 %pick_rows.1 = bf16[32,24,256]{2,1,0:T(8,128)(2,1)} custom-call(s32[1,512]{1,0:T(1,128)} %send_ref.3, bf16[2048,256]{1,0:T(8,128)(2,1)} %own_ref, bf16[16,256]{1,0:T(8,128)(2,1)} %hub_ref.1), custom_call_target="tpu_custom_call" | custom-call | flops 536870912 | bytes 1048576 | tf_op jit(solution)/shard_map/pick_rows/pallas_call | solution.py:355
  3.4 7.3 %all-to-all-start = ((bf16[32,24,256]{2,1,0:T(8,128)(2,1)}), bf16[32,24,256]{2,1,0:T(8,128)(2,1)S(1)}, u32[]{:S(2)}, u32[]{:S(2)}) async-start(bf16[32,24,256]{2,1,0:T(8,128)(2,1)} %pick_rows.1), calls=%async_computation | async-start | bytes 786432 | tf_op jit(solution)/shard_map/all_to_all | solution.py:404
  10.7 0.0 copy-done.7
  10.7 0.0 copy-done.9
  10.7 0.0 copy-done.8
  10.8 0.0 copy-start.5
  10.8 1.2 %copy-done.5 = bf16[2048,256]{1,0:T(8,128)(2,1)S(1)} copy-done((bf16[2048,256]{1,0:T(8,128)(2,1)S(1)}, bf16[2048,256]{1,0:T(8,128)(2,1)}, u32[]{:S(2)}) %copy-start.5) | copy-done | bytes 1048600
  12.0 1.2 %copy-done.6 = bf16[2048,256]{1,0:T(8,128)(2,1)S(1)} copy-done((bf16[2048,256]{1,0:T(8,128)(2,1)S(1)}, bf16[2048,256]{1,0:T(8,128)(2,1)}, u32[]{:S(2)}) %copy-start.6) | copy-done | bytes 1048600
  13.2 7.2 %local_gather.1 = (f32[2048,256]{1,0:T(8,128)S(1)}, bf16[2048,1536]{1,0:T(8,128)(2,1)}) custom-call(s32[1]{0:T(128)} %bitcast.core_ref, s32[4,2048]{1,0:T(4,128)S(1)} %bitcast.8, s32[4,2048]{1,0:T(4,128)S(1)} %bitcast.7, s32[2,2048]{1,0:T(2,128)S(1)} %bitcast.10, bf16[2048,256]{1,0:T(8,128)(2,1)S(1)} %copy-done.5, bf16[2048,256]{1,0:T(8,128)(2,1)S(1)} %copy-done.5, ...), custom_call_target="tpu_custom_call" | custom-call | flops 8589934592 | bytes 6291456 | tf_op jit(solution)/shard_map/local_gather/pallas_call | solution.py:355
  20.4 3.8 %all-to-all-done.table_ref = bf16[32,24,256]{2,1,0:T(8,128)(2,1)S(1)} async-done(((bf16[32,24,256]{2,1,0:T(8,128)(2,1)}), bf16[32,24,256]{2,1,0:T(8,128)(2,1)S(1)}, u32[]{:S(2)}, u32[]{:S(2)}) %all-to-all-start) | async-done | bytes 393248 | tf_op jit(solution)/shard_map/all_to_all | solution.py:404
  24.3 0.1 collective-permute-start
  24.3 1.3 %collective-permute-done.far_ref = bf16[256,256]{1,0:T(8,128)(2,1)S(1)} collective-permute-done((bf16[256,256]{1,0:T(8,128)(2,1)S(1)}, bf16[256,256]{1,0:T(8,128)(2,1)S(1)}, u32[]{:S(2)}, u32[]{:S(2)}) %collective-permute-start) | collective-permute-done | bytes 131104 | tf_op jit(solution)/shard_map/ppermute | solution.py:401
  25.7 0.0 copy-done
  25.7 6.6 %activate.1 = (bf16[2048,256]{1,0:T(8,128)(2,1)}, bf16[2048,256]{1,0:T(8,128)(2,1)}, bf16[32,32,128]{2,1,0:T(8,128)(2,1)S(1)}, f32[32,40,128]{2,1,0:T(8,128)S(1)}, bf16[32,40,128]{2,1,0:T(8,128)(2,1)S(1)}) custom-call(s32[1]{0:T(128)} %bitcast.core_ref, bf16[32,24,256]{2,1,0:T(8,128)(2,1)S(1)} %all-to-all-done.table_ref, ...), custom_call_target="tpu_custom_call" | custom-call | flops 2147483648 | bytes 6291456 | tf_op jit(solution)/shard_map/activate/pallas_call | solution.py:355
  32.3 0.0 copy-start.1
  32.3 0.2 collective-permute-start.1
  32.5 1.5 %collective-permute-done.1.got_ref = bf16[32,40,128]{2,1,0:T(8,128)(2,1)S(1)} collective-permute-done((bf16[32,40,128]{2,1,0:T(8,128)(2,1)S(1)}, bf16[32,40,128]{2,1,0:T(8,128)(2,1)S(1)}, u32[]{:S(2)}, u32[]{:S(2)}) %collective-permute-start.1) | collective-permute-done | bytes 327712 | tf_op jit(solution)/shard_map/ppermute | solution.py:401
  34.0 0.1 join_siblings.1
  34.1 19.8 %all_to_all.15.back_ref = bf16[32,72,128]{2,1,0:T(8,128)(2,1)S(1)} all-to-all(bf16[32,72,128]{2,1,0:T(8,128)(2,1)S(1)} %join_siblings.1), channel_id=1, replica_groups=mesh['row'=4,'col'=8] {'row','col'}, dimensions={0} | all-to-all | bytes 1179648 | tf_op jit(solution)/shard_map/all_to_all | solution.py:404
  53.9 0.7 %weight_sums.1 = bf16[32,8,256]{2,1,0:T(8,128)(2,1)} custom-call(bf16[32,72,128]{2,1,0:T(8,128)(2,1)S(1)} %all_to_all.15.back_ref), custom_call_target="tpu_custom_call" | custom-call | bytes 1179648 | tf_op jit(solution)/shard_map/weight_sums/pallas_call | solution.py:355
  54.6 2.6 %all-to-all-start.2 = ((bf16[32,8,256]{2,1,0:T(8,128)(2,1)}), bf16[32,8,256]{2,1,0:T(8,128)(2,1)S(1)}, u32[]{:S(2)}, u32[]{:S(2)}) async-start(bf16[32,8,256]{2,1,0:T(8,128)(2,1)} %weight_sums.1), calls=%async_computation.2 | async-start | bytes 262144 | tf_op jit(solution)/shard_map/all_to_all | solution.py:404
  57.2 0.0 copy-start.3
  57.2 3.4 %local_scatter.1.scat_ref = f32[2048,256]{1,0:T(8,128)S(1)} custom-call(s32[4,2048]{1,0:T(4,128)S(1)} %bitcast.9, bf16[2048,256]{1,0:T(8,128)(2,1)S(1)} %copy-done.1), custom_call_target="tpu_custom_call" | custom-call | flops 8589934592 | bytes 3145728 | tf_op jit(solution)/shard_map/local_scatter/pallas_call | solution.py:355
  60.6 3.6 %return_scatter.1 = f32[2048,256]{1,0:T(8,128)} custom-call(s32[1,512]{1,0:T(1,128)S(1)} %copy-done.3, bf16[32,72,128]{2,1,0:T(8,128)(2,1)S(1)} %all_to_all.15.back_ref, f32[2048,256]{1,0:T(8,128)S(1)} %local_scatter.1.scat_ref, bf16[2048,256]{1,0:T(8,128)(2,1)S(1)} %copy-done.1, bf16[256,256]{1,0:T(8,128)(2,1)S(1)} %copy-done.2, bf16[256,256]{1,0:T(8,128)(2,1)S(1)} %copy-done), custom_call_target="tpu_custom_call" | custom-call | flops 536870912 | bytes 5242880 | tf_op jit(solution)/shard_map/return_scatter/pallas_call | solution.py:355
  64.3 0.6 all-to-all-done.2.near_ref
  64.9 0.1 collective-permute-start.2
  65.0 0.8 %hub_sums.1 = (f32[1,256]{1,0:T(1,128)}, f32[16,256]{1,0:T(8,128)}) custom-call(bf16[32,72,128]{2,1,0:T(8,128)(2,1)S(1)} %all_to_all.15.back_ref, bf16[256,256]{1,0:T(8,128)(2,1)S(1)} %copy-done), custom_call_target="tpu_custom_call" | custom-call | bytes 1179648 | tf_op jit(solution)/shard_map/hub_sums/pallas_call | solution.py:355
  65.8 0.4 collective-permute-done.2.far_ref
  66.3 0.8 %weights.1 = (f32[256,256]{1,0:T(8,128)}, f32[256,256]{1,0:T(8,128)}) custom-call(s32[1]{0:T(128)} %bitcast.core_ref, bf16[32,8,256]{2,1,0:T(8,128)(2,1)S(1)} %all-to-all-done.2.near_ref, bf16[32,8,256]{2,1,0:T(8,128)(2,1)S(1)} %collective-permute-done.2.far_ref), custom_call_target="tpu_custom_call" | custom-call | bytes 786432 | tf_op jit(solution)/shard_map/weights/pallas_call | solution.py:355
  (9 shorter events, 0.0 us)
Async XLA Ops:
  0.6 10.1 %copy-start.7 = (s32[2048,4]{0,1:T(4,128)S(1)}, s32[2048,4]{0,1:T(4,128)}, u32[]{:S(2)}) copy-start(s32[2048,4]{0,1:T(4,128)} %param.17) | copy-start | bytes 98308
  0.6 10.1 %copy-start.9 = (s32[2048,2]{0,1:T(2,128)S(1)}, s32[2048,2]{0,1:T(2,128)}, u32[]{:S(2)}) copy-start(s32[2048,2]{0,1:T(2,128)} %param.16) | copy-start | bytes 49156
  0.7 10.1 %copy-start.8 = (s32[2048,4]{0,1:T(4,128)S(1)}, s32[2048,4]{0,1:T(4,128)}, u32[]{:S(2)}) copy-start(s32[2048,4]{0,1:T(4,128)} %param.15) | copy-start | bytes 98308
  3.4 20.8 %all-to-all-start = ((bf16[32,24,256]{2,1,0:T(8,128)(2,1)}), bf16[32,24,256]{2,1,0:T(8,128)(2,1)S(1)}, u32[]{:S(2)}, u32[]{:S(2)}) async-start(bf16[32,24,256]{2,1,0:T(8,128)(2,1)} %pick_rows.1), calls=%async_computation | async-start | bytes 786432 | tf_op jit(solution)/shard_map/all_to_all | solution.py:404
  10.8 1.2 %copy-start.5 = (bf16[2048,256]{1,0:T(8,128)(2,1)S(1)}, bf16[2048,256]{1,0:T(8,128)(2,1)}, u32[]{:S(2)}) copy-start(bf16[2048,256]{1,0:T(8,128)(2,1)} %own_ref) | copy-start | bytes 3145732
  12.0 1.2 %copy-start.6 = (bf16[2048,256]{1,0:T(8,128)(2,1)S(1)}, bf16[2048,256]{1,0:T(8,128)(2,1)}, u32[]{:S(2)}) copy-start(bf16[2048,256]{1,0:T(8,128)(2,1)} %cot_ref.1) | copy-start | bytes 3145732
  13.2 12.5 %copy-start = (bf16[256,256]{1,0:T(8,128)(2,1)S(1)}, bf16[256,256]{1,0:T(8,128)(2,1)}, u32[]{:S(2)}) copy-start(bf16[256,256]{1,0:T(8,128)(2,1)} %wn_ref.5) | copy-start | bytes 393220
  13.2 12.5 %copy-start.2 = (bf16[256,256]{1,0:T(8,128)(2,1)S(1)}, bf16[256,256]{1,0:T(8,128)(2,1)}, u32[]{:S(2)}) copy-start(bf16[256,256]{1,0:T(8,128)(2,1)} %ws_ref.3) | copy-start | bytes 393220
  13.2 12.5 %copy-start.4 = (f32[256]{0:T(256)S(1)}, f32[256]{0:T(256)}, u32[]{:S(2)}) copy-start(f32[256]{0:T(256)} %param.14) | copy-start | bytes 3076
  24.3 1.4 %collective-permute-start = (bf16[256,256]{1,0:T(8,128)(2,1)S(1)}, bf16[256,256]{1,0:T(8,128)(2,1)S(1)}, u32[]{:S(2)}, u32[]{:S(2)}) collective-permute-start(bf16[256,256]{1,0:T(8,128)(2,1)S(1)} %take_hubs.1.near_ref), channel_id=1, source_target_pairs={{0,8},{8,0},{16,24},{24,16},{1,9},{9,1},{17,25},{25,17},{2,10},{10... | collective-permute-start | bytes 393224 | tf_op jit(solution)/shard_map/ppermute | solution.py:401
  32.3 24.9 %copy-start.1 = (bf16[2048,256]{1,0:T(8,128)(2,1)S(1)}, bf16[2048,256]{1,0:T(8,128)(2,1)}, u32[]{:S(2)}) copy-start(bf16[2048,256]{1,0:T(8,128)(2,1)} %get-tuple-element.35.grad_ref) | copy-start | bytes 3145732
  32.3 1.7 %collective-permute-start.1 = (bf16[32,40,128]{2,1,0:T(8,128)(2,1)S(1)}, bf16[32,40,128]{2,1,0:T(8,128)(2,1)S(1)}, u32[]{:S(2)}, u32[]{:S(2)}) collective-permute-start(bf16[32,40,128]{2,1,0:T(8,128)(2,1)S(1)} %get-tuple-element.34), channel_id=1, source_target_pairs={{0,8},{8,0},{16,24},{24,16},{1,9},{9,1},{17,25},{25,17},{2,10},{10... | collective-permute-start | bytes 983048 | tf_op jit(solution)/shard_map/ppermute | solution.py:401
  54.6 10.3 %all-to-all-start.2 = ((bf16[32,8,256]{2,1,0:T(8,128)(2,1)}), bf16[32,8,256]{2,1,0:T(8,128)(2,1)S(1)}, u32[]{:S(2)}, u32[]{:S(2)}) async-start(bf16[32,8,256]{2,1,0:T(8,128)(2,1)} %weight_sums.1), calls=%async_computation.2 | async-start | bytes 262144 | tf_op jit(solution)/shard_map/all_to_all | solution.py:404
  57.2 3.4 %copy-start.3 = (s32[1,512]{1,0:T(1,128)S(1)}, s32[1,512]{1,0:T(1,128)}, u32[]{:S(2)}) copy-start(s32[1,512]{1,0:T(1,128)} %send_ref.3) | copy-start | bytes 6148
  64.9 1.3 %collective-permute-start.2 = (bf16[32,8,256]{2,1,0:T(8,128)(2,1)S(1)}, bf16[32,8,256]{2,1,0:T(8,128)(2,1)S(1)}, u32[]{:S(2)}, u32[]{:S(2)}) collective-permute-start(bf16[32,8,256]{2,1,0:T(8,128)(2,1)S(1)} %all-to-all-done.2.near_ref), channel_id=1, source_target_pairs={{0,8},{8,0},{16,24},{24,16},{1,9},{9,1},{17,25},{25,17},{2,10},{10... | collective-permute-start | bytes 393224 | tf_op jit(solution)/shard_map/ppermute | solution.py:401
